TPU v7x, 256 devices: a whole 4x4x8 slice. The times are simulated.
256 devices in a mesh: item: 16 (over x, z_lo), store: 16 (over y, z_hi, core).
Axes of the slice: x: 4, y: 4, z: 8 (z_hi: 2, z_lo: 4; z = z_hi * 4 + z_lo), core: 2. Of those that a mesh axis runs over, the one named last changes fastest.
Arguments:
- sales: float32 [8, 16384, 4096], P(None, 'item', 'store'), may hold values from -6 to 6
- launch_week: int32 [16384], P('item'), may hold values from 0 to 8
- open_week: int32 [4096], P('store'), may hold values from 0 to 7
- item_factors: float32 [16384, 128], P(('item', 'store')), may hold values from -4 to 4
- store_factors: float32 [4096, 128], P(('store', 'item')), may hold values from -4 to 4
- week_factors: float32 [8, 128], replicated, may hold values from -4 to 4
Outputs:
- new_items: float32 [16384, 128], P(('item', 'store'))
- new_stores: float32 [4096, 128], P(('store', 'item'))
- new_weeks: float32 [8, 128], replicated
- losses: float32 [2], replicated
All inputs are finite; a program needn't handle non-finite values.
Results may differ from a plain program's by a relative error of at most 0.0003.
Values sent between devices are 32-bit elements; how exact they have to be, the bound alone decides.
No kernel may reach another device: no remote copies, remote signals or barrier semaphores. Data moves between devices by JAX's collectives and lax.ppermute only.
A program may use at most 64 MiB of HBM per device.

v0:
```python
import functools

import jax
import jax.numpy as jnp
from jax import lax
from jax.experimental import pallas as pl
from jax.experimental.pallas import tpu as pltpu
from jax.sharding import PartitionSpec as P

CORE, ZHI = 1, 2
OUTER = (4, 8, 12)
ZLOS = (1, 2, 3)
MIB = 1 << 20
LONG = 10**11
F32 = jnp.float32
BF16 = jnp.bfloat16
VM = pl.BlockSpec(memory_space=pltpu.VMEM)


def swap(value, axis, bits):
    return lax.ppermute(value, axis, [(i, i ^ bits) for i in range(16)])


def split(value):
    high = value.astype(BF16)
    return high, (value - high.astype(F32)).astype(BF16)


def row_of(axis, rows, bits):
    return pl.multiple_of((lax.axis_index(axis) ^ bits) * rows, rows)


def tree(values):
    while len(values) > 1:
        values = [a + b for a, b in zip(values[::2], values[1::2])]
    return values[0]


def small_call(kernel, outs, *args, flops=None, scratch=()):
    cost = pl.CostEstimate(flops=flops or 0, bytes_accessed=0, transcendentals=0)
    outs = [o if isinstance(o, jax.ShapeDtypeStruct) else jax.ShapeDtypeStruct(o, F32) for o in outs]
    return pl.pallas_call(
        kernel,
        out_shape=outs,
        in_specs=[VM] * len(args),
        out_specs=[VM] * len(outs),
        scratch_shapes=scratch,
        compiler_params=pltpu.CompilerParams(vmem_limit_bytes=8 * MIB),
        cost_estimate=cost,
    )(*args)


def step_kernel(sub, rate_c, riding, *refs):
    sales_ref, late_ref, b_ref, c_ref, old_weeks = refs[:5]
    rows_of = refs[5:7]
    er, gbt_ref, weeks_ref, newc_ref = refs[7:11]
    a_f, a3, at = refs[11:]
    weeks, n_items, n_stores = sales_ref.shape
    rank = a_f.shape[1]
    rows = 256

    for o in range(2):
        for d in range(4):
            for h in range(2):
                row = row_of("store", sub, 4 * d + 2 * h + o)
                a_f[pl.ds(row, sub), :] = rows_of[o][(2 * d + h) * sub : (2 * d + h + 1) * sub, :]
    a = a_f[...]
    high, low = split(a)
    a3[:, :rank] = high
    a3[:, rank : 2 * rank] = low
    a3[:, 2 * rank :] = high
    high, low = split(a.T)
    at[:rank, :] = high
    at[rank:, :] = low
    b = b_ref[...]
    bt = b.T
    c = c_ref[...]
    if riding:
        c = c - rate_c * rows_of[0][8 * sub :, :]
    newc_ref[...] = c

    def factor(w):
        high, low = split(b * c[w : w + 1, :])
        return jnp.concatenate([high, high, low], axis=1)

    def errors(w, i, bc3, total_s):
        part = slice(i * rows, (i + 1) * rows)
        recon = lax.dot_general(a3[part, :], bc3, (((1,), (1,)), ((), ())), preferred_element_type=F32)
        error = jnp.where(late_ref[part, :] <= w, recon - sales_ref[w, part, :], 0.0)
        er[w, part, :] = error.astype(BF16)
        return total_s + jnp.sum((error * error).reshape(rows // 8, 8, n_stores), axis=0)

    n = n_items // rows
    total_s = jnp.zeros((8, n_stores), F32)
    gbt = jnp.zeros((rank, n_stores), F32)
    week_columns = []
    bc3 = factor(0)
    for i in range(n):
        total_s = errors(0, i, bc3, total_s)
    for w in range(weeks):
        if w + 1 < weeks:
            bc3 = factor(w + 1)
            for i in range(n):
                total_s = errors(w + 1, i, bc3, total_s)
        x = jnp.dot(at[...], er[w], preferred_element_type=F32)
        x = x[:rank, :] + x[rank:, :]
        week_columns.append(jnp.sum(x * bt, axis=1, keepdims=True))
        turn = jnp.broadcast_to(c[w : w + 1, :], (rank, rank)).T
        gbt = gbt + jnp.concatenate([turn] * (n_stores // rank), axis=1) * x

    lane = lax.broadcasted_iota(jnp.int32, (rank, rank), 1)
    gc = jnp.zeros((rank, rank), F32)
    for w in range(weeks):
        gc = jnp.where(lane == w, week_columns[w], gc)
    gc = gc.T[:weeks, :]
    s = jnp.sum(total_s, axis=0, keepdims=True)
    loss = s[:, :rank]
    for i in range(1, n_stores // rank):
        loss = loss + s[:, i * rank : (i + 1) * rank]
    at_row = lax.broadcasted_iota(jnp.int32, (8, rank), 0)
    losses = jnp.where(at_row == int(riding), loss, old_weeks[weeks:, :])
    gbt_ref[...] = gbt
    weeks_ref[:weeks, :] = gc
    weeks_ref[weeks:, :] = losses


def step_call(sub, rate_c, riding, sales, late, block_b, factor_c, old_weeks, mine, other):
    weeks, n_items, n_stores = sales.shape
    rank = block_b.shape[1]
    outs = [(rank, n_stores), (weeks + 8, rank), (weeks, rank)]
    args = [sales, late, block_b, factor_c, old_weeks, mine, other]
    return pl.pallas_call(
        functools.partial(step_kernel, sub, rate_c, riding),
        out_shape=[jax.ShapeDtypeStruct(sales.shape, BF16)] + [jax.ShapeDtypeStruct(s, F32) for s in outs],
        in_specs=[VM] * len(args),
        out_specs=[VM] * (1 + len(outs)),
        scratch_shapes=[
            pltpu.VMEM((n_items, rank), F32),
            pltpu.VMEM((n_items, 3 * rank), BF16),
            pltpu.VMEM((2 * rank, n_items), BF16),
        ],
        compiler_params=pltpu.CompilerParams(vmem_limit_bytes=28 * MIB),
        cost_estimate=pl.CostEstimate(
            flops=4 * n_items * n_stores * weeks * rank, bytes_accessed=4 * n_items * n_stores * weeks, transcendentals=0
        ),
    )(*args)


def items_grad_kernel(er, b_ref, c_ref, after_ref, send_ref, own_ref, ga):
    weeks, n_items, n_stores = er.shape
    rank = b_ref.shape[1]
    rows = 256
    b = b_ref[...]
    factors = [jnp.concatenate(split(b * c_ref[w : w + 1, :]), axis=1) for w in range(weeks)]
    for i in range(n_items // rows):
        part = slice(i * rows, (i + 1) * rows)
        g = jnp.dot(er[0, part, :], factors[0], preferred_element_type=F32)
        for w in range(1, weeks):
            g = g + jnp.dot(er[w, part, :], factors[w], preferred_element_type=F32)
        ga[part, :] = g[:, :rank] + g[:, rank:]
    sub = send_ref.shape[0] // 8
    for other, out in ((0, own_ref), (1, send_ref)):
        for d in range(4):
            for h in range(2):
                row = row_of("store", sub, 4 * d + 2 * h + other)
                out[(d * 2 + h) * sub : (d * 2 + h + 1) * sub, :] = ga[pl.ds(row, sub), :]


def items_grad_call(er, block_b, factor_c, after):
    weeks, n_items, n_stores = er.shape
    rank = block_b.shape[1]
    return pl.pallas_call(
        items_grad_kernel,
        out_shape=[jax.ShapeDtypeStruct((n_items // 2, rank), F32)] * 2,
        in_specs=[VM] * 4,
        out_specs=[VM] * 2,
        scratch_shapes=[pltpu.VMEM((n_items, rank), F32)],
        compiler_params=pltpu.CompilerParams(vmem_limit_bytes=16 * MIB),
        cost_estimate=pl.CostEstimate(flops=0, bytes_accessed=0, transcendentals=0),
    )(er, block_b, factor_c, after)


def prepare_kernel(a_hbm, b_hbm, launch_hbm, open_hbm, own_ref, b_ref, late_ref, launch_ref, open_ref, sems):
    pairs = ((b_hbm, b_ref), (launch_hbm, launch_ref), (open_hbm, open_ref), (a_hbm, own_ref))
    copies = [pltpu.make_async_copy(x, y, sems.at[k]) for k, (x, y) in enumerate(pairs)]
    for copy in copies:
        copy.start()
    for copy in copies:
        copy.wait()
    lanes = launch_ref.shape[1]
    opened = open_ref[...]
    for k in range(launch_ref.shape[0]):
        turned = jnp.broadcast_to(launch_ref[k : k + 1, :], (lanes, lanes)).T
        for j in range(opened.shape[1] // lanes):
            part = slice(j * lanes, (j + 1) * lanes)
            late_ref[k * lanes : (k + 1) * lanes, part] = jnp.maximum(turned, opened[:, part])


def join_kernel(own_ref, other_ref, b0, b1, b2, b3, a_out, b_out):
    sub, share = own_ref.shape[0], b0.shape[0]
    a_out[:sub, :] = own_ref[...]
    a_out[sub:, :] = other_ref[...]
    for d, ref in enumerate((b0, b1, b2, b3)):
        b_out[d * share : (d + 1) * share, :] = ref[...]


def assemble_kernel(w0, w1, w2, w3, q0, q1, q2, q3, items_ref, b_ref):
    rows = items_ref.shape[0] // 32 * 8
    for d, ref in enumerate((w0, w1, w2, w3)):
        items_ref[d * rows : (d + 1) * rows, :] = ref[:rows, :]
    if w0.shape[0] > rows:
        items_ref[4 * rows :, :] = (w0[rows:, :] + w1[rows:, :]) + (w2[rows:, :] + w3[rows:, :])
    place_stores((q0, q1, q2, q3), b_ref)


def place_stores(quarters, out_ref):
    share = out_ref.shape[0] // 16
    for e, ref in enumerate(quarters):
        for d in range(4):
            out_ref[pl.ds(row_of("item", share, 4 * e + d), share), :] = ref[d * share : (d + 1) * share, :]


def pack_kernel(used, gbt_ref, mine_ref, core_ref, *refs):
    outs, gb = refs[:4], refs[4]
    gb[...] = gbt_ref[...].T
    share = gb.shape[0] // 16
    more = used - 4 * share
    for e, out in enumerate(outs):
        for d in range(4):
            out[d * share : (d + 1) * share, :] = gb[pl.ds(row_of("item", share, 4 * e + d), share), :]
        out[4 * share : used, :] = mine_ref[:more, :] + core_ref[:more, :]
        if out.shape[0] > used:
            out[used:, :] = jnp.zeros((out.shape[0] - used, out.shape[1]), F32)


def pack_call(gbt, mine, core, used, rows):
    rank, n_stores = gbt.shape
    return pl.pallas_call(
        functools.partial(pack_kernel, used),
        out_shape=[jax.ShapeDtypeStruct((rows, rank), F32)] * 4,
        in_specs=[VM] * 3,
        out_specs=[VM] * 4,
        scratch_shapes=[pltpu.VMEM((n_stores, rank), F32)],
        compiler_params=pltpu.CompilerParams(vmem_limit_bytes=8 * MIB),
        cost_estimate=pl.CostEstimate(flops=LONG, bytes_accessed=0, transcendentals=0),
    )(gbt, mine, core)


def core_sum_kernel(own_ref, got_ref, *outs):
    rows = outs[0].shape[0]
    for k, out in enumerate(outs):
        part = slice(k * rows, (k + 1) * rows)
        out[...] = own_ref[part, :] + got_ref[part, :]


def sum_after_kernel(*refs):
    refs[-1][...] = tree([ref[...] for ref in refs[:-2]])


def sum_kernel(*refs):
    rows = refs[-1].shape[0]
    refs[-1][...] = tree([ref[:rows, :] for ref in refs[:-1]])


def mid_kernel(rate_a, rate_b, share, x0, z1, z2, z3, oldb_ref, mine, got, olda_ref, newb_ref, out_ref):
    terms = (x0, z1, z2, z3)
    for k in range(4):
        total = tree([t[(k ^ d) * share : ((k ^ d) + 1) * share, :] for d, t in enumerate(terms)])
        part = slice(k * share, (k + 1) * share)
        newb_ref[part, :] = oldb_ref[part, :] - rate_b * total
    n = mine.shape[0]
    half = n // 2
    out_ref[:half, :] = olda_ref[:half, :] - rate_a * (mine[:half, :] + got[half:, :])
    out_ref[half:n, :] = olda_ref[half:, :] - rate_a * (mine[half:, :] + got[:half, :])
    out_ref[n:, :] = tree([t[4 * share :, :] for t in terms])


def deal_kernel(share, q0, r1, r2, r3, *outs):
    for d, out in enumerate(outs):
        part = slice(d * share, (d + 1) * share)
        out[:share, :] = (q0[part, :] + r1[part, :]) + (r2[part, :] + r3[part, :])
        out[share:, :] = (q0[4 * share :, :] + r1[4 * share :, :]) + (r2[4 * share :, :] + r3[4 * share :, :])


def halves_kernel(t0, u1, u2, u3, after_ref, keep_ref, send_ref):
    half = keep_ref.shape[0]
    grad = (t0[...] + u1[...]) + (u2[...] + u3[...])
    keep_ref[...] = grad[:half, :]
    send_ref[...] = grad[half:, :]


def last_kernel(rate_b, d0, z1, z2, z3, b_ref, newb_ref, weeks_ref):
    share = newb_ref.shape[0]
    total = (d0[...] + z1[...]) + (z2[...] + z3[...])
    newb_ref[...] = b_ref[:share, :] - rate_b * total[:share, :]
    weeks_ref[...] = total[share:, :]


def end_kernel(rate_a, rate_c, count, keep, got, old_ref, e0, e1, e2, e3, c_ref, newa_ref, newc_ref, loss_ref):
    newa_ref[...] = old_ref[: keep.shape[0], :] - rate_a * (keep[...] + got[...])
    total = (e0[...] + e1[...]) + (e2[...] + e3[...])
    weeks = c_ref.shape[0]
    newc_ref[...] = c_ref[...] - rate_c * total[:weeks, :]
    for k in range(2):
        loss_ref[k] = jnp.sum(total[weeks + k : weeks + k + 1, :]) / count


def body(sales, launch_week, open_week, item_factors, store_factors, week_factors):
    weeks, n_items, n_stores = sales.shape
    total_items = n_items * lax.axis_size("item")
    total_stores = n_stores * lax.axis_size("store")
    count = total_items * total_stores * weeks
    rate_a = 40.0 / (total_stores * weeks)
    rate_b = 40.0 / (total_items * weeks)
    rate_c = 40.0 / (total_items * total_stores)
    sub, rank = item_factors.shape
    share = store_factors.shape[0]
    pair, quarter = (2 * sub, rank), (4 * share, rank)

    def over(values, axis, partners):
        return [swap(v, axis, d) for v, d in zip(values, partners)]

    other = swap(item_factors, "store", ZHI)
    own, own_b, late = pl.pallas_call(
        prepare_kernel,
        out_shape=[
            jax.ShapeDtypeStruct((sub, rank), F32),
            jax.ShapeDtypeStruct((share, rank), F32),
            jax.ShapeDtypeStruct((n_items, n_stores), jnp.int32),
        ],
        in_specs=[pl.BlockSpec(memory_space=pltpu.HBM)] * 4,
        out_specs=[VM] * 3,
        scratch_shapes=[
            pltpu.VMEM((n_items // rank, rank), jnp.int32),
            pltpu.VMEM((1, n_stores), jnp.int32),
            pltpu.SemaphoreType.DMA((4,)),
        ],
        compiler_params=pltpu.CompilerParams(vmem_limit_bytes=8 * MIB),
    )(*[
        pltpu.with_memory_space_constraint(x, pltpu.HBM)
        for x in (item_factors, store_factors, launch_week.reshape(-1, rank), open_week.reshape(1, -1))
    ])
    near = over([own_b] * 3, "item", ZLOS)
    mine_a, mine_b = small_call(join_kernel, [pair, quarter], own, other, own_b, *near, flops=LONG)
    rows = [mine_a] + over([mine_a] * 3, "store", OUTER)
    quarters = [mine_b] + over([mine_b] * 3, "item", OUTER)
    items, block_b = small_call(assemble_kernel, [(8 * sub, rank), (n_stores, rank)], *rows, *quarters, flops=LONG)
    others = swap(items, "store", CORE)
    old = jnp.zeros((weeks + 8, rank), F32)
    errors, gbt, old, factor_c = step_call(sub, rate_c, False, sales, late, block_b, week_factors, old, items, others)

    (part_c,) = small_call(sum_kernel, [(weeks + 8, rank)], old, swap(old, "store", CORE))
    got_c = swap(part_c, "store", ZHI)
    send, own = items_grad_call(errors, block_b, factor_c, part_c)
    parts = small_call(core_sum_kernel, [pair] * 4, own, swap(send, "store", CORE))
    parts = [parts[0]] + over(parts[1:], "store", OUTER)
    dealt = pack_call(gbt, part_c, got_c, 4 * share + weeks, 2 * sub + weeks)
    dealt = [dealt[0]] + over(dealt[1:], "item", OUTER)
    (part_a,) = small_call(sum_after_kernel, [pair], *parts, dealt[0])
    got_a = swap(part_a, "store", ZHI)
    (part_b,) = small_call(sum_kernel, [(4 * share + weeks, rank)], *dealt)
    near = over([part_b] * 3, "item", ZLOS)
    mine_b, packed = small_call(
        functools.partial(mid_kernel, rate_a, rate_b, share),
        [quarter, (2 * sub + weeks, rank)],
        part_b, *near, mine_b, part_a, got_a, mine_a,
    )
    rows = [packed] + over([packed] * 3, "store", OUTER)
    quarters = [mine_b] + over([mine_b] * 3, "item", OUTER)
    items, block_b = small_call(
        assemble_kernel, [(8 * sub + weeks, rank), (n_stores, rank)], *rows, *quarters
    )
    others = swap(items, "store", CORE)
    errors, gbt, old, factor_c = step_call(sub, rate_c, True, sales, late, block_b, factor_c, old, items, others)

    (part_c,) = small_call(sum_kernel, [(weeks + 8, rank)], old, swap(old, "store", CORE))
    got_c = swap(part_c, "store", ZHI)
    send, own = items_grad_call(errors, block_b, factor_c, part_c)
    parts = small_call(core_sum_kernel, [pair] * 4, own, swap(send, "store", CORE))
    parts = [parts[0]] + over(parts[1:], "store", OUTER)
    dealt = pack_call(gbt, part_c, got_c, 4 * share + weeks + 8, 4 * share + weeks + 8)
    dealt = [dealt[0]] + over(dealt[1:], "item", OUTER)
    keep, send = small_call(halves_kernel, [(sub, rank)] * 2, *parts, dealt[0])
    got_a = swap(send, "store", ZHI)
    near = small_call(functools.partial(deal_kernel, share), [(share + weeks + 8, rank)] * 4, *dealt)
    near = [near[0]] + over(near[1:], "item", ZLOS)
    shard_b, part_c = small_call(
        functools.partial(last_kernel, rate_b), [(share, rank), (weeks + 8, rank)], *near, mine_b
    )
    shard_a, factor_c, losses = pl.pallas_call(
        functools.partial(end_kernel, rate_a, rate_c, 2.0 * count),
        out_shape=[jax.ShapeDtypeStruct(s, F32) for s in ((sub, rank), (weeks, rank), (2,))],
        in_specs=[VM] * 8,
        out_specs=[VM, VM, pl.BlockSpec(memory_space=pltpu.SMEM)],
        compiler_params=pltpu.CompilerParams(vmem_limit_bytes=8 * MIB),
        cost_estimate=pl.CostEstimate(flops=0, bytes_accessed=0, transcendentals=0),
    )(keep, got_a, packed, part_c, *over([part_c] * 3, "store", OUTER), factor_c)
    return shard_a, shard_b, factor_c, losses


def solution(mesh):
    in_specs = (
        P(None, "item", "store"),
        P("item"),
        P("store"),
        P(("item", "store"), None),
        P(("store", "item"), None),
        P(),
    )
    out_specs = (P(("item", "store"), None), P(("store", "item"), None), P(), P())
    return jax.shard_map(body, mesh=mesh, in_specs=in_specs, out_specs=out_specs, check_vma=False)
```

profile of v0, /device:TPU:6, one launch (start us, length us, event | category | flops | bytes accessed | tf_op | source)
XLA Modules:
  0.0 117.1 jit_solution(3046944900805141722)
XLA Ops:
  0.6 7.3 %collective-permute-start = (f32[64,128]{1,0:T(8,128)}, f32[64,128]{1,0:T(8,128)S(1)}, u32[]{:S(2)}, u32[]{:S(2)}) collective-permute-start(f32[64,128]{1,0:T(8,128)} %a_hbm.1), channel_id=1, source_target_pairs={{0,2},{1,3},{2,0},{3,1},{4,6},{5,7},{6,4},{7,5},{8,10},{9,11},{10,... | collective-permute-start | bytes 98312 | tf_op jit(solution)/shard_map/ppermute | solution.py:21
  9.0 2.0 %collective-permute-start.3 = (f32[16,128]{1,0:T(8,128)S(1)}, f32[16,128]{1,0:T(8,128)S(1)}, u32[]{:S(2)}, u32[]{:S(2)}) collective-permute-start(f32[16,128]{1,0:T(8,128)S(1)} %get-tuple-element.56.b0), channel_id=1, source_target_pairs={{0,48},{16,32},{32,16},{48,0},{64,112},{80,96},{96,80},{112,64},{1... | collective-permute-start | bytes 24584 | tf_op jit(solution)/shard_map/ppermute | solution.py:21
  11.6 1.9 %collective-permute-start.1 = (f32[16,128]{1,0:T(8,128)S(1)}, f32[16,128]{1,0:T(8,128)S(1)}, u32[]{:S(2)}, u32[]{:S(2)}) collective-permute-start(f32[16,128]{1,0:T(8,128)S(1)} %get-tuple-element.56.b0), channel_id=1, source_target_pairs={{0,16},{16,0},{32,48},{48,32},{64,80},{80,64},{96,112},{112,96},{1... | collective-permute-start | bytes 24584 | tf_op jit(solution)/shard_map/ppermute | solution.py:21
  16.1 3.0 %collective-permute-start.6 = (f32[128,128]{1,0:T(8,128)S(1)}, f32[128,128]{1,0:T(8,128)S(1)}, u32[]{:S(2)}, u32[]{:S(2)}) collective-permute-start(f32[128,128]{1,0:T(8,128)S(1)} %get-tuple-element.57.w0.olda_ref), channel_id=1, source_target_pairs={{0,12},{1,13},{2,14},{3,15},{4,8},{5,9},{6,10},{7,11},{8,4},{9,5},... | collective-permute-start | bytes 196616 | tf_op jit(solution)/shard_map/ppermute | solution.py:21
  20.2 2.4 %collective-permute-start.8 = (f32[64,128]{1,0:T(8,128)S(1)}, f32[64,128]{1,0:T(8,128)S(1)}, u32[]{:S(2)}, u32[]{:S(2)}) collective-permute-start(f32[64,128]{1,0:T(8,128)S(1)} %get-tuple-element.58.q0.oldb_ref), channel_id=1, source_target_pairs={{0,128},{16,144},{32,160},{48,176},{64,192},{80,208},{96,224},{112... | collective-permute-start | bytes 98312 | tf_op jit(solution)/shard_map/ppermute | solution.py:21
  23.9 1.8 %collective-permute-done.8.q2 = f32[64,128]{1,0:T(8,128)S(1)} collective-permute-done((f32[64,128]{1,0:T(8,128)S(1)}, f32[64,128]{1,0:T(8,128)S(1)}, u32[]{:S(2)}, u32[]{:S(2)}) %collective-permute-start.8) | collective-permute-done | bytes 32800 | tf_op jit(solution)/shard_map/ppermute | solution.py:21
  28.3 1.7 %copy-done = f32[8,1024,256]{2,1,0:T(8,128)S(1)} copy-done((f32[8,1024,256]{2,1,0:T(8,128)S(1)}, f32[8,1024,256]{2,1,0:T(8,128)}, u32[]{:S(2)}) %copy-start) | copy-done | bytes 8388632
  30.0 4.0 %shard_map.96 = (bf16[8,1024,256]{2,1,0:T(8,128)(2,1)S(1)}, f32[128,256]{1,0:T(8,128)S(1)}, f32[16,128]{1,0:T(8,128)S(1)}, f32[8,128]{1,0:T(8,128)S(1)}) custom-call(f32[8,1024,256]{2,1,0:T(8,128)S(1)} %copy-done, s32[1024,256]{1,0:T(8,128)S(1)} %get-tuple-element.54.refs_1_, f32[256,128]{1,0:T(8,128)S(1)} %get-tuple-element.59.refs_2_.b_ref, ...), custom_call_target="tpu_custom_call" | custom-call | flops 1073741824 | bytes 8388608 | tf_op jit(solution)/shard_map/pallas_call | solution.py:132
  36.7 1.6 %collective-permute-start.12 = (f32[16,128]{1,0:T(8,128)S(1)}, f32[16,128]{1,0:T(8,128)S(1)}, u32[]{:S(2)}, u32[]{:S(2)}) collective-permute-start(f32[16,128]{1,0:T(8,128)S(1)} %shard_map.97.mine_ref.after_ref), channel_id=1, source_target_pairs={{0,2},{1,3},{2,0},{3,1},{4,6},{5,7},{6,4},{7,5},{8,10},{9,11},{10,... | collective-permute-start | bytes 24584 | tf_op jit(solution)/shard_map/ppermute | solution.py:21
  38.3 1.7 %collective-permute-start.20 = (f32[128,128]{1,0:T(8,128)S(1)}, f32[128,128]{1,0:T(8,128)S(1)}, u32[]{:S(2)}, u32[]{:S(2)}) collective-permute-start(f32[128,128]{1,0:T(8,128)S(1)} %get-tuple-element.72), channel_id=1, source_target_pairs={{0,4},{1,5},{2,6},{3,7},{4,0},{5,1},{6,2},{7,3},{8,12},{9,13},{10,... | collective-permute-start | bytes 196616 | tf_op jit(solution)/shard_map/ppermute | solution.py:21
  40.0 2.9 %collective-permute-start.21 = (f32[128,128]{1,0:T(8,128)S(1)}, f32[128,128]{1,0:T(8,128)S(1)}, u32[]{:S(2)}, u32[]{:S(2)}) collective-permute-start(f32[128,128]{1,0:T(8,128)S(1)} %get-tuple-element.73), channel_id=1, source_target_pairs={{0,8},{1,9},{2,10},{3,11},{4,12},{5,13},{6,14},{7,15},{8,0},{9,1},... | collective-permute-start | bytes 196616 | tf_op jit(solution)/shard_map/ppermute | solution.py:21
  45.8 2.1 %collective-permute-start.14 = (f32[136,128]{1,0:T(8,128)S(1)}, f32[136,128]{1,0:T(8,128)S(1)}, u32[]{:S(2)}, u32[]{:S(2)}) collective-permute-start(f32[136,128]{1,0:T(8,128)S(1)} %get-tuple-element.65), channel_id=1, source_target_pairs={{0,128},{16,144},{32,160},{48,176},{64,192},{80,208},{96,224},{112... | collective-permute-start | bytes 208904 | tf_op jit(solution)/shard_map/ppermute | solution.py:21
  49.4 3.6 %collective-permute-start.23 = (f32[128,128]{1,0:T(8,128)S(1)}, f32[128,128]{1,0:T(8,128)S(1)}, u32[]{:S(2)}, u32[]{:S(2)}) collective-permute-start(f32[128,128]{1,0:T(8,128)S(1)} %shard_map.102.mine), channel_id=1, source_target_pairs={{0,2},{1,3},{2,0},{3,1},{4,6},{5,7},{6,4},{7,5},{8,10},{9,11},{10,... | collective-permute-start | bytes 196616 | tf_op jit(solution)/shard_map/ppermute | solution.py:21
  53.5 2.0 %collective-permute-start.18 = (f32[72,128]{1,0:T(8,128)S(1)}, f32[72,128]{1,0:T(8,128)S(1)}, u32[]{:S(2)}, u32[]{:S(2)}) collective-permute-start(f32[72,128]{1,0:T(8,128)S(1)} %shard_map.99.x0), channel_id=1, source_target_pairs={{0,48},{16,32},{32,16},{48,0},{64,112},{80,96},{96,80},{112,64},{1... | collective-permute-start | bytes 110600 | tf_op jit(solution)/shard_map/ppermute | solution.py:21
  58.0 1.5 %collective-permute-done.18.z3 = f32[72,128]{1,0:T(8,128)S(1)} collective-permute-done((f32[72,128]{1,0:T(8,128)S(1)}, f32[72,128]{1,0:T(8,128)S(1)}, u32[]{:S(2)}, u32[]{:S(2)}) %collective-permute-start.18) | collective-permute-done | bytes 36896 | tf_op jit(solution)/shard_map/ppermute | solution.py:21
  60.8 3.2 %collective-permute-start.26 = (f32[136,128]{1,0:T(8,128)S(1)}, f32[136,128]{1,0:T(8,128)S(1)}, u32[]{:S(2)}, u32[]{:S(2)}) collective-permute-start(f32[136,128]{1,0:T(8,128)S(1)} %get-tuple-element.75.w0.old_ref), channel_id=1, source_target_pairs={{0,12},{1,13},{2,14},{3,15},{4,8},{5,9},{6,10},{7,11},{8,4},{9,5},... | collective-permute-start | bytes 208904 | tf_op jit(solution)/shard_map/ppermute | solution.py:21
  64.9 1.6 %collective-permute-start.29 = (f32[64,128]{1,0:T(8,128)S(1)}, f32[64,128]{1,0:T(8,128)S(1)}, u32[]{:S(2)}, u32[]{:S(2)}) collective-permute-start(f32[64,128]{1,0:T(8,128)S(1)} %get-tuple-element.76.q0.b_ref), channel_id=1, source_target_pairs={{0,192},{16,208},{32,224},{48,240},{64,128},{80,144},{96,160},{112... | collective-permute-start | bytes 98312 | tf_op jit(solution)/shard_map/ppermute | solution.py:21
  67.8 2.2 %collective-permute-done.29.q3 = f32[64,128]{1,0:T(8,128)S(1)} collective-permute-done((f32[64,128]{1,0:T(8,128)S(1)}, f32[64,128]{1,0:T(8,128)S(1)}, u32[]{:S(2)}, u32[]{:S(2)}) %collective-permute-start.29) | collective-permute-done | bytes 32800 | tf_op jit(solution)/shard_map/ppermute | solution.py:21
  70.1 1.9 %collective-permute-done.28.q2 = f32[64,128]{1,0:T(8,128)S(1)} collective-permute-done((f32[64,128]{1,0:T(8,128)S(1)}, f32[64,128]{1,0:T(8,128)S(1)}, u32[]{:S(2)}, u32[]{:S(2)}) %collective-permute-start.28) | collective-permute-done | bytes 32800 | tf_op jit(solution)/shard_map/ppermute | solution.py:21
  71.9 2.0 %collective-permute-done.27.q1 = f32[64,128]{1,0:T(8,128)S(1)} collective-permute-done((f32[64,128]{1,0:T(8,128)S(1)}, f32[64,128]{1,0:T(8,128)S(1)}, u32[]{:S(2)}, u32[]{:S(2)}) %collective-permute-start.27) | collective-permute-done | bytes 32800 | tf_op jit(solution)/shard_map/ppermute | solution.py:21
  74.4 1.5 %collective-permute-done.30.refs_6_ = f32[520,128]{1,0:T(8,128)S(1)} collective-permute-done((f32[520,128]{1,0:T(8,128)S(1)}, f32[520,128]{1,0:T(8,128)S(1)}, u32[]{:S(2)}, u32[]{:S(2)}) %collective-permute-start.30) | collective-permute-done | bytes 266272 | tf_op jit(solution)/shard_map/ppermute | solution.py:21
  75.9 3.9 %shard_map.105 = (bf16[8,1024,256]{2,1,0:T(8,128)(2,1)S(1)}, f32[128,256]{1,0:T(8,128)S(1)}, f32[16,128]{1,0:T(8,128)S(1)}, f32[8,128]{1,0:T(8,128)S(1)}) custom-call(f32[8,1024,256]{2,1,0:T(8,128)S(1)} %copy-done, s32[1024,256]{1,0:T(8,128)S(1)} %get-tuple-element.54.refs_1_, f32[256,128]{1,0:T(8,128)S(1)} %get-tuple-element.77.refs_2_.b_ref, ...), custom_call_target="tpu_custom_call" | custom-call | flops 1073741824 | bytes 8388608 | tf_op jit(solution)/shard_map/pallas_call | solution.py:132
  82.7 3.3 %collective-permute-start.36 = (f32[16,128]{1,0:T(8,128)S(1)}, f32[16,128]{1,0:T(8,128)S(1)}, u32[]{:S(2)}, u32[]{:S(2)}) collective-permute-start(f32[16,128]{1,0:T(8,128)S(1)} %shard_map.106.after_ref.mine_ref), channel_id=1, source_target_pairs={{0,2},{1,3},{2,0},{3,1},{4,6},{5,7},{6,4},{7,5},{8,10},{9,11},{10,... | collective-permute-start | bytes 24584 | tf_op jit(solution)/shard_map/ppermute | solution.py:21
  87.0 3.5 %collective-permute-start.34 = (f32[128,128]{1,0:T(8,128)S(1)}, f32[128,128]{1,0:T(8,128)S(1)}, u32[]{:S(2)}, u32[]{:S(2)}) collective-permute-start(f32[128,128]{1,0:T(8,128)S(1)} %get-tuple-element.86), channel_id=1, source_target_pairs={{0,8},{1,9},{2,10},{3,11},{4,12},{5,13},{6,14},{7,15},{8,0},{9,1},... | collective-permute-start | bytes 196616 | tf_op jit(solution)/shard_map/ppermute | solution.py:21
  91.0 2.9 %collective-permute-start.39 = (f32[80,128]{1,0:T(8,128)S(1)}, f32[80,128]{1,0:T(8,128)S(1)}, u32[]{:S(2)}, u32[]{:S(2)}) collective-permute-start(f32[80,128]{1,0:T(8,128)S(1)} %get-tuple-element.93), channel_id=1, source_target_pairs={{0,128},{16,144},{32,160},{48,176},{64,192},{80,208},{96,224},{112... | collective-permute-start | bytes 122888 | tf_op jit(solution)/shard_map/ppermute | solution.py:21
  94.0 1.7 %collective-permute-start.40 = (f32[80,128]{1,0:T(8,128)S(1)}, f32[80,128]{1,0:T(8,128)S(1)}, u32[]{:S(2)}, u32[]{:S(2)}) collective-permute-start(f32[80,128]{1,0:T(8,128)S(1)} %get-tuple-element.94), channel_id=1, source_target_pairs={{0,192},{16,208},{32,224},{48,240},{64,128},{80,144},{96,160},{112... | collective-permute-start | bytes 122888 | tf_op jit(solution)/shard_map/ppermute | solution.py:21
  96.1 2.8 %collective-permute-start.37 = (f32[64,128]{1,0:T(8,128)S(1)}, f32[64,128]{1,0:T(8,128)S(1)}, u32[]{:S(2)}, u32[]{:S(2)}) collective-permute-start(f32[64,128]{1,0:T(8,128)S(1)} %get-tuple-element.91), channel_id=1, source_target_pairs={{0,2},{1,3},{2,0},{3,1},{4,6},{5,7},{6,4},{7,5},{8,10},{9,11},{10,... | collective-permute-start | bytes 98312 | tf_op jit(solution)/shard_map/ppermute | solution.py:21
  100.2 1.6 %collective-permute-start.42 = (f32[32,128]{1,0:T(8,128)S(1)}, f32[32,128]{1,0:T(8,128)S(1)}, u32[]{:S(2)}, u32[]{:S(2)}) collective-permute-start(f32[32,128]{1,0:T(8,128)S(1)} %get-tuple-element.97), channel_id=1, source_target_pairs={{0,32},{16,48},{32,0},{48,16},{64,96},{80,112},{96,64},{112,80},{1... | collective-permute-start | bytes 49160 | tf_op jit(solution)/shard_map/ppermute | solution.py:21
  101.8 1.9 %collective-permute-start.43 = (f32[32,128]{1,0:T(8,128)S(1)}, f32[32,128]{1,0:T(8,128)S(1)}, u32[]{:S(2)}, u32[]{:S(2)}) collective-permute-start(f32[32,128]{1,0:T(8,128)S(1)} %get-tuple-element.98), channel_id=1, source_target_pairs={{0,48},{16,32},{32,16},{48,0},{64,112},{80,96},{96,80},{112,64},{1... | collective-permute-start | bytes 49160 | tf_op jit(solution)/shard_map/ppermute | solution.py:21
  104.9 2.5 %collective-permute-done.43.z3 = f32[32,128]{1,0:T(8,128)S(1)} collective-permute-done((f32[32,128]{1,0:T(8,128)S(1)}, f32[32,128]{1,0:T(8,128)S(1)}, u32[]{:S(2)}, u32[]{:S(2)}) %collective-permute-start.43) | collective-permute-done | bytes 16416 | tf_op jit(solution)/shard_map/ppermute | solution.py:21
  107.9 3.1 %collective-permute-start.46 = (f32[16,128]{1,0:T(8,128)S(1)}, f32[16,128]{1,0:T(8,128)S(1)}, u32[]{:S(2)}, u32[]{:S(2)}) collective-permute-start(f32[16,128]{1,0:T(8,128)S(1)} %get-tuple-element.99.e0), channel_id=1, source_target_pairs={{0,12},{1,13},{2,14},{3,15},{4,8},{5,9},{6,10},{7,11},{8,4},{9,5},... | collective-permute-start | bytes 24584 | tf_op jit(solution)/shard_map/ppermute | solution.py:21
  112.8 3.4 %collective-permute-done.45.e2 = f32[16,128]{1,0:T(8,128)S(1)} collective-permute-done((f32[16,128]{1,0:T(8,128)S(1)}, f32[16,128]{1,0:T(8,128)S(1)}, u32[]{:S(2)}, u32[]{:S(2)}) %collective-permute-start.45) | collective-permute-done | bytes 8224 | tf_op jit(solution)/shard_map/ppermute | solution.py:21
  (88 shorter events, 33.3 us)
Async XLA Ops:
  0.6 14.9 %collective-permute-start = (f32[64,128]{1,0:T(8,128)}, f32[64,128]{1,0:T(8,128)S(1)}, u32[]{:S(2)}, u32[]{:S(2)}) collective-permute-start(f32[64,128]{1,0:T(8,128)} %a_hbm.1), channel_id=1, source_target_pairs={{0,2},{1,3},{2,0},{3,1},{4,6},{5,7},{6,4},{7,5},{8,10},{9,11},{10,... | collective-permute-start | bytes 98312 | tf_op jit(solution)/shard_map/ppermute | solution.py:21
  9.0 5.5 %collective-permute-start.3 = (f32[16,128]{1,0:T(8,128)S(1)}, f32[16,128]{1,0:T(8,128)S(1)}, u32[]{:S(2)}, u32[]{:S(2)}) collective-permute-start(f32[16,128]{1,0:T(8,128)S(1)} %get-tuple-element.56.b0), channel_id=1, source_target_pairs={{0,48},{16,32},{32,16},{48,0},{64,112},{80,96},{96,80},{112,64},{1... | collective-permute-start | bytes 24584 | tf_op jit(solution)/shard_map/ppermute | solution.py:21
  15.6 7.1 %collective-permute-start.9 = (f32[64,128]{1,0:T(8,128)S(1)}, f32[64,128]{1,0:T(8,128)S(1)}, u32[]{:S(2)}, u32[]{:S(2)}) collective-permute-start(f32[64,128]{1,0:T(8,128)S(1)} %get-tuple-element.58.q0.oldb_ref), channel_id=1, source_target_pairs={{0,192},{16,208},{32,224},{48,240},{64,128},{80,144},{96,160},{112... | collective-permute-start | bytes 98312 | tf_op jit(solution)/shard_map/ppermute | solution.py:21
  16.1 10.4 %collective-permute-start.6 = (f32[128,128]{1,0:T(8,128)S(1)}, f32[128,128]{1,0:T(8,128)S(1)}, u32[]{:S(2)}, u32[]{:S(2)}) collective-permute-start(f32[128,128]{1,0:T(8,128)S(1)} %get-tuple-element.57.w0.olda_ref), channel_id=1, source_target_pairs={{0,12},{1,13},{2,14},{3,15},{4,8},{5,9},{6,10},{7,11},{8,4},{9,5},... | collective-permute-start | bytes 196616 | tf_op jit(solution)/shard_map/ppermute | solution.py:21
  19.1 7.4 %collective-permute-start.5 = (f32[128,128]{1,0:T(8,128)S(1)}, f32[128,128]{1,0:T(8,128)S(1)}, u32[]{:S(2)}, u32[]{:S(2)}) collective-permute-start(f32[128,128]{1,0:T(8,128)S(1)} %get-tuple-element.57.w0.olda_ref), channel_id=1, source_target_pairs={{0,8},{1,9},{2,10},{3,11},{4,12},{5,13},{6,14},{7,15},{8,0},{9,1},... | collective-permute-start | bytes 196616 | tf_op jit(solution)/shard_map/ppermute | solution.py:21
  19.8 6.8 %collective-permute-start.4 = (f32[128,128]{1,0:T(8,128)S(1)}, f32[128,128]{1,0:T(8,128)S(1)}, u32[]{:S(2)}, u32[]{:S(2)}) collective-permute-start(f32[128,128]{1,0:T(8,128)S(1)} %get-tuple-element.57.w0.olda_ref), channel_id=1, source_target_pairs={{0,4},{1,5},{2,6},{3,7},{4,0},{5,1},{6,2},{7,3},{8,12},{9,13},{10,... | collective-permute-start | bytes 196616 | tf_op jit(solution)/shard_map/ppermute | solution.py:21
  20.2 5.4 %collective-permute-start.8 = (f32[64,128]{1,0:T(8,128)S(1)}, f32[64,128]{1,0:T(8,128)S(1)}, u32[]{:S(2)}, u32[]{:S(2)}) collective-permute-start(f32[64,128]{1,0:T(8,128)S(1)} %get-tuple-element.58.q0.oldb_ref), channel_id=1, source_target_pairs={{0,128},{16,144},{32,160},{48,176},{64,192},{80,208},{96,224},{112... | collective-permute-start | bytes 98312 | tf_op jit(solution)/shard_map/ppermute | solution.py:21
  36.7 7.7 %collective-permute-start.12 = (f32[16,128]{1,0:T(8,128)S(1)}, f32[16,128]{1,0:T(8,128)S(1)}, u32[]{:S(2)}, u32[]{:S(2)}) collective-permute-start(f32[16,128]{1,0:T(8,128)S(1)} %shard_map.97.mine_ref.after_ref), channel_id=1, source_target_pairs={{0,2},{1,3},{2,0},{3,1},{4,6},{5,7},{6,4},{7,5},{8,10},{9,11},{10,... | collective-permute-start | bytes 24584 | tf_op jit(solution)/shard_map/ppermute | solution.py:21
  38.3 9.6 %collective-permute-start.20 = (f32[128,128]{1,0:T(8,128)S(1)}, f32[128,128]{1,0:T(8,128)S(1)}, u32[]{:S(2)}, u32[]{:S(2)}) collective-permute-start(f32[128,128]{1,0:T(8,128)S(1)} %get-tuple-element.72), channel_id=1, source_target_pairs={{0,4},{1,5},{2,6},{3,7},{4,0},{5,1},{6,2},{7,3},{8,12},{9,13},{10,... | collective-permute-start | bytes 196616 | tf_op jit(solution)/shard_map/ppermute | solution.py:21
  40.0 9.3 %collective-permute-start.21 = (f32[128,128]{1,0:T(8,128)S(1)}, f32[128,128]{1,0:T(8,128)S(1)}, u32[]{:S(2)}, u32[]{:S(2)}) collective-permute-start(f32[128,128]{1,0:T(8,128)S(1)} %get-tuple-element.73), channel_id=1, source_target_pairs={{0,8},{1,9},{2,10},{3,11},{4,12},{5,13},{6,14},{7,15},{8,0},{9,1},... | collective-permute-start | bytes 196616 | tf_op jit(solution)/shard_map/ppermute | solution.py:21
  42.9 6.4 %collective-permute-start.22 = (f32[128,128]{1,0:T(8,128)S(1)}, f32[128,128]{1,0:T(8,128)S(1)}, u32[]{:S(2)}, u32[]{:S(2)}) collective-permute-start(f32[128,128]{1,0:T(8,128)S(1)} %get-tuple-element.74), channel_id=1, source_target_pairs={{0,12},{1,13},{2,14},{3,15},{4,8},{5,9},{6,10},{7,11},{8,4},{9,5},... | collective-permute-start | bytes 196616 | tf_op jit(solution)/shard_map/ppermute | solution.py:21
  44.5 8.4 %collective-permute-start.13 = (f32[136,128]{1,0:T(8,128)S(1)}, f32[136,128]{1,0:T(8,128)S(1)}, u32[]{:S(2)}, u32[]{:S(2)}) collective-permute-start(f32[136,128]{1,0:T(8,128)S(1)} %get-tuple-element.64), channel_id=1, source_target_pairs={{0,64},{16,80},{32,96},{48,112},{64,0},{80,16},{96,32},{112,48},{1... | collective-permute-start | bytes 208904 | tf_op jit(solution)/shard_map/ppermute | solution.py:21
  45.8 7.2 %collective-permute-start.14 = (f32[136,128]{1,0:T(8,128)S(1)}, f32[136,128]{1,0:T(8,128)S(1)}, u32[]{:S(2)}, u32[]{:S(2)}) collective-permute-start(f32[136,128]{1,0:T(8,128)S(1)} %get-tuple-element.65), channel_id=1, source_target_pairs={{0,128},{16,144},{32,160},{48,176},{64,192},{80,208},{96,224},{112... | collective-permute-start | bytes 208904 | tf_op jit(solution)/shard_map/ppermute | solution.py:21
  47.9 5.5 %collective-permute-start.15 = (f32[136,128]{1,0:T(8,128)S(1)}, f32[136,128]{1,0:T(8,128)S(1)}, u32[]{:S(2)}, u32[]{:S(2)}) collective-permute-start(f32[136,128]{1,0:T(8,128)S(1)} %get-tuple-element.66), channel_id=1, source_target_pairs={{0,192},{16,208},{32,224},{48,240},{64,128},{80,144},{96,160},{112... | collective-permute-start | bytes 208904 | tf_op jit(solution)/shard_map/ppermute | solution.py:21
  49.4 11.4 %collective-permute-start.23 = (f32[128,128]{1,0:T(8,128)S(1)}, f32[128,128]{1,0:T(8,128)S(1)}, u32[]{:S(2)}, u32[]{:S(2)}) collective-permute-start(f32[128,128]{1,0:T(8,128)S(1)} %shard_map.102.mine), channel_id=1, source_target_pairs={{0,2},{1,3},{2,0},{3,1},{4,6},{5,7},{6,4},{7,5},{8,10},{9,11},{10,... | collective-permute-start | bytes 196616 | tf_op jit(solution)/shard_map/ppermute | solution.py:21
  53.5 6.0 %collective-permute-start.18 = (f32[72,128]{1,0:T(8,128)S(1)}, f32[72,128]{1,0:T(8,128)S(1)}, u32[]{:S(2)}, u32[]{:S(2)}) collective-permute-start(f32[72,128]{1,0:T(8,128)S(1)} %shard_map.99.x0), channel_id=1, source_target_pairs={{0,48},{16,32},{32,16},{48,0},{64,112},{80,96},{96,80},{112,64},{1... | collective-permute-start | bytes 110600 | tf_op jit(solution)/shard_map/ppermute | solution.py:21
  55.5 5.3 %collective-permute-start.17 = (f32[72,128]{1,0:T(8,128)S(1)}, f32[72,128]{1,0:T(8,128)S(1)}, u32[]{:S(2)}, u32[]{:S(2)}) collective-permute-start(f32[72,128]{1,0:T(8,128)S(1)} %shard_map.99.x0), channel_id=1, source_target_pairs={{0,32},{16,48},{32,0},{48,16},{64,96},{80,112},{96,64},{112,80},{1... | collective-permute-start | bytes 110600 | tf_op jit(solution)/shard_map/ppermute | solution.py:21
  60.8 13.2 %collective-permute-start.26 = (f32[136,128]{1,0:T(8,128)S(1)}, f32[136,128]{1,0:T(8,128)S(1)}, u32[]{:S(2)}, u32[]{:S(2)}) collective-permute-start(f32[136,128]{1,0:T(8,128)S(1)} %get-tuple-element.75.w0.old_ref), channel_id=1, source_target_pairs={{0,12},{1,13},{2,14},{3,15},{4,8},{5,9},{6,10},{7,11},{8,4},{9,5},... | collective-permute-start | bytes 208904 | tf_op jit(solution)/shard_map/ppermute | solution.py:21
  63.9 10.0 %collective-permute-start.25 = (f32[136,128]{1,0:T(8,128)S(1)}, f32[136,128]{1,0:T(8,128)S(1)}, u32[]{:S(2)}, u32[]{:S(2)}) collective-permute-start(f32[136,128]{1,0:T(8,128)S(1)} %get-tuple-element.75.w0.old_ref), channel_id=1, source_target_pairs={{0,8},{1,9},{2,10},{3,11},{4,12},{5,13},{6,14},{7,15},{8,0},{9,1},... | collective-permute-start | bytes 208904 | tf_op jit(solution)/shard_map/ppermute | solution.py:21
  64.6 9.4 %collective-permute-start.24 = (f32[136,128]{1,0:T(8,128)S(1)}, f32[136,128]{1,0:T(8,128)S(1)}, u32[]{:S(2)}, u32[]{:S(2)}) collective-permute-start(f32[136,128]{1,0:T(8,128)S(1)} %get-tuple-element.75.w0.old_ref), channel_id=1, source_target_pairs={{0,4},{1,5},{2,6},{3,7},{4,0},{5,1},{6,2},{7,3},{8,12},{9,13},{10,... | collective-permute-start | bytes 208904 | tf_op jit(solution)/shard_map/ppermute | solution.py:21
  64.9 5.1 %collective-permute-start.29 = (f32[64,128]{1,0:T(8,128)S(1)}, f32[64,128]{1,0:T(8,128)S(1)}, u32[]{:S(2)}, u32[]{:S(2)}) collective-permute-start(f32[64,128]{1,0:T(8,128)S(1)} %get-tuple-element.76.q0.b_ref), channel_id=1, source_target_pairs={{0,192},{16,208},{32,224},{48,240},{64,128},{80,144},{96,160},{112... | collective-permute-start | bytes 98312 | tf_op jit(solution)/shard_map/ppermute | solution.py:21
  66.5 5.4 %collective-permute-start.28 = (f32[64,128]{1,0:T(8,128)S(1)}, f32[64,128]{1,0:T(8,128)S(1)}, u32[]{:S(2)}, u32[]{:S(2)}) collective-permute-start(f32[64,128]{1,0:T(8,128)S(1)} %get-tuple-element.76.q0.b_ref), channel_id=1, source_target_pairs={{0,128},{16,144},{32,160},{48,176},{64,192},{80,208},{96,224},{112... | collective-permute-start | bytes 98312 | tf_op jit(solution)/shard_map/ppermute | solution.py:21
  82.7 8.2 %collective-permute-start.36 = (f32[16,128]{1,0:T(8,128)S(1)}, f32[16,128]{1,0:T(8,128)S(1)}, u32[]{:S(2)}, u32[]{:S(2)}) collective-permute-start(f32[16,128]{1,0:T(8,128)S(1)} %shard_map.106.after_ref.mine_ref), channel_id=1, source_target_pairs={{0,2},{1,3},{2,0},{3,1},{4,6},{5,7},{6,4},{7,5},{8,10},{9,11},{10,... | collective-permute-start | bytes 24584 | tf_op jit(solution)/shard_map/ppermute | solution.py:21
  86.0 8.0 %collective-permute-start.33 = (f32[128,128]{1,0:T(8,128)S(1)}, f32[128,128]{1,0:T(8,128)S(1)}, u32[]{:S(2)}, u32[]{:S(2)}) collective-permute-start(f32[128,128]{1,0:T(8,128)S(1)} %get-tuple-element.85), channel_id=1, source_target_pairs={{0,4},{1,5},{2,6},{3,7},{4,0},{5,1},{6,2},{7,3},{8,12},{9,13},{10,... | collective-permute-start | bytes 196616 | tf_op jit(solution)/shard_map/ppermute | solution.py:21
  87.0 8.7 %collective-permute-start.34 = (f32[128,128]{1,0:T(8,128)S(1)}, f32[128,128]{1,0:T(8,128)S(1)}, u32[]{:S(2)}, u32[]{:S(2)}) collective-permute-start(f32[128,128]{1,0:T(8,128)S(1)} %get-tuple-element.86), channel_id=1, source_target_pairs={{0,8},{1,9},{2,10},{3,11},{4,12},{5,13},{6,14},{7,15},{8,0},{9,1},... | collective-permute-start | bytes 196616 | tf_op jit(solution)/shard_map/ppermute | solution.py:21
  90.6 5.5 %collective-permute-start.35 = (f32[128,128]{1,0:T(8,128)S(1)}, f32[128,128]{1,0:T(8,128)S(1)}, u32[]{:S(2)}, u32[]{:S(2)}) collective-permute-start(f32[128,128]{1,0:T(8,128)S(1)} %get-tuple-element.87), channel_id=1, source_target_pairs={{0,12},{1,13},{2,14},{3,15},{4,8},{5,9},{6,10},{7,11},{8,4},{9,5},... | collective-permute-start | bytes 196616 | tf_op jit(solution)/shard_map/ppermute | solution.py:21
  90.9 7.9 %collective-permute-start.38 = (f32[80,128]{1,0:T(8,128)S(1)}, f32[80,128]{1,0:T(8,128)S(1)}, u32[]{:S(2)}, u32[]{:S(2)}) collective-permute-start(f32[80,128]{1,0:T(8,128)S(1)} %get-tuple-element.92), channel_id=1, source_target_pairs={{0,64},{16,80},{32,96},{48,112},{64,0},{80,16},{96,32},{112,48},{1... | collective-permute-start | bytes 122888 | tf_op jit(solution)/shard_map/ppermute | solution.py:21
  91.0 7.8 %collective-permute-start.39 = (f32[80,128]{1,0:T(8,128)S(1)}, f32[80,128]{1,0:T(8,128)S(1)}, u32[]{:S(2)}, u32[]{:S(2)}) collective-permute-start(f32[80,128]{1,0:T(8,128)S(1)} %get-tuple-element.93), channel_id=1, source_target_pairs={{0,128},{16,144},{32,160},{48,176},{64,192},{80,208},{96,224},{112... | collective-permute-start | bytes 122888 | tf_op jit(solution)/shard_map/ppermute | solution.py:21
  94.0 5.2 %collective-permute-start.40 = (f32[80,128]{1,0:T(8,128)S(1)}, f32[80,128]{1,0:T(8,128)S(1)}, u32[]{:S(2)}, u32[]{:S(2)}) collective-permute-start(f32[80,128]{1,0:T(8,128)S(1)} %get-tuple-element.94), channel_id=1, source_target_pairs={{0,192},{16,208},{32,224},{48,240},{64,128},{80,144},{96,160},{112... | collective-permute-start | bytes 122888 | tf_op jit(solution)/shard_map/ppermute | solution.py:21
  96.1 20.2 %collective-permute-start.37 = (f32[64,128]{1,0:T(8,128)S(1)}, f32[64,128]{1,0:T(8,128)S(1)}, u32[]{:S(2)}, u32[]{:S(2)}) collective-permute-start(f32[64,128]{1,0:T(8,128)S(1)} %get-tuple-element.91), channel_id=1, source_target_pairs={{0,2},{1,3},{2,0},{3,1},{4,6},{5,7},{6,4},{7,5},{8,10},{9,11},{10,... | collective-permute-start | bytes 98312 | tf_op jit(solution)/shard_map/ppermute | solution.py:21
  101.8 5.5 %collective-permute-start.43 = (f32[32,128]{1,0:T(8,128)S(1)}, f32[32,128]{1,0:T(8,128)S(1)}, u32[]{:S(2)}, u32[]{:S(2)}) collective-permute-start(f32[32,128]{1,0:T(8,128)S(1)} %get-tuple-element.98), channel_id=1, source_target_pairs={{0,48},{16,32},{32,16},{48,0},{64,112},{80,96},{96,80},{112,64},{1... | collective-permute-start | bytes 49160 | tf_op jit(solution)/shard_map/ppermute | solution.py:21
  111.1 5.2 %collective-permute-start.45 = (f32[16,128]{1,0:T(8,128)S(1)}, f32[16,128]{1,0:T(8,128)S(1)}, u32[]{:S(2)}, u32[]{:S(2)}) collective-permute-start(f32[16,128]{1,0:T(8,128)S(1)} %get-tuple-element.99.e0), channel_id=1, source_target_pairs={{0,8},{1,9},{2,10},{3,11},{4,12},{5,13},{6,14},{7,15},{8,0},{9,1},... | collective-permute-start | bytes 24584 | tf_op jit(solution)/shard_map/ppermute | solution.py:21
  (17 other events, 66.4 us)
where the time goes:
time: 117 us
  starting transfers between devices  71.8 us (61%)
  waiting for transfers between devices  29.3 us (25%)
  Pallas kernels  13.3 us (11%)
  local copies, waits for them, and re-layouts  1.72 us (1%)
    ppermute x47, starting transfers between devices, swap(): return lax.ppermute(value, axis, [(i, i ^ bits) for i in range(16)])  71.8 us
    ppermute x47, waiting for transfers between devices, swap(): return lax.ppermute(value, axis, [(i, i ^ bits) for i in range(16)])  29.3 us
    pallas_call x2, Pallas kernels, step_call(): pl.pallas_call(functools.partial(step_kernel, sub, rate_c, riding), out_s...  7.9 us
    pallas_call x2, Pallas kernels, items_grad_call(): pl.pallas_call(items_grad_kernel, out_shape=[jax.ShapeDtypeStruct((n_item...  2.6 us
  transfers between devices with their start and end apart: 47, of which 21 were waited for; matrix products, arithmetic and copies ran while one was open for 0% of the time, Pallas kernels for 2%

commit v1 on v0

--- a/solution.py
+++ b/solution.py
@@ -19,6 +19,17 @@
 
 def swap(value, axis, bits):
     return lax.ppermute(value, axis, [(i, i ^ bits) for i in range(16)])
+
+
+def chip_swap(value, item_way, store_way):
+    pairs = []
+    for item in range(16):
+        for store in range(16):
+            if store & CORE:
+                pairs.append((item * 16 + store, (item ^ store_way) * 16 + store))
+            elif item_way:
+                pairs.append((item * 16 + store, item * 16 + (store ^ item_way)))
+    return lax.ppermute(value, ("item", "store"), pairs)
 
 
 def split(value):
@@ -50,21 +61,14 @@
     )(*args)
 
 
-def step_kernel(sub, rate_c, riding, *refs):
-    sales_ref, late_ref, b_ref, c_ref, old_weeks = refs[:5]
-    rows_of = refs[5:7]
-    er, gbt_ref, weeks_ref, newc_ref = refs[7:11]
-    a_f, a3, at = refs[11:]
+def step_kernel(rate_c, riding, *refs):
+    sales_ref, late_ref, a_ref, b_ref, c_ref, old_weeks = refs[:6]
+    er, gbt_ref, weeks_ref, newc_ref, a3, at = refs[-6:]
     weeks, n_items, n_stores = sales_ref.shape
-    rank = a_f.shape[1]
+    rank = a_ref.shape[1]
     rows = 256
 
-    for o in range(2):
-        for d in range(4):
-            for h in range(2):
-                row = row_of("store", sub, 4 * d + 2 * h + o)
-                a_f[pl.ds(row, sub), :] = rows_of[o][(2 * d + h) * sub : (2 * d + h + 1) * sub, :]
-    a = a_f[...]
+    a = a_ref[...]
     high, low = split(a)
     a3[:, :rank] = high
     a3[:, rank : 2 * rank] = low
@@ -76,7 +80,7 @@
     bt = b.T
     c = c_ref[...]
     if riding:
-        c = c - rate_c * rows_of[0][8 * sub :, :]
+        c = c - rate_c * refs[6][...]
     newc_ref[...] = c
 
     def factor(w):
@@ -124,18 +128,17 @@
     weeks_ref[weeks:, :] = losses
 
 
-def step_call(sub, rate_c, riding, sales, late, block_b, factor_c, old_weeks, mine, other):
+def step_call(rate_c, riding, sales, late, block_a, block_b, factor_c, old_weeks, *grad_c):
     weeks, n_items, n_stores = sales.shape
     rank = block_b.shape[1]
     outs = [(rank, n_stores), (weeks + 8, rank), (weeks, rank)]
-    args = [sales, late, block_b, factor_c, old_weeks, mine, other]
+    args = [sales, late, block_a, block_b, factor_c, old_weeks, *grad_c]
     return pl.pallas_call(
-        functools.partial(step_kernel, sub, rate_c, riding),
+        functools.partial(step_kernel, rate_c, riding),
         out_shape=[jax.ShapeDtypeStruct(sales.shape, BF16)] + [jax.ShapeDtypeStruct(s, F32) for s in outs],
         in_specs=[VM] * len(args),
         out_specs=[VM] * (1 + len(outs)),
         scratch_shapes=[
-            pltpu.VMEM((n_items, rank), F32),
             pltpu.VMEM((n_items, 3 * rank), BF16),
             pltpu.VMEM((2 * rank, n_items), BF16),
         ],
@@ -196,28 +199,111 @@
             late_ref[k * lanes : (k + 1) * lanes, part] = jnp.maximum(turned, opened[:, part])
 
 
-def join_kernel(own_ref, other_ref, b0, b1, b2, b3, a_out, b_out):
-    sub, share = own_ref.shape[0], b0.shape[0]
-    a_out[:sub, :] = own_ref[...]
-    a_out[sub:, :] = other_ref[...]
-    for d, ref in enumerate((b0, b1, b2, b3)):
-        b_out[d * share : (d + 1) * share, :] = ref[...]
-
-
-def assemble_kernel(w0, w1, w2, w3, q0, q1, q2, q3, items_ref, b_ref):
-    rows = items_ref.shape[0] // 32 * 8
+def on_core(which):
+    return pl.when(lax.axis_index("store") % 2 == which)
+
+
+def near_kernel(own_a, other_a, own_b, other_b, z1, z2):
+    sub, share = own_a.shape[0], own_b.shape[0]
+
+    @on_core(0)
+    def _():
+        z1[:sub, :] = own_a[...]
+        z1[sub:, :] = other_a[...]
+        z2[...] = jnp.zeros_like(z2)
+
+    @on_core(1)
+    def _():
+        z1[...] = jnp.zeros_like(z1)
+        for ref in (z1, z2):
+            ref[:share, :] = other_b[...]
+            ref[share : 2 * share, :] = own_b[...]
+
+
+def join_kernel(z1, z2, g1, g2, g3, out_ref):
+    rows, few = z1.shape[0], z2.shape[0]
+
+    @on_core(0)
+    def _():
+        out_ref[:rows, :] = z1[...]
+        out_ref[rows:, :] = g1[...]
+
+    @on_core(1)
+    def _():
+        out_ref[:few, :] = z2[...]
+        out_ref[few : 2 * few, :] = g1[:few, :]
+        out_ref[2 * few : 3 * few, :] = g2[...]
+        out_ref[3 * few : 4 * few, :] = g3[...]
+        out_ref[4 * few :, :] = jnp.zeros((out_ref.shape[0] - 4 * few, out_ref.shape[1]), F32)
+
+
+def merge_kernel(sub, share, mine, other, out_ref):
+    weeks = mine.shape[0] - 2 * sub - 4 * share
+    first = 2 * sub + weeks
+
+    @on_core(0)
+    def _():
+        for h in range(2):
+            part = slice(h * sub, (h + 1) * sub)
+            out_ref[2 * h * sub : (2 * h + 1) * sub, :] = mine[part, :]
+            out_ref[(2 * h + 1) * sub : (2 * h + 2) * sub, :] = other[part, :]
+        out_ref[4 * sub :, :] = mine[2 * sub : first, :]
+
+    @on_core(1)
+    def _():
+        for d in range(4):
+            part = slice(first + d * share, first + (d + 1) * share)
+            out_ref[2 * d * share : (2 * d + 1) * share, :] = other[part, :]
+            out_ref[(2 * d + 1) * share : (2 * d + 2) * share, :] = mine[part, :]
+        out_ref[8 * share :, :] = jnp.zeros((out_ref.shape[0] - 8 * share, out_ref.shape[1]), F32)
+
+
+def stack_kernel(rows, w0, w1, w2, w3, out_ref):
     for d, ref in enumerate((w0, w1, w2, w3)):
-        items_ref[d * rows : (d + 1) * rows, :] = ref[:rows, :]
+        out_ref[d * rows : (d + 1) * rows, :] = ref[:rows, :]
     if w0.shape[0] > rows:
-        items_ref[4 * rows :, :] = (w0[rows:, :] + w1[rows:, :]) + (w2[rows:, :] + w3[rows:, :])
-    place_stores((q0, q1, q2, q3), b_ref)
-
-
-def place_stores(quarters, out_ref):
-    share = out_ref.shape[0] // 16
-    for e, ref in enumerate(quarters):
-        for d in range(4):
-            out_ref[pl.ds(row_of("item", share, 4 * e + d), share), :] = ref[d * share : (d + 1) * share, :]
+        out_ref[4 * rows :, :] = (w0[rows:, :] + w1[rows:, :]) + (w2[rows:, :] + w3[rows:, :])
+
+
+def unstack_kernel(sub, share, mine, other, a_ref, b_ref, near_a, near_b, *weeks_ref):
+    core = lax.axis_index("store") % 2
+    store, item = lax.axis_index("store") - core, lax.axis_index("item")
+    rows = 4 * sub
+    for which, items, stores in ((0, mine, other), (1, other, mine)):
+
+        @on_core(which)
+        def _():
+            for d in range(4):
+                for h in range(2):
+                    for o in range(2):
+                        to = pl.multiple_of(((store ^ (4 * d + 2 * h)) + o) * sub, sub)
+                        at = d * rows + (2 * h + o) * sub
+                        a_ref[pl.ds(to, sub), :] = items[at : at + sub, :]
+            for e in range(4):
+                for d in range(4):
+                    to = pl.multiple_of((item ^ (4 * e + d)) * share, share)
+                    at = e * rows + (2 * d + which) * share
+                    b_ref[pl.ds(to, share), :] = stores[at : at + share, :]
+            for h in range(2):
+                at = (2 * h + which) * sub
+                near_a[h * sub : (h + 1) * sub, :] = items[at : at + sub, :]
+            for d in range(4):
+                at = (2 * d + which) * share
+                near_b[d * share : (d + 1) * share, :] = stores[at : at + share, :]
+            for ref in weeks_ref:
+                ref[...] = items[4 * rows :, :]
+
+
+def far_gather(sub, share, value, weeks, flops=None):
+    rank = value.shape[1]
+    rows = [value] + [chip_swap(value, d, d) for d in OUTER]
+    (stack,) = small_call(
+        functools.partial(stack_kernel, 4 * sub), [(16 * sub + weeks, rank)], *rows, flops=flops
+    )
+    outs = [(16 * sub, rank), (16 * share, rank), (2 * sub, rank), (4 * share, rank)]
+    outs = outs + ([(weeks, rank)] if weeks else [])
+    other = swap(stack, "store", CORE)
+    return small_call(functools.partial(unstack_kernel, sub, share), outs, stack, other)
 
 
 def pack_kernel(used, gbt_ref, mine_ref, core_ref, *refs):
@@ -262,17 +348,18 @@
     refs[-1][...] = tree([ref[:rows, :] for ref in refs[:-1]])
 
 
-def mid_kernel(rate_a, rate_b, share, x0, z1, z2, z3, oldb_ref, mine, got, olda_ref, newb_ref, out_ref):
+def mid_kernel(rate_a, rate_b, share, x0, z1, z2, z3, oldb_ref, mine, got, olda_ref, out_ref):
     terms = (x0, z1, z2, z3)
+    n = mine.shape[0]
+    half = n // 2
+    first = n + x0.shape[0] - 4 * share
     for k in range(4):
         total = tree([t[(k ^ d) * share : ((k ^ d) + 1) * share, :] for d, t in enumerate(terms)])
         part = slice(k * share, (k + 1) * share)
-        newb_ref[part, :] = oldb_ref[part, :] - rate_b * total
-    n = mine.shape[0]
-    half = n // 2
+        out_ref[first + k * share : first + (k + 1) * share, :] = oldb_ref[part, :] - rate_b * total
     out_ref[:half, :] = olda_ref[:half, :] - rate_a * (mine[:half, :] + got[half:, :])
     out_ref[half:n, :] = olda_ref[half:, :] - rate_a * (mine[half:, :] + got[:half, :])
-    out_ref[n:, :] = tree([t[4 * share :, :] for t in terms])
+    out_ref[n:first, :] = tree([t[4 * share :, :] for t in terms])
 
 
 def deal_kernel(share, q0, r1, r2, r3, *outs):
@@ -320,7 +407,8 @@
     def over(values, axis, partners):
         return [swap(v, axis, d) for v, d in zip(values, partners)]
 
-    other = swap(item_factors, "store", ZHI)
+    other_a = swap(item_factors, "store", CORE)
+    other_b = swap(store_factors, "store", CORE)
     own, own_b, late = pl.pallas_call(
         prepare_kernel,
         out_shape=[
@@ -340,14 +428,12 @@
         pltpu.with_memory_space_constraint(x, pltpu.HBM)
         for x in (item_factors, store_factors, launch_week.reshape(-1, rank), open_week.reshape(1, -1))
     ])
-    near = over([own_b] * 3, "item", ZLOS)
-    mine_a, mine_b = small_call(join_kernel, [pair, quarter], own, other, own_b, *near, flops=LONG)
-    rows = [mine_a] + over([mine_a] * 3, "store", OUTER)
-    quarters = [mine_b] + over([mine_b] * 3, "item", OUTER)
-    items, block_b = small_call(assemble_kernel, [(8 * sub, rank), (n_stores, rank)], *rows, *quarters, flops=LONG)
-    others = swap(items, "store", CORE)
+    z1, z2 = small_call(near_kernel, [pair, (2 * share, rank)], own, other_a, own_b, other_b)
+    near = [chip_swap(z1, ZHI, 1), chip_swap(z2, 0, 2), chip_swap(z2, 0, 3)]
+    (value,) = small_call(join_kernel, [(4 * sub, rank)], z1, z2, *near)
+    block_a, block_b, mine_a, mine_b = far_gather(sub, share, value, 0, flops=LONG)
     old = jnp.zeros((weeks + 8, rank), F32)
-    errors, gbt, old, factor_c = step_call(sub, rate_c, False, sales, late, block_b, week_factors, old, items, others)
+    errors, gbt, old, factor_c = step_call(rate_c, False, sales, late, block_a, block_b, week_factors, old)
 
     (part_c,) = small_call(sum_kernel, [(weeks + 8, rank)], old, swap(old, "store", CORE))
     got_c = swap(part_c, "store", ZHI)
@@ -360,18 +446,16 @@
     got_a = swap(part_a, "store", ZHI)
     (part_b,) = small_call(sum_kernel, [(4 * share + weeks, rank)], *dealt)
     near = over([part_b] * 3, "item", ZLOS)
-    mine_b, packed = small_call(
+    (new,) = small_call(
         functools.partial(mid_kernel, rate_a, rate_b, share),
-        [quarter, (2 * sub + weeks, rank)],
+        [(2 * sub + weeks + 4 * share, rank)],
         part_b, *near, mine_b, part_a, got_a, mine_a,
     )
-    rows = [packed] + over([packed] * 3, "store", OUTER)
-    quarters = [mine_b] + over([mine_b] * 3, "item", OUTER)
-    items, block_b = small_call(
-        assemble_kernel, [(8 * sub + weeks, rank), (n_stores, rank)], *rows, *quarters
+    (value,) = small_call(
+        functools.partial(merge_kernel, sub, share), [(4 * sub + weeks, rank)], new, swap(new, "store", CORE)
     )
-    others = swap(items, "store", CORE)
-    errors, gbt, old, factor_c = step_call(sub, rate_c, True, sales, late, block_b, factor_c, old, items, others)
+    block_a, block_b, mine_a, mine_b, grad_c = far_gather(sub, share, value, weeks)
+    errors, gbt, old, factor_c = step_call(rate_c, True, sales, late, block_a, block_b, factor_c, old, grad_c)
 
     (part_c,) = small_call(sum_kernel, [(weeks + 8, rank)], old, swap(old, "store", CORE))
     got_c = swap(part_c, "store", ZHI)
@@ -394,7 +478,7 @@
         out_specs=[VM, VM, pl.BlockSpec(memory_space=pltpu.SMEM)],
         compiler_params=pltpu.CompilerParams(vmem_limit_bytes=8 * MIB),
         cost_estimate=pl.CostEstimate(flops=0, bytes_accessed=0, transcendentals=0),
-    )(keep, got_a, packed, part_c, *over([part_c] * 3, "store", OUTER), factor_c)
+    )(keep, got_a, mine_a, part_c, *over([part_c] * 3, "store", OUTER), factor_c)
     return shard_a, shard_b, factor_c, losses
 
 

time: 117 us -> 111 us (0.949)
  starting transfers between devices: 71.8 us -> 66.2 us
    ppermute x47 -> x34, starting transfers between devices: 71.8 us -> 49.2 us  [swap(): return lax.ppermute(value, axis, [(i, i ^ bits) for i in range(16)])]
    ppermute x0 -> x9, starting transfers between devices: none -> 16.9 us  [chip_swap(): return lax.ppermute(value, ('item', 'store'), pairs)]
    ppermute x47 -> x34, waiting for transfers between devices: 29.3 us -> 17.5 us  [swap(): return lax.ppermute(value, axis, [(i, i ^ bits) for i in range(16)])]
    ppermute x0 -> x9, waiting for transfers between devices: none -> 11.2 us  [chip_swap(): return lax.ppermute(value, ('item', 'store'), pairs)]
  transfers between devices with their start and end apart: 47 -> 43, of which waited for: 21 -> 17; matrix products, arithmetic and copies ran while one was open for 0% -> 0% of each run, Pallas kernels for 2% -> 2%
where the time goes in v1:
time: 111 us
  starting transfers between devices  66.2 us (60%)
  waiting for transfers between devices  28.8 us (26%)
  Pallas kernels  13.8 us (12%)
  local copies, waits for them, and re-layouts  1.27 us (1%)
    ppermute x34, starting transfers between devices, swap(): return lax.ppermute(value, axis, [(i, i ^ bits) for i in range(16)])  49.2 us
    ppermute x34, waiting for transfers between devices, swap(): return lax.ppermute(value, axis, [(i, i ^ bits) for i in range(16)])  17.5 us
    ppermute x9, starting transfers between devices, chip_swap(): return lax.ppermute(value, ('item', 'store'), pairs)  16.9 us
    ppermute x9, waiting for transfers between devices, chip_swap(): return lax.ppermute(value, ('item', 'store'), pairs)  11.2 us
    pallas_call x2, Pallas kernels, step_call(): pl.pallas_call(functools.partial(step_kernel, rate_c, riding), out_shape=...  8.29 us
    pallas_call x2, Pallas kernels, items_grad_call(): pl.pallas_call(items_grad_kernel, out_shape=[jax.ShapeDtypeStruct((n_item...  2.6 us
  transfers between devices with their start and end apart: 43, of which 17 were waited for; matrix products, arithmetic and copies ran while one was open for 0% of the time, Pallas kernels for 2%

profile of v1, /device:TPU:6, one launch (start us, length us, event | category | flops | bytes accessed | tf_op | source)
XLA Modules:
  0.0 111.1 jit_solution(10101096583082872629)
XLA Ops:
  2.3 7.3 %collective-permute-start.2 = (f32[128,128]{1,0:T(8,128)S(1)}, f32[128,128]{1,0:T(8,128)S(1)}, u32[]{:S(2)}, u32[]{:S(2)}) collective-permute-start(f32[128,128]{1,0:T(8,128)S(1)} %get-tuple-element.60.z1), channel_id=1, source_target_pairs={{0,2},{1,17},{2,0},{3,19},{4,6},{5,21},{6,4},{7,23},{8,10},{9,25},... | collective-permute-start | bytes 196616 | tf_op jit(solution)/shard_map/ppermute | solution.py:32
  12.3 3.1 %collective-permute-start.7 = (f32[256,128]{1,0:T(8,128)S(1)}, f32[256,128]{1,0:T(8,128)S(1)}, u32[]{:S(2)}, u32[]{:S(2)}) collective-permute-start(f32[256,128]{1,0:T(8,128)S(1)} %shard_map.95.w0), channel_id=1, source_target_pairs={{0,12},{1,193},{2,14},{3,195},{4,8},{5,197},{6,10},{7,199},{8,4},{... | collective-permute-start | bytes 393224 | tf_op jit(solution)/shard_map/ppermute | solution.py:32
  16.4 2.8 %collective-permute-done.7.w3 = f32[256,128]{1,0:T(8,128)S(1)} collective-permute-done((f32[256,128]{1,0:T(8,128)S(1)}, f32[256,128]{1,0:T(8,128)S(1)}, u32[]{:S(2)}, u32[]{:S(2)}) %collective-permute-start.7) | collective-permute-done | bytes 131104 | tf_op jit(solution)/shard_map/ppermute | solution.py:32
  19.3 2.5 %collective-permute-done.6.w2 = f32[256,128]{1,0:T(8,128)S(1)} collective-permute-done((f32[256,128]{1,0:T(8,128)S(1)}, f32[256,128]{1,0:T(8,128)S(1)}, u32[]{:S(2)}, u32[]{:S(2)}) %collective-permute-start.6) | collective-permute-done | bytes 131104 | tf_op jit(solution)/shard_map/ppermute | solution.py:32
  22.0 1.9 %collective-permute-done.8.other = f32[1024,128]{1,0:T(8,128)S(1)} collective-permute-done((f32[1024,128]{1,0:T(8,128)S(1)}, f32[1024,128]{1,0:T(8,128)S(1)}, u32[]{:S(2)}, u32[]{:S(2)}) %collective-permute-start.8) | collective-permute-done | bytes 524320 | tf_op jit(solution)/shard_map/ppermute | solution.py:21
  25.2 4.2 %shard_map.98 = (bf16[8,1024,256]{2,1,0:T(8,128)(2,1)S(1)}, f32[128,256]{1,0:T(8,128)S(1)}, f32[16,128]{1,0:T(8,128)S(1)}, f32[8,128]{1,0:T(8,128)S(1)}) custom-call(f32[8,1024,256]{2,1,0:T(8,128)S(1)} %copy-done, s32[1024,256]{1,0:T(8,128)S(1)} %get-tuple-element.57.refs_1_, f32[1024,128]{1,0:T(8,128)S(1)} %get-tuple-element.62.refs_2_, ...), custom_call_target="tpu_custom_call" | custom-call | flops 1073741824 | bytes 8388608 | tf_op jit(solution)/shard_map/pallas_call | solution.py:136
  30.6 1.3 %shard_map.102 = (f32[512,128]{1,0:T(8,128)S(1)}, f32[512,128]{1,0:T(8,128)S(1)}) custom-call(bf16[8,1024,256]{2,1,0:T(8,128)(2,1)S(1)} %get-tuple-element.71.er, f32[256,128]{1,0:T(8,128)S(1)} %get-tuple-element.63.refs_3_.b_ref, f32[8,128]{1,0:T(8,128)S(1)} %get-tuple-element.72.c_ref.refs_4_, f32[16,128]{1,0:T(8,128)S(1)} %shard_map.99.mine_ref.after_ref), custom_call_target="tpu_custom_call" | custom-call | tf_op jit(solution)/shard_map/pallas_call | solution.py:175
  32.2 6.3 %collective-permute-start.10 = (f32[16,128]{1,0:T(8,128)S(1)}, f32[16,128]{1,0:T(8,128)S(1)}, u32[]{:S(2)}, u32[]{:S(2)}) collective-permute-start(f32[16,128]{1,0:T(8,128)S(1)} %shard_map.99.mine_ref.after_ref), channel_id=1, source_target_pairs={{0,2},{1,3},{2,0},{3,1},{4,6},{5,7},{6,4},{7,5},{8,10},{9,11},{10,... | collective-permute-start | bytes 24584 | tf_op jit(solution)/shard_map/ppermute | solution.py:21
  39.1 2.9 %collective-permute-start.19 = (f32[128,128]{1,0:T(8,128)S(1)}, f32[128,128]{1,0:T(8,128)S(1)}, u32[]{:S(2)}, u32[]{:S(2)}) collective-permute-start(f32[128,128]{1,0:T(8,128)S(1)} %get-tuple-element.77), channel_id=1, source_target_pairs={{0,8},{1,9},{2,10},{3,11},{4,12},{5,13},{6,14},{7,15},{8,0},{9,1},... | collective-permute-start | bytes 196616 | tf_op jit(solution)/shard_map/ppermute | solution.py:21
  45.4 2.8 %collective-permute-start.13 = (f32[136,128]{1,0:T(8,128)S(1)}, f32[136,128]{1,0:T(8,128)S(1)}, u32[]{:S(2)}, u32[]{:S(2)}) collective-permute-start(f32[136,128]{1,0:T(8,128)S(1)} %get-tuple-element.69), channel_id=1, source_target_pairs={{0,192},{16,208},{32,224},{48,240},{64,128},{80,144},{96,160},{112... | collective-permute-start | bytes 208904 | tf_op jit(solution)/shard_map/ppermute | solution.py:21
  48.2 2.8 %collective-permute-start.21 = (f32[128,128]{1,0:T(8,128)S(1)}, f32[128,128]{1,0:T(8,128)S(1)}, u32[]{:S(2)}, u32[]{:S(2)}) collective-permute-start(f32[128,128]{1,0:T(8,128)S(1)} %shard_map.104.mine), channel_id=1, source_target_pairs={{0,2},{1,3},{2,0},{3,1},{4,6},{5,7},{6,4},{7,5},{8,10},{9,11},{10,... | collective-permute-start | bytes 196616 | tf_op jit(solution)/shard_map/ppermute | solution.py:21
  51.1 1.3 %collective-permute-start.16 = (f32[72,128]{1,0:T(8,128)S(1)}, f32[72,128]{1,0:T(8,128)S(1)}, u32[]{:S(2)}, u32[]{:S(2)}) collective-permute-start(f32[72,128]{1,0:T(8,128)S(1)} %shard_map.101.x0), channel_id=1, source_target_pairs={{0,48},{16,32},{32,16},{48,0},{64,112},{80,96},{96,80},{112,64},{1... | collective-permute-start | bytes 110600 | tf_op jit(solution)/shard_map/ppermute | solution.py:21
  52.9 2.6 %collective-permute-start.14 = (f32[72,128]{1,0:T(8,128)S(1)}, f32[72,128]{1,0:T(8,128)S(1)}, u32[]{:S(2)}, u32[]{:S(2)}) collective-permute-start(f32[72,128]{1,0:T(8,128)S(1)} %shard_map.101.x0), channel_id=1, source_target_pairs={{0,16},{16,0},{32,48},{48,32},{64,80},{80,64},{96,112},{112,96},{1... | collective-permute-start | bytes 110600 | tf_op jit(solution)/shard_map/ppermute | solution.py:21
  55.6 1.4 %collective-permute-done.16.z3 = f32[72,128]{1,0:T(8,128)S(1)} collective-permute-done((f32[72,128]{1,0:T(8,128)S(1)}, f32[72,128]{1,0:T(8,128)S(1)}, u32[]{:S(2)}, u32[]{:S(2)}) %collective-permute-start.16) | collective-permute-done | bytes 36896 | tf_op jit(solution)/shard_map/ppermute | solution.py:21
  59.4 2.3 %collective-permute-start.25 = (f32[264,128]{1,0:T(8,128)S(1)}, f32[264,128]{1,0:T(8,128)S(1)}, u32[]{:S(2)}, u32[]{:S(2)}) collective-permute-start(f32[264,128]{1,0:T(8,128)S(1)} %shard_map.106.w0), channel_id=1, source_target_pairs={{0,12},{1,193},{2,14},{3,195},{4,8},{5,197},{6,10},{7,199},{8,4},{... | collective-permute-start | bytes 405512 | tf_op jit(solution)/shard_map/ppermute | solution.py:32
  62.0 1.5 %collective-permute-start.23 = (f32[264,128]{1,0:T(8,128)S(1)}, f32[264,128]{1,0:T(8,128)S(1)}, u32[]{:S(2)}, u32[]{:S(2)}) collective-permute-start(f32[264,128]{1,0:T(8,128)S(1)} %shard_map.106.w0), channel_id=1, source_target_pairs={{0,4},{1,65},{2,6},{3,67},{4,0},{5,69},{6,2},{7,71},{8,12},{9,73},... | collective-permute-start | bytes 405512 | tf_op jit(solution)/shard_map/ppermute | solution.py:32
  63.5 2.1 %collective-permute-done.25.w3 = f32[264,128]{1,0:T(8,128)S(1)} collective-permute-done((f32[264,128]{1,0:T(8,128)S(1)}, f32[264,128]{1,0:T(8,128)S(1)}, u32[]{:S(2)}, u32[]{:S(2)}) %collective-permute-start.25) | collective-permute-done | bytes 135200 | tf_op jit(solution)/shard_map/ppermute | solution.py:32
  65.7 2.5 %collective-permute-done.24.w2 = f32[264,128]{1,0:T(8,128)S(1)} collective-permute-done((f32[264,128]{1,0:T(8,128)S(1)}, f32[264,128]{1,0:T(8,128)S(1)}, u32[]{:S(2)}, u32[]{:S(2)}) %collective-permute-start.24) | collective-permute-done | bytes 135200 | tf_op jit(solution)/shard_map/ppermute | solution.py:32
  68.3 1.9 %collective-permute-done.26.other = f32[1032,128]{1,0:T(8,128)S(1)} collective-permute-done((f32[1032,128]{1,0:T(8,128)S(1)}, f32[1032,128]{1,0:T(8,128)S(1)}, u32[]{:S(2)}, u32[]{:S(2)}) %collective-permute-start.26) | collective-permute-done | bytes 528416 | tf_op jit(solution)/shard_map/ppermute | solution.py:21
  70.2 4.1 %shard_map.109 = (bf16[8,1024,256]{2,1,0:T(8,128)(2,1)S(1)}, f32[128,256]{1,0:T(8,128)S(1)}, f32[16,128]{1,0:T(8,128)S(1)}, f32[8,128]{1,0:T(8,128)S(1)}) custom-call(f32[8,1024,256]{2,1,0:T(8,128)S(1)} %copy-done, s32[1024,256]{1,0:T(8,128)S(1)} %get-tuple-element.57.refs_1_, f32[1024,128]{1,0:T(8,128)S(1)} %get-tuple-element.80.refs_2_, ...), custom_call_target="tpu_custom_call" | custom-call | flops 1073741824 | bytes 8388608 | tf_op jit(solution)/shard_map/pallas_call | solution.py:136
  75.6 1.3 %shard_map.111 = (f32[512,128]{1,0:T(8,128)S(1)}, f32[512,128]{1,0:T(8,128)S(1)}) custom-call(bf16[8,1024,256]{2,1,0:T(8,128)(2,1)S(1)} %get-tuple-element.83.er, f32[256,128]{1,0:T(8,128)S(1)} %get-tuple-element.81.refs_3_.b_ref, f32[8,128]{1,0:T(8,128)S(1)} %get-tuple-element.84.c_ref, f32[16,128]{1,0:T(8,128)S(1)} %shard_map.110.after_ref.mine_ref), custom_call_target="tpu_custom_call" | custom-call | tf_op jit(solution)/shard_map/pallas_call | solution.py:175
  77.4 3.0 %collective-permute-start.32 = (f32[16,128]{1,0:T(8,128)S(1)}, f32[16,128]{1,0:T(8,128)S(1)}, u32[]{:S(2)}, u32[]{:S(2)}) collective-permute-start(f32[16,128]{1,0:T(8,128)S(1)} %shard_map.110.after_ref.mine_ref), channel_id=1, source_target_pairs={{0,2},{1,3},{2,0},{3,1},{4,6},{5,7},{6,4},{7,5},{8,10},{9,11},{10,... | collective-permute-start | bytes 24584 | tf_op jit(solution)/shard_map/ppermute | solution.py:21
  81.1 2.9 %collective-permute-start.30 = (f32[128,128]{1,0:T(8,128)S(1)}, f32[128,128]{1,0:T(8,128)S(1)}, u32[]{:S(2)}, u32[]{:S(2)}) collective-permute-start(f32[128,128]{1,0:T(8,128)S(1)} %get-tuple-element.90), channel_id=1, source_target_pairs={{0,8},{1,9},{2,10},{3,11},{4,12},{5,13},{6,14},{7,15},{8,0},{9,1},... | collective-permute-start | bytes 196616 | tf_op jit(solution)/shard_map/ppermute | solution.py:21
  85.7 3.4 %collective-permute-start.35 = (f32[80,128]{1,0:T(8,128)S(1)}, f32[80,128]{1,0:T(8,128)S(1)}, u32[]{:S(2)}, u32[]{:S(2)}) collective-permute-start(f32[80,128]{1,0:T(8,128)S(1)} %get-tuple-element.98), channel_id=1, source_target_pairs={{0,128},{16,144},{32,160},{48,176},{64,192},{80,208},{96,224},{112... | collective-permute-start | bytes 122888 | tf_op jit(solution)/shard_map/ppermute | solution.py:21
  90.2 3.0 %collective-permute-start.33 = (f32[64,128]{1,0:T(8,128)S(1)}, f32[64,128]{1,0:T(8,128)S(1)}, u32[]{:S(2)}, u32[]{:S(2)}) collective-permute-start(f32[64,128]{1,0:T(8,128)S(1)} %get-tuple-element.95), channel_id=1, source_target_pairs={{0,2},{1,3},{2,0},{3,1},{4,6},{5,7},{6,4},{7,5},{8,10},{9,11},{10,... | collective-permute-start | bytes 98312 | tf_op jit(solution)/shard_map/ppermute | solution.py:21
  94.3 1.7 %collective-permute-start.37 = (f32[32,128]{1,0:T(8,128)S(1)}, f32[32,128]{1,0:T(8,128)S(1)}, u32[]{:S(2)}, u32[]{:S(2)}) collective-permute-start(f32[32,128]{1,0:T(8,128)S(1)} %get-tuple-element.101), channel_id=1, source_target_pairs={{0,16},{16,0},{32,48},{48,32},{64,80},{80,64},{96,112},{112,96},{1... | collective-permute-start | bytes 49160 | tf_op jit(solution)/shard_map/ppermute | solution.py:21
  97.0 1.8 %collective-permute-start.39 = (f32[32,128]{1,0:T(8,128)S(1)}, f32[32,128]{1,0:T(8,128)S(1)}, u32[]{:S(2)}, u32[]{:S(2)}) collective-permute-start(f32[32,128]{1,0:T(8,128)S(1)} %get-tuple-element.103), channel_id=1, source_target_pairs={{0,48},{16,32},{32,16},{48,0},{64,112},{80,96},{96,80},{112,64},{1... | collective-permute-start | bytes 49160 | tf_op jit(solution)/shard_map/ppermute | solution.py:21
  98.8 1.9 %collective-permute-done.38.z2 = f32[32,128]{1,0:T(8,128)S(1)} collective-permute-done((f32[32,128]{1,0:T(8,128)S(1)}, f32[32,128]{1,0:T(8,128)S(1)}, u32[]{:S(2)}, u32[]{:S(2)}) %collective-permute-start.38) | collective-permute-done | bytes 16416 | tf_op jit(solution)/shard_map/ppermute | solution.py:21
  100.7 1.8 %collective-permute-done.39.z3 = f32[32,128]{1,0:T(8,128)S(1)} collective-permute-done((f32[32,128]{1,0:T(8,128)S(1)}, f32[32,128]{1,0:T(8,128)S(1)}, u32[]{:S(2)}, u32[]{:S(2)}) %collective-permute-start.39) | collective-permute-done | bytes 16416 | tf_op jit(solution)/shard_map/ppermute | solution.py:21
  103.1 2.0 %collective-permute-start.42 = (f32[16,128]{1,0:T(8,128)S(1)}, f32[16,128]{1,0:T(8,128)S(1)}, u32[]{:S(2)}, u32[]{:S(2)}) collective-permute-start(f32[16,128]{1,0:T(8,128)S(1)} %get-tuple-element.105.e0), channel_id=1, source_target_pairs={{0,12},{1,13},{2,14},{3,15},{4,8},{5,9},{6,10},{7,11},{8,4},{9,5},... | collective-permute-start | bytes 24584 | tf_op jit(solution)/shard_map/ppermute | solution.py:21
  105.8 1.5 %collective-permute-start.40 = (f32[16,128]{1,0:T(8,128)S(1)}, f32[16,128]{1,0:T(8,128)S(1)}, u32[]{:S(2)}, u32[]{:S(2)}) collective-permute-start(f32[16,128]{1,0:T(8,128)S(1)} %get-tuple-element.105.e0), channel_id=1, source_target_pairs={{0,4},{1,5},{2,6},{3,7},{4,0},{5,1},{6,2},{7,3},{8,12},{9,13},{10,... | collective-permute-start | bytes 24584 | tf_op jit(solution)/shard_map/ppermute | solution.py:21
  108.0 2.3 %collective-permute-done.41.e2 = f32[16,128]{1,0:T(8,128)S(1)} collective-permute-done((f32[16,128]{1,0:T(8,128)S(1)}, f32[16,128]{1,0:T(8,128)S(1)}, u32[]{:S(2)}, u32[]{:S(2)}) %collective-permute-start.41) | collective-permute-done | bytes 8224 | tf_op jit(solution)/shard_map/ppermute | solution.py:21
  (84 shorter events, 25.9 us)
Async XLA Ops:
  2.3 9.9 %collective-permute-start.2 = (f32[128,128]{1,0:T(8,128)S(1)}, f32[128,128]{1,0:T(8,128)S(1)}, u32[]{:S(2)}, u32[]{:S(2)}) collective-permute-start(f32[128,128]{1,0:T(8,128)S(1)} %get-tuple-element.60.z1), channel_id=1, source_target_pairs={{0,2},{1,17},{2,0},{3,19},{4,6},{5,21},{6,4},{7,23},{8,10},{9,25},... | collective-permute-start | bytes 196616 | tf_op jit(solution)/shard_map/ppermute | solution.py:32
  12.3 7.0 %collective-permute-start.7 = (f32[256,128]{1,0:T(8,128)S(1)}, f32[256,128]{1,0:T(8,128)S(1)}, u32[]{:S(2)}, u32[]{:S(2)}) collective-permute-start(f32[256,128]{1,0:T(8,128)S(1)} %shard_map.95.w0), channel_id=1, source_target_pairs={{0,12},{1,193},{2,14},{3,195},{4,8},{5,197},{6,10},{7,199},{8,4},{... | collective-permute-start | bytes 393224 | tf_op jit(solution)/shard_map/ppermute | solution.py:32
  15.4 6.5 %collective-permute-start.6 = (f32[256,128]{1,0:T(8,128)S(1)}, f32[256,128]{1,0:T(8,128)S(1)}, u32[]{:S(2)}, u32[]{:S(2)}) collective-permute-start(f32[256,128]{1,0:T(8,128)S(1)} %shard_map.95.w0), channel_id=1, source_target_pairs={{0,8},{1,129},{2,10},{3,131},{4,12},{5,133},{6,14},{7,135},{8,0},{... | collective-permute-start | bytes 393224 | tf_op jit(solution)/shard_map/ppermute | solution.py:32
  16.0 5.8 %collective-permute-start.5 = (f32[256,128]{1,0:T(8,128)S(1)}, f32[256,128]{1,0:T(8,128)S(1)}, u32[]{:S(2)}, u32[]{:S(2)}) collective-permute-start(f32[256,128]{1,0:T(8,128)S(1)} %shard_map.95.w0), channel_id=1, source_target_pairs={{0,4},{1,65},{2,6},{3,67},{4,0},{5,69},{6,2},{7,71},{8,12},{9,73},... | collective-permute-start | bytes 393224 | tf_op jit(solution)/shard_map/ppermute | solution.py:32
  31.9 6.5 %collective-permute-start.17 = (f32[512,128]{1,0:T(8,128)S(1)}, f32[512,128]{1,0:T(8,128)S(1)}, u32[]{:S(2)}, u32[]{:S(2)}) collective-permute-start(f32[512,128]{1,0:T(8,128)S(1)} %get-tuple-element.74), channel_id=1, source_target_pairs={{0,1},{1,0},{2,3},{3,2},{4,5},{5,4},{6,7},{7,6},{8,9},{9,8},{10,11... | collective-permute-start | bytes 786440 | tf_op jit(solution)/shard_map/ppermute | solution.py:21
  32.2 11.1 %collective-permute-start.10 = (f32[16,128]{1,0:T(8,128)S(1)}, f32[16,128]{1,0:T(8,128)S(1)}, u32[]{:S(2)}, u32[]{:S(2)}) collective-permute-start(f32[16,128]{1,0:T(8,128)S(1)} %shard_map.99.mine_ref.after_ref), channel_id=1, source_target_pairs={{0,2},{1,3},{2,0},{3,1},{4,6},{5,7},{6,4},{7,5},{8,10},{9,11},{10,... | collective-permute-start | bytes 24584 | tf_op jit(solution)/shard_map/ppermute | solution.py:21
  38.5 6.9 %collective-permute-start.18 = (f32[128,128]{1,0:T(8,128)S(1)}, f32[128,128]{1,0:T(8,128)S(1)}, u32[]{:S(2)}, u32[]{:S(2)}) collective-permute-start(f32[128,128]{1,0:T(8,128)S(1)} %get-tuple-element.76), channel_id=1, source_target_pairs={{0,4},{1,5},{2,6},{3,7},{4,0},{5,1},{6,2},{7,3},{8,12},{9,13},{10,... | collective-permute-start | bytes 196616 | tf_op jit(solution)/shard_map/ppermute | solution.py:21
  39.1 9.1 %collective-permute-start.19 = (f32[128,128]{1,0:T(8,128)S(1)}, f32[128,128]{1,0:T(8,128)S(1)}, u32[]{:S(2)}, u32[]{:S(2)}) collective-permute-start(f32[128,128]{1,0:T(8,128)S(1)} %get-tuple-element.77), channel_id=1, source_target_pairs={{0,8},{1,9},{2,10},{3,11},{4,12},{5,13},{6,14},{7,15},{8,0},{9,1},... | collective-permute-start | bytes 196616 | tf_op jit(solution)/shard_map/ppermute | solution.py:21
  42.0 6.2 %collective-permute-start.20 = (f32[128,128]{1,0:T(8,128)S(1)}, f32[128,128]{1,0:T(8,128)S(1)}, u32[]{:S(2)}, u32[]{:S(2)}) collective-permute-start(f32[128,128]{1,0:T(8,128)S(1)} %get-tuple-element.78), channel_id=1, source_target_pairs={{0,12},{1,13},{2,14},{3,15},{4,8},{5,9},{6,10},{7,11},{8,4},{9,5},... | collective-permute-start | bytes 196616 | tf_op jit(solution)/shard_map/ppermute | solution.py:21
  43.4 7.6 %collective-permute-start.11 = (f32[136,128]{1,0:T(8,128)S(1)}, f32[136,128]{1,0:T(8,128)S(1)}, u32[]{:S(2)}, u32[]{:S(2)}) collective-permute-start(f32[136,128]{1,0:T(8,128)S(1)} %get-tuple-element.67), channel_id=1, source_target_pairs={{0,64},{16,80},{32,96},{48,112},{64,0},{80,16},{96,32},{112,48},{1... | collective-permute-start | bytes 208904 | tf_op jit(solution)/shard_map/ppermute | solution.py:21
  44.3 6.7 %collective-permute-start.12 = (f32[136,128]{1,0:T(8,128)S(1)}, f32[136,128]{1,0:T(8,128)S(1)}, u32[]{:S(2)}, u32[]{:S(2)}) collective-permute-start(f32[136,128]{1,0:T(8,128)S(1)} %get-tuple-element.68), channel_id=1, source_target_pairs={{0,128},{16,144},{32,160},{48,176},{64,192},{80,208},{96,224},{112... | collective-permute-start | bytes 208904 | tf_op jit(solution)/shard_map/ppermute | solution.py:21
  45.4 5.6 %collective-permute-start.13 = (f32[136,128]{1,0:T(8,128)S(1)}, f32[136,128]{1,0:T(8,128)S(1)}, u32[]{:S(2)}, u32[]{:S(2)}) collective-permute-start(f32[136,128]{1,0:T(8,128)S(1)} %get-tuple-element.69), channel_id=1, source_target_pairs={{0,192},{16,208},{32,224},{48,240},{64,128},{80,144},{96,160},{112... | collective-permute-start | bytes 208904 | tf_op jit(solution)/shard_map/ppermute | solution.py:21
  48.2 9.7 %collective-permute-start.21 = (f32[128,128]{1,0:T(8,128)S(1)}, f32[128,128]{1,0:T(8,128)S(1)}, u32[]{:S(2)}, u32[]{:S(2)}) collective-permute-start(f32[128,128]{1,0:T(8,128)S(1)} %shard_map.104.mine), channel_id=1, source_target_pairs={{0,2},{1,3},{2,0},{3,1},{4,6},{5,7},{6,4},{7,5},{8,10},{9,11},{10,... | collective-permute-start | bytes 196616 | tf_op jit(solution)/shard_map/ppermute | solution.py:21
  51.1 5.8 %collective-permute-start.16 = (f32[72,128]{1,0:T(8,128)S(1)}, f32[72,128]{1,0:T(8,128)S(1)}, u32[]{:S(2)}, u32[]{:S(2)}) collective-permute-start(f32[72,128]{1,0:T(8,128)S(1)} %shard_map.101.x0), channel_id=1, source_target_pairs={{0,48},{16,32},{32,16},{48,0},{64,112},{80,96},{96,80},{112,64},{1... | collective-permute-start | bytes 110600 | tf_op jit(solution)/shard_map/ppermute | solution.py:21
  52.4 5.5 %collective-permute-start.15 = (f32[72,128]{1,0:T(8,128)S(1)}, f32[72,128]{1,0:T(8,128)S(1)}, u32[]{:S(2)}, u32[]{:S(2)}) collective-permute-start(f32[72,128]{1,0:T(8,128)S(1)} %shard_map.101.x0), channel_id=1, source_target_pairs={{0,32},{16,48},{32,0},{48,16},{64,96},{80,112},{96,64},{112,80},{1... | collective-permute-start | bytes 110600 | tf_op jit(solution)/shard_map/ppermute | solution.py:21
  52.9 5.0 %collective-permute-start.14 = (f32[72,128]{1,0:T(8,128)S(1)}, f32[72,128]{1,0:T(8,128)S(1)}, u32[]{:S(2)}, u32[]{:S(2)}) collective-permute-start(f32[72,128]{1,0:T(8,128)S(1)} %shard_map.101.x0), channel_id=1, source_target_pairs={{0,16},{16,0},{32,48},{48,32},{64,80},{80,64},{96,112},{112,96},{1... | collective-permute-start | bytes 110600 | tf_op jit(solution)/shard_map/ppermute | solution.py:21
  59.4 6.3 %collective-permute-start.25 = (f32[264,128]{1,0:T(8,128)S(1)}, f32[264,128]{1,0:T(8,128)S(1)}, u32[]{:S(2)}, u32[]{:S(2)}) collective-permute-start(f32[264,128]{1,0:T(8,128)S(1)} %shard_map.106.w0), channel_id=1, source_target_pairs={{0,12},{1,193},{2,14},{3,195},{4,8},{5,197},{6,10},{7,199},{8,4},{... | collective-permute-start | bytes 405512 | tf_op jit(solution)/shard_map/ppermute | solution.py:32
  61.6 6.5 %collective-permute-start.24 = (f32[264,128]{1,0:T(8,128)S(1)}, f32[264,128]{1,0:T(8,128)S(1)}, u32[]{:S(2)}, u32[]{:S(2)}) collective-permute-start(f32[264,128]{1,0:T(8,128)S(1)} %shard_map.106.w0), channel_id=1, source_target_pairs={{0,8},{1,129},{2,10},{3,131},{4,12},{5,133},{6,14},{7,135},{8,0},{... | collective-permute-start | bytes 405512 | tf_op jit(solution)/shard_map/ppermute | solution.py:32
  62.0 6.1 %collective-permute-start.23 = (f32[264,128]{1,0:T(8,128)S(1)}, f32[264,128]{1,0:T(8,128)S(1)}, u32[]{:S(2)}, u32[]{:S(2)}) collective-permute-start(f32[264,128]{1,0:T(8,128)S(1)} %shard_map.106.w0), channel_id=1, source_target_pairs={{0,4},{1,65},{2,6},{3,67},{4,0},{5,69},{6,2},{7,71},{8,12},{9,73},... | collective-permute-start | bytes 405512 | tf_op jit(solution)/shard_map/ppermute | solution.py:32
  77.4 7.9 %collective-permute-start.32 = (f32[16,128]{1,0:T(8,128)S(1)}, f32[16,128]{1,0:T(8,128)S(1)}, u32[]{:S(2)}, u32[]{:S(2)}) collective-permute-start(f32[16,128]{1,0:T(8,128)S(1)} %shard_map.110.after_ref.mine_ref), channel_id=1, source_target_pairs={{0,2},{1,3},{2,0},{3,1},{4,6},{5,7},{6,4},{7,5},{8,10},{9,11},{10,... | collective-permute-start | bytes 24584 | tf_op jit(solution)/shard_map/ppermute | solution.py:21
  80.5 8.6 %collective-permute-start.29 = (f32[128,128]{1,0:T(8,128)S(1)}, f32[128,128]{1,0:T(8,128)S(1)}, u32[]{:S(2)}, u32[]{:S(2)}) collective-permute-start(f32[128,128]{1,0:T(8,128)S(1)} %get-tuple-element.89), channel_id=1, source_target_pairs={{0,4},{1,5},{2,6},{3,7},{4,0},{5,1},{6,2},{7,3},{8,12},{9,13},{10,... | collective-permute-start | bytes 196616 | tf_op jit(solution)/shard_map/ppermute | solution.py:21
  81.1 9.0 %collective-permute-start.30 = (f32[128,128]{1,0:T(8,128)S(1)}, f32[128,128]{1,0:T(8,128)S(1)}, u32[]{:S(2)}, u32[]{:S(2)}) collective-permute-start(f32[128,128]{1,0:T(8,128)S(1)} %get-tuple-element.90), channel_id=1, source_target_pairs={{0,8},{1,9},{2,10},{3,11},{4,12},{5,13},{6,14},{7,15},{8,0},{9,1},... | collective-permute-start | bytes 196616 | tf_op jit(solution)/shard_map/ppermute | solution.py:21
  84.0 6.2 %collective-permute-start.31 = (f32[128,128]{1,0:T(8,128)S(1)}, f32[128,128]{1,0:T(8,128)S(1)}, u32[]{:S(2)}, u32[]{:S(2)}) collective-permute-start(f32[128,128]{1,0:T(8,128)S(1)} %get-tuple-element.91), channel_id=1, source_target_pairs={{0,12},{1,13},{2,14},{3,15},{4,8},{5,9},{6,10},{7,11},{8,4},{9,5},... | collective-permute-start | bytes 196616 | tf_op jit(solution)/shard_map/ppermute | solution.py:21
  85.4 7.8 %collective-permute-start.34 = (f32[80,128]{1,0:T(8,128)S(1)}, f32[80,128]{1,0:T(8,128)S(1)}, u32[]{:S(2)}, u32[]{:S(2)}) collective-permute-start(f32[80,128]{1,0:T(8,128)S(1)} %get-tuple-element.97), channel_id=1, source_target_pairs={{0,64},{16,80},{32,96},{48,112},{64,0},{80,16},{96,32},{112,48},{1... | collective-permute-start | bytes 122888 | tf_op jit(solution)/shard_map/ppermute | solution.py:21
  85.7 7.5 %collective-permute-start.35 = (f32[80,128]{1,0:T(8,128)S(1)}, f32[80,128]{1,0:T(8,128)S(1)}, u32[]{:S(2)}, u32[]{:S(2)}) collective-permute-start(f32[80,128]{1,0:T(8,128)S(1)} %get-tuple-element.98), channel_id=1, source_target_pairs={{0,128},{16,144},{32,160},{48,176},{64,192},{80,208},{96,224},{112... | collective-permute-start | bytes 122888 | tf_op jit(solution)/shard_map/ppermute | solution.py:21
  89.1 5.2 %collective-permute-start.36 = (f32[80,128]{1,0:T(8,128)S(1)}, f32[80,128]{1,0:T(8,128)S(1)}, u32[]{:S(2)}, u32[]{:S(2)}) collective-permute-start(f32[80,128]{1,0:T(8,128)S(1)} %get-tuple-element.99), channel_id=1, source_target_pairs={{0,192},{16,208},{32,224},{48,240},{64,128},{80,144},{96,160},{112... | collective-permute-start | bytes 122888 | tf_op jit(solution)/shard_map/ppermute | solution.py:21
  90.2 20.0 %collective-permute-start.33 = (f32[64,128]{1,0:T(8,128)S(1)}, f32[64,128]{1,0:T(8,128)S(1)}, u32[]{:S(2)}, u32[]{:S(2)}) collective-permute-start(f32[64,128]{1,0:T(8,128)S(1)} %get-tuple-element.95), channel_id=1, source_target_pairs={{0,2},{1,3},{2,0},{3,1},{4,6},{5,7},{6,4},{7,5},{8,10},{9,11},{10,... | collective-permute-start | bytes 98312 | tf_op jit(solution)/shard_map/ppermute | solution.py:21
  96.1 4.6 %collective-permute-start.38 = (f32[32,128]{1,0:T(8,128)S(1)}, f32[32,128]{1,0:T(8,128)S(1)}, u32[]{:S(2)}, u32[]{:S(2)}) collective-permute-start(f32[32,128]{1,0:T(8,128)S(1)} %get-tuple-element.102), channel_id=1, source_target_pairs={{0,32},{16,48},{32,0},{48,16},{64,96},{80,112},{96,64},{112,80},{1... | collective-permute-start | bytes 49160 | tf_op jit(solution)/shard_map/ppermute | solution.py:21
  97.0 5.5 %collective-permute-start.39 = (f32[32,128]{1,0:T(8,128)S(1)}, f32[32,128]{1,0:T(8,128)S(1)}, u32[]{:S(2)}, u32[]{:S(2)}) collective-permute-start(f32[32,128]{1,0:T(8,128)S(1)} %get-tuple-element.103), channel_id=1, source_target_pairs={{0,48},{16,32},{32,16},{48,0},{64,112},{80,96},{96,80},{112,64},{1... | collective-permute-start | bytes 49160 | tf_op jit(solution)/shard_map/ppermute | solution.py:21
  103.1 4.9 %collective-permute-start.42 = (f32[16,128]{1,0:T(8,128)S(1)}, f32[16,128]{1,0:T(8,128)S(1)}, u32[]{:S(2)}, u32[]{:S(2)}) collective-permute-start(f32[16,128]{1,0:T(8,128)S(1)} %get-tuple-element.105.e0), channel_id=1, source_target_pairs={{0,12},{1,13},{2,14},{3,15},{4,8},{5,9},{6,10},{7,11},{8,4},{9,5},... | collective-permute-start | bytes 24584 | tf_op jit(solution)/shard_map/ppermute | solution.py:21
  105.1 5.2 %collective-permute-start.41 = (f32[16,128]{1,0:T(8,128)S(1)}, f32[16,128]{1,0:T(8,128)S(1)}, u32[]{:S(2)}, u32[]{:S(2)}) collective-permute-start(f32[16,128]{1,0:T(8,128)S(1)} %get-tuple-element.105.e0), channel_id=1, source_target_pairs={{0,8},{1,9},{2,10},{3,11},{4,12},{5,13},{6,14},{7,15},{8,0},{9,1},... | collective-permute-start | bytes 24584 | tf_op jit(solution)/shard_map/ppermute | solution.py:21
  105.8 4.5 %collective-permute-start.40 = (f32[16,128]{1,0:T(8,128)S(1)}, f32[16,128]{1,0:T(8,128)S(1)}, u32[]{:S(2)}, u32[]{:S(2)}) collective-permute-start(f32[16,128]{1,0:T(8,128)S(1)} %get-tuple-element.105.e0), channel_id=1, source_target_pairs={{0,4},{1,5},{2,6},{3,7},{4,0},{5,1},{6,2},{7,3},{8,12},{9,13},{10,... | collective-permute-start | bytes 24584 | tf_op jit(solution)/shard_map/ppermute | solution.py:21
  (13 other events, 36.2 us)

commit v2 on v1

--- a/solution.py
+++ b/solution.py
@@ -258,14 +258,8 @@
         out_ref[8 * share :, :] = jnp.zeros((out_ref.shape[0] - 8 * share, out_ref.shape[1]), F32)
 
 
-def stack_kernel(rows, w0, w1, w2, w3, out_ref):
-    for d, ref in enumerate((w0, w1, w2, w3)):
-        out_ref[d * rows : (d + 1) * rows, :] = ref[:rows, :]
-    if w0.shape[0] > rows:
-        out_ref[4 * rows :, :] = (w0[rows:, :] + w1[rows:, :]) + (w2[rows:, :] + w3[rows:, :])
-
-
-def unstack_kernel(sub, share, mine, other, a_ref, b_ref, near_a, near_b, *weeks_ref):
+def unstack_kernel(sub, share, *refs):
+    mine, other, (a_ref, b_ref, near_a, near_b), weeks_ref = refs[:4], refs[4:8], refs[8:12], refs[12:]
     core = lax.axis_index("store") % 2
     store, item = lax.axis_index("store") - core, lax.axis_index("item")
     rows = 4 * sub
@@ -277,33 +271,30 @@
                 for h in range(2):
                     for o in range(2):
                         to = pl.multiple_of(((store ^ (4 * d + 2 * h)) + o) * sub, sub)
-                        at = d * rows + (2 * h + o) * sub
-                        a_ref[pl.ds(to, sub), :] = items[at : at + sub, :]
+                        at = (2 * h + o) * sub
+                        a_ref[pl.ds(to, sub), :] = items[d][at : at + sub, :]
             for e in range(4):
                 for d in range(4):
                     to = pl.multiple_of((item ^ (4 * e + d)) * share, share)
-                    at = e * rows + (2 * d + which) * share
-                    b_ref[pl.ds(to, share), :] = stores[at : at + share, :]
+                    at = (2 * d + which) * share
+                    b_ref[pl.ds(to, share), :] = stores[e][at : at + share, :]
             for h in range(2):
                 at = (2 * h + which) * sub
-                near_a[h * sub : (h + 1) * sub, :] = items[at : at + sub, :]
+                near_a[h * sub : (h + 1) * sub, :] = items[0][at : at + sub, :]
             for d in range(4):
                 at = (2 * d + which) * share
-                near_b[d * share : (d + 1) * share, :] = stores[at : at + share, :]
+                near_b[d * share : (d + 1) * share, :] = stores[0][at : at + share, :]
             for ref in weeks_ref:
-                ref[...] = items[4 * rows :, :]
-
-
-def far_gather(sub, share, value, weeks, flops=None):
+                ref[...] = tree([item[rows:, :] for item in items])
+
+
+def far_gather(sub, share, value, weeks):
     rank = value.shape[1]
     rows = [value] + [chip_swap(value, d, d) for d in OUTER]
-    (stack,) = small_call(
-        functools.partial(stack_kernel, 4 * sub), [(16 * sub + weeks, rank)], *rows, flops=flops
-    )
     outs = [(16 * sub, rank), (16 * share, rank), (2 * sub, rank), (4 * share, rank)]
     outs = outs + ([(weeks, rank)] if weeks else [])
-    other = swap(stack, "store", CORE)
-    return small_call(functools.partial(unstack_kernel, sub, share), outs, stack, other)
+    others = [swap(row, "store", CORE) for row in rows]
+    return small_call(functools.partial(unstack_kernel, sub, share), outs, *rows, *others)
 
 
 def pack_kernel(used, gbt_ref, mine_ref, core_ref, *refs):
@@ -376,14 +367,16 @@
     send_ref[...] = grad[half:, :]
 
 
-def last_kernel(rate_b, d0, z1, z2, z3, b_ref, newb_ref, weeks_ref):
-    share = newb_ref.shape[0]
+def last_kernel(d0, z1, z2, z3, grad_ref, weeks_ref):
+    share = grad_ref.shape[0]
     total = (d0[...] + z1[...]) + (z2[...] + z3[...])
-    newb_ref[...] = b_ref[:share, :] - rate_b * total[:share, :]
+    grad_ref[...] = total[:share, :]
     weeks_ref[...] = total[share:, :]
 
 
-def end_kernel(rate_a, rate_c, count, keep, got, old_ref, e0, e1, e2, e3, c_ref, newa_ref, newc_ref, loss_ref):
+def end_kernel(rate_a, rate_b, rate_c, count, *refs):
+    keep, got, old_ref, e0, e1, e2, e3, c_ref, gradb_ref, b_ref, newa_ref, newb_ref, newc_ref, loss_ref = refs
+    newb_ref[...] = b_ref[: newb_ref.shape[0], :] - rate_b * gradb_ref[...]
     newa_ref[...] = old_ref[: keep.shape[0], :] - rate_a * (keep[...] + got[...])
     total = (e0[...] + e1[...]) + (e2[...] + e3[...])
     weeks = c_ref.shape[0]
@@ -430,8 +423,8 @@
     ])
     z1, z2 = small_call(near_kernel, [pair, (2 * share, rank)], own, other_a, own_b, other_b)
     near = [chip_swap(z1, ZHI, 1), chip_swap(z2, 0, 2), chip_swap(z2, 0, 3)]
-    (value,) = small_call(join_kernel, [(4 * sub, rank)], z1, z2, *near)
-    block_a, block_b, mine_a, mine_b = far_gather(sub, share, value, 0, flops=LONG)
+    (value,) = small_call(join_kernel, [(4 * sub, rank)], z1, z2, *near, flops=LONG)
+    block_a, block_b, mine_a, mine_b = far_gather(sub, share, value, 0)
     old = jnp.zeros((weeks + 8, rank), F32)
     errors, gbt, old, factor_c = step_call(rate_c, False, sales, late, block_a, block_b, week_factors, old)
 
@@ -468,17 +461,15 @@
     got_a = swap(send, "store", ZHI)
     near = small_call(functools.partial(deal_kernel, share), [(share + weeks + 8, rank)] * 4, *dealt)
     near = [near[0]] + over(near[1:], "item", ZLOS)
-    shard_b, part_c = small_call(
-        functools.partial(last_kernel, rate_b), [(share, rank), (weeks + 8, rank)], *near, mine_b
-    )
-    shard_a, factor_c, losses = pl.pallas_call(
-        functools.partial(end_kernel, rate_a, rate_c, 2.0 * count),
-        out_shape=[jax.ShapeDtypeStruct(s, F32) for s in ((sub, rank), (weeks, rank), (2,))],
-        in_specs=[VM] * 8,
-        out_specs=[VM, VM, pl.BlockSpec(memory_space=pltpu.SMEM)],
+    grad_b, part_c = small_call(last_kernel, [(share, rank), (weeks + 8, rank)], *near)
+    shard_a, shard_b, factor_c, losses = pl.pallas_call(
+        functools.partial(end_kernel, rate_a, rate_b, rate_c, 2.0 * count),
+        out_shape=[jax.ShapeDtypeStruct(s, F32) for s in ((sub, rank), (share, rank), (weeks, rank), (2,))],
+        in_specs=[VM] * 10,
+        out_specs=[VM, VM, VM, pl.BlockSpec(memory_space=pltpu.SMEM)],
         compiler_params=pltpu.CompilerParams(vmem_limit_bytes=8 * MIB),
         cost_estimate=pl.CostEstimate(flops=0, bytes_accessed=0, transcendentals=0),
-    )(keep, got_a, mine_a, part_c, *over([part_c] * 3, "store", OUTER), factor_c)
+    )(keep, got_a, mine_a, part_c, *over([part_c] * 3, "store", OUTER), factor_c, grad_b, mine_b)
     return shard_a, shard_b, factor_c, losses
 
 

time: 111 us -> 108 us (0.973)
  waiting for transfers between devices: 28.8 us -> 21.9 us
  starting transfers between devices: 66.2 us -> 71.6 us
  local copies, waits for them, and re-layouts: 1.27 us -> 0.01 us
    ppermute x34 -> x40, starting transfers between devices: 49.2 us -> 54.3 us  [swap(): return lax.ppermute(value, axis, [(i, i ^ bits) for i in range(16)])]
    ppermute x9, waiting for transfers between devices: 11.2 us -> 7.48 us  [chip_swap(): return lax.ppermute(value, ('item', 'store'), pairs)]
    ppermute x34 -> x40, waiting for transfers between devices: 17.5 us -> 14.4 us  [swap(): return lax.ppermute(value, axis, [(i, i ^ bits) for i in range(16)])]
    unnamed x4 -> x6, local copies, waits for them, and re-layouts: 1.27 us -> 0.01 us
  transfers between devices with their start and end apart: 43 -> 49, of which waited for: 17 -> 20; matrix products, arithmetic and copies ran while one was open for 0% -> 0% of each run, Pallas kernels for 2% -> 1%
where the time goes in v2:
time: 108 us
  starting transfers between devices  71.6 us (66%)
  waiting for transfers between devices  21.9 us (20%)
  Pallas kernels  13.3 us (12%)
  between operations  1.09 us (1%)
    ppermute x40, starting transfers between devices, swap(): return lax.ppermute(value, axis, [(i, i ^ bits) for i in range(16)])  54.3 us
    ppermute x9, starting transfers between devices, chip_swap(): return lax.ppermute(value, ('item', 'store'), pairs)  17.2 us
    ppermute x40, waiting for transfers between devices, swap(): return lax.ppermute(value, axis, [(i, i ^ bits) for i in range(16)])  14.4 us
    pallas_call x2, Pallas kernels, step_call(): pl.pallas_call(functools.partial(step_kernel, rate_c, riding), out_shape=...  8.29 us
    ppermute x9, waiting for transfers between devices, chip_swap(): return lax.ppermute(value, ('item', 'store'), pairs)  7.48 us
    pallas_call x2, Pallas kernels, items_grad_call(): pl.pallas_call(items_grad_kernel, out_shape=[jax.ShapeDtypeStruct((n_item...  2.61 us
  transfers between devices with their start and end apart: 49, of which 20 were waited for; matrix products, arithmetic and copies ran while one was open for 0% of the time, Pallas kernels for 1%

profile of v2, /device:TPU:6, one launch (start us, length us, event | category | flops | bytes accessed | tf_op | source)
XLA Modules:
  0.0 107.9 jit_solution(11714060978084843378)
XLA Ops:
  2.3 7.3 %collective-permute-start.2 = (f32[128,128]{1,0:T(8,128)S(1)}, f32[128,128]{1,0:T(8,128)S(1)}, u32[]{:S(2)}, u32[]{:S(2)}) collective-permute-start(f32[128,128]{1,0:T(8,128)S(1)} %get-tuple-element.57.z1), channel_id=1, source_target_pairs={{0,2},{1,17},{2,0},{3,19},{4,6},{5,21},{6,4},{7,23},{8,10},{9,25},... | collective-permute-start | bytes 196616 | tf_op jit(solution)/shard_map/ppermute | solution.py:32
  12.2 3.1 %collective-permute-start.7 = (f32[256,128]{1,0:T(8,128)S(1)}, f32[256,128]{1,0:T(8,128)S(1)}, u32[]{:S(2)}, u32[]{:S(2)}) collective-permute-start(f32[256,128]{1,0:T(8,128)S(1)} %shard_map.95.refs_0_), channel_id=1, source_target_pairs={{0,12},{1,193},{2,14},{3,195},{4,8},{5,197},{6,10},{7,199},{8,4},{... | collective-permute-start | bytes 393224 | tf_op jit(solution)/shard_map/ppermute | solution.py:32
  16.4 1.6 %collective-permute-start.8 = (f32[256,128]{1,0:T(8,128)S(1)}, f32[256,128]{1,0:T(8,128)S(1)}, u32[]{:S(2)}, u32[]{:S(2)}) collective-permute-start(f32[256,128]{1,0:T(8,128)S(1)} %shard_map.95.refs_0_), channel_id=1, source_target_pairs={{0,1},{1,0},{2,3},{3,2},{4,5},{5,4},{6,7},{7,6},{8,9},{9,8},{10,11... | collective-permute-start | bytes 393224 | tf_op jit(solution)/shard_map/ppermute | solution.py:21
  19.3 2.2 %collective-permute-start.11 = (f32[256,128]{1,0:T(8,128)S(1)}, f32[256,128]{1,0:T(8,128)S(1)}, u32[]{:S(2)}, u32[]{:S(2)}) collective-permute-start(f32[256,128]{1,0:T(8,128)S(1)} %collective-permute-done.7.refs_3_), channel_id=1, source_target_pairs={{0,1},{1,0},{2,3},{3,2},{4,5},{5,4},{6,7},{7,6},{8,9},{9,8},{10,11... | collective-permute-start | bytes 393224 | tf_op jit(solution)/shard_map/ppermute | solution.py:21
  23.5 4.2 %shard_map.97 = (bf16[8,1024,256]{2,1,0:T(8,128)(2,1)S(1)}, f32[128,256]{1,0:T(8,128)S(1)}, f32[16,128]{1,0:T(8,128)S(1)}, f32[8,128]{1,0:T(8,128)S(1)}) custom-call(f32[8,1024,256]{2,1,0:T(8,128)S(1)} %bitcast.3, s32[1024,256]{1,0:T(8,128)S(1)} %get-tuple-element.54.refs_1_, f32[1024,128]{1,0:T(8,128)S(1)} %get-tuple-element.59.refs_2_, ...), custom_call_target="tpu_custom_call" | custom-call | flops 1073741824 | bytes 8388608 | tf_op jit(solution)/shard_map/pallas_call | solution.py:136
  30.6 6.1 %collective-permute-start.13 = (f32[16,128]{1,0:T(8,128)S(1)}, f32[16,128]{1,0:T(8,128)S(1)}, u32[]{:S(2)}, u32[]{:S(2)}) collective-permute-start(f32[16,128]{1,0:T(8,128)S(1)} %shard_map.98.mine_ref.after_ref), channel_id=1, source_target_pairs={{0,2},{1,3},{2,0},{3,1},{4,6},{5,7},{6,4},{7,5},{8,10},{9,11},{10,... | collective-permute-start | bytes 24584 | tf_op jit(solution)/shard_map/ppermute | solution.py:21
  37.1 2.9 %collective-permute-start.22 = (f32[128,128]{1,0:T(8,128)S(1)}, f32[128,128]{1,0:T(8,128)S(1)}, u32[]{:S(2)}, u32[]{:S(2)}) collective-permute-start(f32[128,128]{1,0:T(8,128)S(1)} %get-tuple-element.74), channel_id=1, source_target_pairs={{0,8},{1,9},{2,10},{3,11},{4,12},{5,13},{6,14},{7,15},{8,0},{9,1},... | collective-permute-start | bytes 196616 | tf_op jit(solution)/shard_map/ppermute | solution.py:21
  40.0 1.5 %collective-permute-start.23 = (f32[128,128]{1,0:T(8,128)S(1)}, f32[128,128]{1,0:T(8,128)S(1)}, u32[]{:S(2)}, u32[]{:S(2)}) collective-permute-start(f32[128,128]{1,0:T(8,128)S(1)} %get-tuple-element.75), channel_id=1, source_target_pairs={{0,12},{1,13},{2,14},{3,15},{4,8},{5,9},{6,10},{7,11},{8,4},{9,5},... | collective-permute-start | bytes 196616 | tf_op jit(solution)/shard_map/ppermute | solution.py:21
  43.7 2.8 %collective-permute-start.16 = (f32[136,128]{1,0:T(8,128)S(1)}, f32[136,128]{1,0:T(8,128)S(1)}, u32[]{:S(2)}, u32[]{:S(2)}) collective-permute-start(f32[136,128]{1,0:T(8,128)S(1)} %get-tuple-element.66), channel_id=1, source_target_pairs={{0,192},{16,208},{32,224},{48,240},{64,128},{80,144},{96,160},{112... | collective-permute-start | bytes 208904 | tf_op jit(solution)/shard_map/ppermute | solution.py:21
  46.5 2.8 %collective-permute-start.24 = (f32[128,128]{1,0:T(8,128)S(1)}, f32[128,128]{1,0:T(8,128)S(1)}, u32[]{:S(2)}, u32[]{:S(2)}) collective-permute-start(f32[128,128]{1,0:T(8,128)S(1)} %shard_map.103.mine), channel_id=1, source_target_pairs={{0,2},{1,3},{2,0},{3,1},{4,6},{5,7},{6,4},{7,5},{8,10},{9,11},{10,... | collective-permute-start | bytes 196616 | tf_op jit(solution)/shard_map/ppermute | solution.py:21
  49.3 1.5 %collective-permute-start.19 = (f32[72,128]{1,0:T(8,128)S(1)}, f32[72,128]{1,0:T(8,128)S(1)}, u32[]{:S(2)}, u32[]{:S(2)}) collective-permute-start(f32[72,128]{1,0:T(8,128)S(1)} %shard_map.100.x0), channel_id=1, source_target_pairs={{0,48},{16,32},{32,16},{48,0},{64,112},{80,96},{96,80},{112,64},{1... | collective-permute-start | bytes 110600 | tf_op jit(solution)/shard_map/ppermute | solution.py:21
  51.3 2.4 %collective-permute-start.17 = (f32[72,128]{1,0:T(8,128)S(1)}, f32[72,128]{1,0:T(8,128)S(1)}, u32[]{:S(2)}, u32[]{:S(2)}) collective-permute-start(f32[72,128]{1,0:T(8,128)S(1)} %shard_map.100.x0), channel_id=1, source_target_pairs={{0,16},{16,0},{32,48},{48,32},{64,80},{80,64},{96,112},{112,96},{1... | collective-permute-start | bytes 110600 | tf_op jit(solution)/shard_map/ppermute | solution.py:21
  53.8 1.4 %collective-permute-done.19.z3 = f32[72,128]{1,0:T(8,128)S(1)} collective-permute-done((f32[72,128]{1,0:T(8,128)S(1)}, f32[72,128]{1,0:T(8,128)S(1)}, u32[]{:S(2)}, u32[]{:S(2)}) %collective-permute-start.19) | collective-permute-done | bytes 36896 | tf_op jit(solution)/shard_map/ppermute | solution.py:21
  57.6 2.6 %collective-permute-start.28 = (f32[264,128]{1,0:T(8,128)S(1)}, f32[264,128]{1,0:T(8,128)S(1)}, u32[]{:S(2)}, u32[]{:S(2)}) collective-permute-start(f32[264,128]{1,0:T(8,128)S(1)} %shard_map.105.refs_0_), channel_id=1, source_target_pairs={{0,12},{1,193},{2,14},{3,195},{4,8},{5,197},{6,10},{7,199},{8,4},{... | collective-permute-start | bytes 405512 | tf_op jit(solution)/shard_map/ppermute | solution.py:32
  60.2 1.6 %collective-permute-start.26 = (f32[264,128]{1,0:T(8,128)S(1)}, f32[264,128]{1,0:T(8,128)S(1)}, u32[]{:S(2)}, u32[]{:S(2)}) collective-permute-start(f32[264,128]{1,0:T(8,128)S(1)} %shard_map.105.refs_0_), channel_id=1, source_target_pairs={{0,4},{1,65},{2,6},{3,67},{4,0},{5,69},{6,2},{7,71},{8,12},{9,73},... | collective-permute-start | bytes 405512 | tf_op jit(solution)/shard_map/ppermute | solution.py:32
  61.8 2.4 %collective-permute-done.28.refs_3_ = f32[264,128]{1,0:T(8,128)S(1)} collective-permute-done((f32[264,128]{1,0:T(8,128)S(1)}, f32[264,128]{1,0:T(8,128)S(1)}, u32[]{:S(2)}, u32[]{:S(2)}) %collective-permute-start.28) | collective-permute-done | bytes 135200 | tf_op jit(solution)/shard_map/ppermute | solution.py:32
  64.2 2.5 %collective-permute-done.27.refs_2_ = f32[264,128]{1,0:T(8,128)S(1)} collective-permute-done((f32[264,128]{1,0:T(8,128)S(1)}, f32[264,128]{1,0:T(8,128)S(1)}, u32[]{:S(2)}, u32[]{:S(2)}) %collective-permute-start.27) | collective-permute-done | bytes 135200 | tf_op jit(solution)/shard_map/ppermute | solution.py:32
  68.6 4.1 %shard_map.107 = (bf16[8,1024,256]{2,1,0:T(8,128)(2,1)S(1)}, f32[128,256]{1,0:T(8,128)S(1)}, f32[16,128]{1,0:T(8,128)S(1)}, f32[8,128]{1,0:T(8,128)S(1)}) custom-call(f32[8,1024,256]{2,1,0:T(8,128)S(1)} %bitcast.3, s32[1024,256]{1,0:T(8,128)S(1)} %get-tuple-element.54.refs_1_, f32[1024,128]{1,0:T(8,128)S(1)} %get-tuple-element.77.refs_2_, ...), custom_call_target="tpu_custom_call" | custom-call | flops 1073741824 | bytes 8388608 | tf_op jit(solution)/shard_map/pallas_call | solution.py:136
  74.0 1.3 %shard_map.109 = (f32[512,128]{1,0:T(8,128)S(1)}, f32[512,128]{1,0:T(8,128)S(1)}) custom-call(bf16[8,1024,256]{2,1,0:T(8,128)(2,1)S(1)} %get-tuple-element.80.er, f32[256,128]{1,0:T(8,128)S(1)} %get-tuple-element.78.refs_3_.b_ref, f32[8,128]{1,0:T(8,128)S(1)} %get-tuple-element.81.c_ref.refs_7_, f32[16,128]{1,0:T(8,128)S(1)} %shard_map.108.after_ref.mine_ref), custom_call_target="tpu_custom_call" | custom-call | tf_op jit(solution)/shard_map/pallas_call | solution.py:175
  75.7 2.7 %collective-permute-start.38 = (f32[16,128]{1,0:T(8,128)S(1)}, f32[16,128]{1,0:T(8,128)S(1)}, u32[]{:S(2)}, u32[]{:S(2)}) collective-permute-start(f32[16,128]{1,0:T(8,128)S(1)} %shard_map.108.after_ref.mine_ref), channel_id=1, source_target_pairs={{0,2},{1,3},{2,0},{3,1},{4,6},{5,7},{6,4},{7,5},{8,10},{9,11},{10,... | collective-permute-start | bytes 24584 | tf_op jit(solution)/shard_map/ppermute | solution.py:21
  78.8 2.9 %collective-permute-start.36 = (f32[128,128]{1,0:T(8,128)S(1)}, f32[128,128]{1,0:T(8,128)S(1)}, u32[]{:S(2)}, u32[]{:S(2)}) collective-permute-start(f32[128,128]{1,0:T(8,128)S(1)} %get-tuple-element.87), channel_id=1, source_target_pairs={{0,8},{1,9},{2,10},{3,11},{4,12},{5,13},{6,14},{7,15},{8,0},{9,1},... | collective-permute-start | bytes 196616 | tf_op jit(solution)/shard_map/ppermute | solution.py:21
  81.7 1.6 %collective-permute-start.37 = (f32[128,128]{1,0:T(8,128)S(1)}, f32[128,128]{1,0:T(8,128)S(1)}, u32[]{:S(2)}, u32[]{:S(2)}) collective-permute-start(f32[128,128]{1,0:T(8,128)S(1)} %get-tuple-element.88), channel_id=1, source_target_pairs={{0,12},{1,13},{2,14},{3,15},{4,8},{5,9},{6,10},{7,11},{8,4},{9,5},... | collective-permute-start | bytes 196616 | tf_op jit(solution)/shard_map/ppermute | solution.py:21
  83.5 3.3 %collective-permute-start.41 = (f32[80,128]{1,0:T(8,128)S(1)}, f32[80,128]{1,0:T(8,128)S(1)}, u32[]{:S(2)}, u32[]{:S(2)}) collective-permute-start(f32[80,128]{1,0:T(8,128)S(1)} %get-tuple-element.95), channel_id=1, source_target_pairs={{0,128},{16,144},{32,160},{48,176},{64,192},{80,208},{96,224},{112... | collective-permute-start | bytes 122888 | tf_op jit(solution)/shard_map/ppermute | solution.py:21
  86.7 1.4 %collective-permute-start.42 = (f32[80,128]{1,0:T(8,128)S(1)}, f32[80,128]{1,0:T(8,128)S(1)}, u32[]{:S(2)}, u32[]{:S(2)}) collective-permute-start(f32[80,128]{1,0:T(8,128)S(1)} %get-tuple-element.96), channel_id=1, source_target_pairs={{0,192},{16,208},{32,224},{48,240},{64,128},{80,144},{96,160},{112... | collective-permute-start | bytes 122888 | tf_op jit(solution)/shard_map/ppermute | solution.py:21
  88.2 3.3 %collective-permute-start.39 = (f32[64,128]{1,0:T(8,128)S(1)}, f32[64,128]{1,0:T(8,128)S(1)}, u32[]{:S(2)}, u32[]{:S(2)}) collective-permute-start(f32[64,128]{1,0:T(8,128)S(1)} %get-tuple-element.92), channel_id=1, source_target_pairs={{0,2},{1,3},{2,0},{3,1},{4,6},{5,7},{6,4},{7,5},{8,10},{9,11},{10,... | collective-permute-start | bytes 98312 | tf_op jit(solution)/shard_map/ppermute | solution.py:21
  92.0 1.7 %collective-permute-start.43 = (f32[32,128]{1,0:T(8,128)S(1)}, f32[32,128]{1,0:T(8,128)S(1)}, u32[]{:S(2)}, u32[]{:S(2)}) collective-permute-start(f32[32,128]{1,0:T(8,128)S(1)} %get-tuple-element.98), channel_id=1, source_target_pairs={{0,16},{16,0},{32,48},{48,32},{64,80},{80,64},{96,112},{112,96},{1... | collective-permute-start | bytes 49160 | tf_op jit(solution)/shard_map/ppermute | solution.py:21
  94.6 1.9 %collective-permute-start.45 = (f32[32,128]{1,0:T(8,128)S(1)}, f32[32,128]{1,0:T(8,128)S(1)}, u32[]{:S(2)}, u32[]{:S(2)}) collective-permute-start(f32[32,128]{1,0:T(8,128)S(1)} %get-tuple-element.100), channel_id=1, source_target_pairs={{0,48},{16,32},{32,16},{48,0},{64,112},{80,96},{96,80},{112,64},{1... | collective-permute-start | bytes 49160 | tf_op jit(solution)/shard_map/ppermute | solution.py:21
  96.4 1.9 %collective-permute-done.44.z2 = f32[32,128]{1,0:T(8,128)S(1)} collective-permute-done((f32[32,128]{1,0:T(8,128)S(1)}, f32[32,128]{1,0:T(8,128)S(1)}, u32[]{:S(2)}, u32[]{:S(2)}) %collective-permute-start.44) | collective-permute-done | bytes 16416 | tf_op jit(solution)/shard_map/ppermute | solution.py:21
  98.3 1.8 %collective-permute-done.45.z3 = f32[32,128]{1,0:T(8,128)S(1)} collective-permute-done((f32[32,128]{1,0:T(8,128)S(1)}, f32[32,128]{1,0:T(8,128)S(1)}, u32[]{:S(2)}, u32[]{:S(2)}) %collective-permute-start.45) | collective-permute-done | bytes 16416 | tf_op jit(solution)/shard_map/ppermute | solution.py:21
  100.1 1.8 %collective-permute-start.48 = (f32[16,128]{1,0:T(8,128)S(1)}, f32[16,128]{1,0:T(8,128)S(1)}, u32[]{:S(2)}, u32[]{:S(2)}) collective-permute-start(f32[16,128]{1,0:T(8,128)S(1)} %get-tuple-element.101.refs_3_), channel_id=1, source_target_pairs={{0,12},{1,13},{2,14},{3,15},{4,8},{5,9},{6,10},{7,11},{8,4},{9,5},... | collective-permute-start | bytes 24584 | tf_op jit(solution)/shard_map/ppermute | solution.py:21
  102.8 1.5 %collective-permute-start.46 = (f32[16,128]{1,0:T(8,128)S(1)}, f32[16,128]{1,0:T(8,128)S(1)}, u32[]{:S(2)}, u32[]{:S(2)}) collective-permute-start(f32[16,128]{1,0:T(8,128)S(1)} %get-tuple-element.101.refs_3_), channel_id=1, source_target_pairs={{0,4},{1,5},{2,6},{3,7},{4,0},{5,1},{6,2},{7,3},{8,12},{9,13},{10,... | collective-permute-start | bytes 24584 | tf_op jit(solution)/shard_map/ppermute | solution.py:21
  105.1 2.0 %collective-permute-done.47.refs_5_ = f32[16,128]{1,0:T(8,128)S(1)} collective-permute-done((f32[16,128]{1,0:T(8,128)S(1)}, f32[16,128]{1,0:T(8,128)S(1)}, u32[]{:S(2)}, u32[]{:S(2)}) %collective-permute-start.47) | collective-permute-done | bytes 8224 | tf_op jit(solution)/shard_map/ppermute | solution.py:21
  (97 shorter events, 24.8 us)
Async XLA Ops:
  2.3 9.9 %collective-permute-start.2 = (f32[128,128]{1,0:T(8,128)S(1)}, f32[128,128]{1,0:T(8,128)S(1)}, u32[]{:S(2)}, u32[]{:S(2)}) collective-permute-start(f32[128,128]{1,0:T(8,128)S(1)} %get-tuple-element.57.z1), channel_id=1, source_target_pairs={{0,2},{1,17},{2,0},{3,19},{4,6},{5,21},{6,4},{7,23},{8,10},{9,25},... | collective-permute-start | bytes 196616 | tf_op jit(solution)/shard_map/ppermute | solution.py:32
  12.2 7.0 %collective-permute-start.7 = (f32[256,128]{1,0:T(8,128)S(1)}, f32[256,128]{1,0:T(8,128)S(1)}, u32[]{:S(2)}, u32[]{:S(2)}) collective-permute-start(f32[256,128]{1,0:T(8,128)S(1)} %shard_map.95.refs_0_), channel_id=1, source_target_pairs={{0,12},{1,193},{2,14},{3,195},{4,8},{5,197},{6,10},{7,199},{8,4},{... | collective-permute-start | bytes 393224 | tf_op jit(solution)/shard_map/ppermute | solution.py:32
  15.3 6.5 %collective-permute-start.6 = (f32[256,128]{1,0:T(8,128)S(1)}, f32[256,128]{1,0:T(8,128)S(1)}, u32[]{:S(2)}, u32[]{:S(2)}) collective-permute-start(f32[256,128]{1,0:T(8,128)S(1)} %shard_map.95.refs_0_), channel_id=1, source_target_pairs={{0,8},{1,129},{2,10},{3,131},{4,12},{5,133},{6,14},{7,135},{8,0},{... | collective-permute-start | bytes 393224 | tf_op jit(solution)/shard_map/ppermute | solution.py:32
  16.0 5.8 %collective-permute-start.5 = (f32[256,128]{1,0:T(8,128)S(1)}, f32[256,128]{1,0:T(8,128)S(1)}, u32[]{:S(2)}, u32[]{:S(2)}) collective-permute-start(f32[256,128]{1,0:T(8,128)S(1)} %shard_map.95.refs_0_), channel_id=1, source_target_pairs={{0,4},{1,65},{2,6},{3,67},{4,0},{5,69},{6,2},{7,71},{8,12},{9,73},... | collective-permute-start | bytes 393224 | tf_op jit(solution)/shard_map/ppermute | solution.py:32
  16.4 5.9 %collective-permute-start.8 = (f32[256,128]{1,0:T(8,128)S(1)}, f32[256,128]{1,0:T(8,128)S(1)}, u32[]{:S(2)}, u32[]{:S(2)}) collective-permute-start(f32[256,128]{1,0:T(8,128)S(1)} %shard_map.95.refs_0_), channel_id=1, source_target_pairs={{0,1},{1,0},{2,3},{3,2},{4,5},{5,4},{6,7},{7,6},{8,9},{9,8},{10,11... | collective-permute-start | bytes 393224 | tf_op jit(solution)/shard_map/ppermute | solution.py:21
  30.2 6.5 %collective-permute-start.20 = (f32[512,128]{1,0:T(8,128)S(1)}, f32[512,128]{1,0:T(8,128)S(1)}, u32[]{:S(2)}, u32[]{:S(2)}) collective-permute-start(f32[512,128]{1,0:T(8,128)S(1)} %get-tuple-element.71), channel_id=1, source_target_pairs={{0,1},{1,0},{2,3},{3,2},{4,5},{5,4},{6,7},{7,6},{8,9},{9,8},{10,11... | collective-permute-start | bytes 786440 | tf_op jit(solution)/shard_map/ppermute | solution.py:21
  30.6 10.9 %collective-permute-start.13 = (f32[16,128]{1,0:T(8,128)S(1)}, f32[16,128]{1,0:T(8,128)S(1)}, u32[]{:S(2)}, u32[]{:S(2)}) collective-permute-start(f32[16,128]{1,0:T(8,128)S(1)} %shard_map.98.mine_ref.after_ref), channel_id=1, source_target_pairs={{0,2},{1,3},{2,0},{3,1},{4,6},{5,7},{6,4},{7,5},{8,10},{9,11},{10,... | collective-permute-start | bytes 24584 | tf_op jit(solution)/shard_map/ppermute | solution.py:21
  36.7 6.9 %collective-permute-start.21 = (f32[128,128]{1,0:T(8,128)S(1)}, f32[128,128]{1,0:T(8,128)S(1)}, u32[]{:S(2)}, u32[]{:S(2)}) collective-permute-start(f32[128,128]{1,0:T(8,128)S(1)} %get-tuple-element.73), channel_id=1, source_target_pairs={{0,4},{1,5},{2,6},{3,7},{4,0},{5,1},{6,2},{7,3},{8,12},{9,13},{10,... | collective-permute-start | bytes 196616 | tf_op jit(solution)/shard_map/ppermute | solution.py:21
  37.1 9.3 %collective-permute-start.22 = (f32[128,128]{1,0:T(8,128)S(1)}, f32[128,128]{1,0:T(8,128)S(1)}, u32[]{:S(2)}, u32[]{:S(2)}) collective-permute-start(f32[128,128]{1,0:T(8,128)S(1)} %get-tuple-element.74), channel_id=1, source_target_pairs={{0,8},{1,9},{2,10},{3,11},{4,12},{5,13},{6,14},{7,15},{8,0},{9,1},... | collective-permute-start | bytes 196616 | tf_op jit(solution)/shard_map/ppermute | solution.py:21
  40.0 6.4 %collective-permute-start.23 = (f32[128,128]{1,0:T(8,128)S(1)}, f32[128,128]{1,0:T(8,128)S(1)}, u32[]{:S(2)}, u32[]{:S(2)}) collective-permute-start(f32[128,128]{1,0:T(8,128)S(1)} %get-tuple-element.75), channel_id=1, source_target_pairs={{0,12},{1,13},{2,14},{3,15},{4,8},{5,9},{6,10},{7,11},{8,4},{9,5},... | collective-permute-start | bytes 196616 | tf_op jit(solution)/shard_map/ppermute | solution.py:21
  41.6 7.6 %collective-permute-start.14 = (f32[136,128]{1,0:T(8,128)S(1)}, f32[136,128]{1,0:T(8,128)S(1)}, u32[]{:S(2)}, u32[]{:S(2)}) collective-permute-start(f32[136,128]{1,0:T(8,128)S(1)} %get-tuple-element.64), channel_id=1, source_target_pairs={{0,64},{16,80},{32,96},{48,112},{64,0},{80,16},{96,32},{112,48},{1... | collective-permute-start | bytes 208904 | tf_op jit(solution)/shard_map/ppermute | solution.py:21
  42.5 6.7 %collective-permute-start.15 = (f32[136,128]{1,0:T(8,128)S(1)}, f32[136,128]{1,0:T(8,128)S(1)}, u32[]{:S(2)}, u32[]{:S(2)}) collective-permute-start(f32[136,128]{1,0:T(8,128)S(1)} %get-tuple-element.65), channel_id=1, source_target_pairs={{0,128},{16,144},{32,160},{48,176},{64,192},{80,208},{96,224},{112... | collective-permute-start | bytes 208904 | tf_op jit(solution)/shard_map/ppermute | solution.py:21
  43.7 5.6 %collective-permute-start.16 = (f32[136,128]{1,0:T(8,128)S(1)}, f32[136,128]{1,0:T(8,128)S(1)}, u32[]{:S(2)}, u32[]{:S(2)}) collective-permute-start(f32[136,128]{1,0:T(8,128)S(1)} %get-tuple-element.66), channel_id=1, source_target_pairs={{0,192},{16,208},{32,224},{48,240},{64,128},{80,144},{96,160},{112... | collective-permute-start | bytes 208904 | tf_op jit(solution)/shard_map/ppermute | solution.py:21
  46.5 9.7 %collective-permute-start.24 = (f32[128,128]{1,0:T(8,128)S(1)}, f32[128,128]{1,0:T(8,128)S(1)}, u32[]{:S(2)}, u32[]{:S(2)}) collective-permute-start(f32[128,128]{1,0:T(8,128)S(1)} %shard_map.103.mine), channel_id=1, source_target_pairs={{0,2},{1,3},{2,0},{3,1},{4,6},{5,7},{6,4},{7,5},{8,10},{9,11},{10,... | collective-permute-start | bytes 196616 | tf_op jit(solution)/shard_map/ppermute | solution.py:21
  49.3 5.8 %collective-permute-start.19 = (f32[72,128]{1,0:T(8,128)S(1)}, f32[72,128]{1,0:T(8,128)S(1)}, u32[]{:S(2)}, u32[]{:S(2)}) collective-permute-start(f32[72,128]{1,0:T(8,128)S(1)} %shard_map.100.x0), channel_id=1, source_target_pairs={{0,48},{16,32},{32,16},{48,0},{64,112},{80,96},{96,80},{112,64},{1... | collective-permute-start | bytes 110600 | tf_op jit(solution)/shard_map/ppermute | solution.py:21
  50.8 5.4 %collective-permute-start.18 = (f32[72,128]{1,0:T(8,128)S(1)}, f32[72,128]{1,0:T(8,128)S(1)}, u32[]{:S(2)}, u32[]{:S(2)}) collective-permute-start(f32[72,128]{1,0:T(8,128)S(1)} %shard_map.100.x0), channel_id=1, source_target_pairs={{0,32},{16,48},{32,0},{48,16},{64,96},{80,112},{96,64},{112,80},{1... | collective-permute-start | bytes 110600 | tf_op jit(solution)/shard_map/ppermute | solution.py:21
  51.3 4.8 %collective-permute-start.17 = (f32[72,128]{1,0:T(8,128)S(1)}, f32[72,128]{1,0:T(8,128)S(1)}, u32[]{:S(2)}, u32[]{:S(2)}) collective-permute-start(f32[72,128]{1,0:T(8,128)S(1)} %shard_map.100.x0), channel_id=1, source_target_pairs={{0,16},{16,0},{32,48},{48,32},{64,80},{80,64},{96,112},{112,96},{1... | collective-permute-start | bytes 110600 | tf_op jit(solution)/shard_map/ppermute | solution.py:21
  57.6 6.6 %collective-permute-start.28 = (f32[264,128]{1,0:T(8,128)S(1)}, f32[264,128]{1,0:T(8,128)S(1)}, u32[]{:S(2)}, u32[]{:S(2)}) collective-permute-start(f32[264,128]{1,0:T(8,128)S(1)} %shard_map.105.refs_0_), channel_id=1, source_target_pairs={{0,12},{1,193},{2,14},{3,195},{4,8},{5,197},{6,10},{7,199},{8,4},{... | collective-permute-start | bytes 405512 | tf_op jit(solution)/shard_map/ppermute | solution.py:32
  60.2 6.5 %collective-permute-start.27 = (f32[264,128]{1,0:T(8,128)S(1)}, f32[264,128]{1,0:T(8,128)S(1)}, u32[]{:S(2)}, u32[]{:S(2)}) collective-permute-start(f32[264,128]{1,0:T(8,128)S(1)} %shard_map.105.refs_0_), channel_id=1, source_target_pairs={{0,8},{1,129},{2,10},{3,131},{4,12},{5,133},{6,14},{7,135},{8,0},{... | collective-permute-start | bytes 405512 | tf_op jit(solution)/shard_map/ppermute | solution.py:32
  60.2 6.5 %collective-permute-start.26 = (f32[264,128]{1,0:T(8,128)S(1)}, f32[264,128]{1,0:T(8,128)S(1)}, u32[]{:S(2)}, u32[]{:S(2)}) collective-permute-start(f32[264,128]{1,0:T(8,128)S(1)} %shard_map.105.refs_0_), channel_id=1, source_target_pairs={{0,4},{1,65},{2,6},{3,67},{4,0},{5,69},{6,2},{7,71},{8,12},{9,73},... | collective-permute-start | bytes 405512 | tf_op jit(solution)/shard_map/ppermute | solution.py:32
  61.8 5.5 %collective-permute-start.29 = (f32[264,128]{1,0:T(8,128)S(1)}, f32[264,128]{1,0:T(8,128)S(1)}, u32[]{:S(2)}, u32[]{:S(2)}) collective-permute-start(f32[264,128]{1,0:T(8,128)S(1)} %shard_map.105.refs_0_), channel_id=1, source_target_pairs={{0,1},{1,0},{2,3},{3,2},{4,5},{5,4},{6,7},{7,6},{8,9},{9,8},{10,11... | collective-permute-start | bytes 405512 | tf_op jit(solution)/shard_map/ppermute | solution.py:21
  75.7 7.6 %collective-permute-start.38 = (f32[16,128]{1,0:T(8,128)S(1)}, f32[16,128]{1,0:T(8,128)S(1)}, u32[]{:S(2)}, u32[]{:S(2)}) collective-permute-start(f32[16,128]{1,0:T(8,128)S(1)} %shard_map.108.after_ref.mine_ref), channel_id=1, source_target_pairs={{0,2},{1,3},{2,0},{3,1},{4,6},{5,7},{6,4},{7,5},{8,10},{9,11},{10,... | collective-permute-start | bytes 24584 | tf_op jit(solution)/shard_map/ppermute | solution.py:21
  78.5 8.3 %collective-permute-start.35 = (f32[128,128]{1,0:T(8,128)S(1)}, f32[128,128]{1,0:T(8,128)S(1)}, u32[]{:S(2)}, u32[]{:S(2)}) collective-permute-start(f32[128,128]{1,0:T(8,128)S(1)} %get-tuple-element.86), channel_id=1, source_target_pairs={{0,4},{1,5},{2,6},{3,7},{4,0},{5,1},{6,2},{7,3},{8,12},{9,13},{10,... | collective-permute-start | bytes 196616 | tf_op jit(solution)/shard_map/ppermute | solution.py:21
  78.8 9.4 %collective-permute-start.36 = (f32[128,128]{1,0:T(8,128)S(1)}, f32[128,128]{1,0:T(8,128)S(1)}, u32[]{:S(2)}, u32[]{:S(2)}) collective-permute-start(f32[128,128]{1,0:T(8,128)S(1)} %get-tuple-element.87), channel_id=1, source_target_pairs={{0,8},{1,9},{2,10},{3,11},{4,12},{5,13},{6,14},{7,15},{8,0},{9,1},... | collective-permute-start | bytes 196616 | tf_op jit(solution)/shard_map/ppermute | solution.py:21
  81.7 6.5 %collective-permute-start.37 = (f32[128,128]{1,0:T(8,128)S(1)}, f32[128,128]{1,0:T(8,128)S(1)}, u32[]{:S(2)}, u32[]{:S(2)}) collective-permute-start(f32[128,128]{1,0:T(8,128)S(1)} %get-tuple-element.88), channel_id=1, source_target_pairs={{0,12},{1,13},{2,14},{3,15},{4,8},{5,9},{6,10},{7,11},{8,4},{9,5},... | collective-permute-start | bytes 196616 | tf_op jit(solution)/shard_map/ppermute | solution.py:21
  83.4 8.1 %collective-permute-start.40 = (f32[80,128]{1,0:T(8,128)S(1)}, f32[80,128]{1,0:T(8,128)S(1)}, u32[]{:S(2)}, u32[]{:S(2)}) collective-permute-start(f32[80,128]{1,0:T(8,128)S(1)} %get-tuple-element.94), channel_id=1, source_target_pairs={{0,64},{16,80},{32,96},{48,112},{64,0},{80,16},{96,32},{112,48},{1... | collective-permute-start | bytes 122888 | tf_op jit(solution)/shard_map/ppermute | solution.py:21
  83.5 8.0 %collective-permute-start.41 = (f32[80,128]{1,0:T(8,128)S(1)}, f32[80,128]{1,0:T(8,128)S(1)}, u32[]{:S(2)}, u32[]{:S(2)}) collective-permute-start(f32[80,128]{1,0:T(8,128)S(1)} %get-tuple-element.95), channel_id=1, source_target_pairs={{0,128},{16,144},{32,160},{48,176},{64,192},{80,208},{96,224},{112... | collective-permute-start | bytes 122888 | tf_op jit(solution)/shard_map/ppermute | solution.py:21
  86.7 5.2 %collective-permute-start.42 = (f32[80,128]{1,0:T(8,128)S(1)}, f32[80,128]{1,0:T(8,128)S(1)}, u32[]{:S(2)}, u32[]{:S(2)}) collective-permute-start(f32[80,128]{1,0:T(8,128)S(1)} %get-tuple-element.96), channel_id=1, source_target_pairs={{0,192},{16,208},{32,224},{48,240},{64,128},{80,144},{96,160},{112... | collective-permute-start | bytes 122888 | tf_op jit(solution)/shard_map/ppermute | solution.py:21
  88.2 18.9 %collective-permute-start.39 = (f32[64,128]{1,0:T(8,128)S(1)}, f32[64,128]{1,0:T(8,128)S(1)}, u32[]{:S(2)}, u32[]{:S(2)}) collective-permute-start(f32[64,128]{1,0:T(8,128)S(1)} %get-tuple-element.92), channel_id=1, source_target_pairs={{0,2},{1,3},{2,0},{3,1},{4,6},{5,7},{6,4},{7,5},{8,10},{9,11},{10,... | collective-permute-start | bytes 98312 | tf_op jit(solution)/shard_map/ppermute | solution.py:21
  94.6 5.5 %collective-permute-start.45 = (f32[32,128]{1,0:T(8,128)S(1)}, f32[32,128]{1,0:T(8,128)S(1)}, u32[]{:S(2)}, u32[]{:S(2)}) collective-permute-start(f32[32,128]{1,0:T(8,128)S(1)} %get-tuple-element.100), channel_id=1, source_target_pairs={{0,48},{16,32},{32,16},{48,0},{64,112},{80,96},{96,80},{112,64},{1... | collective-permute-start | bytes 49160 | tf_op jit(solution)/shard_map/ppermute | solution.py:21
  100.1 4.9 %collective-permute-start.48 = (f32[16,128]{1,0:T(8,128)S(1)}, f32[16,128]{1,0:T(8,128)S(1)}, u32[]{:S(2)}, u32[]{:S(2)}) collective-permute-start(f32[16,128]{1,0:T(8,128)S(1)} %get-tuple-element.101.refs_3_), channel_id=1, source_target_pairs={{0,12},{1,13},{2,14},{3,15},{4,8},{5,9},{6,10},{7,11},{8,4},{9,5},... | collective-permute-start | bytes 24584 | tf_op jit(solution)/shard_map/ppermute | solution.py:21
  101.9 5.2 %collective-permute-start.47 = (f32[16,128]{1,0:T(8,128)S(1)}, f32[16,128]{1,0:T(8,128)S(1)}, u32[]{:S(2)}, u32[]{:S(2)}) collective-permute-start(f32[16,128]{1,0:T(8,128)S(1)} %get-tuple-element.101.refs_3_), channel_id=1, source_target_pairs={{0,8},{1,9},{2,10},{3,11},{4,12},{5,13},{6,14},{7,15},{8,0},{9,1},... | collective-permute-start | bytes 24584 | tf_op jit(solution)/shard_map/ppermute | solution.py:21
  (20 other events, 79.5 us)

commit v3 on v2

--- a/solution.py
+++ b/solution.py
@@ -220,7 +220,7 @@
             ref[share : 2 * share, :] = own_b[...]
 
 
-def join_kernel(z1, z2, g1, g2, g3, out_ref):
+def join_kernel(z1, z2, g3, g2, g1, out_ref):
     rows, few = z1.shape[0], z2.shape[0]
 
     @on_core(0)
@@ -247,7 +247,7 @@
             part = slice(h * sub, (h + 1) * sub)
             out_ref[2 * h * sub : (2 * h + 1) * sub, :] = mine[part, :]
             out_ref[(2 * h + 1) * sub : (2 * h + 2) * sub, :] = other[part, :]
-        out_ref[4 * sub :, :] = mine[2 * sub : first, :]
+        out_ref[4 * sub :, :] = mine[2 * sub : first, :] + other[2 * sub : first, :]
 
     @on_core(1)
     def _():
@@ -259,7 +259,7 @@
 
 
 def unstack_kernel(sub, share, *refs):
-    mine, other, (a_ref, b_ref, near_a, near_b), weeks_ref = refs[:4], refs[4:8], refs[8:12], refs[12:]
+    mine, other, (a_ref, b_ref, near_a, near_b), weeks_ref = refs[3::-1], refs[7:3:-1], refs[8:12], refs[12:]
     core = lax.axis_index("store") % 2
     store, item = lax.axis_index("store") - core, lax.axis_index("item")
     rows = 4 * sub
@@ -294,7 +294,7 @@
     outs = [(16 * sub, rank), (16 * share, rank), (2 * sub, rank), (4 * share, rank)]
     outs = outs + ([(weeks, rank)] if weeks else [])
     others = [swap(row, "store", CORE) for row in rows]
-    return small_call(functools.partial(unstack_kernel, sub, share), outs, *rows, *others)
+    return small_call(functools.partial(unstack_kernel, sub, share), outs, *rows[::-1], *others[::-1])
 
 
 def pack_kernel(used, gbt_ref, mine_ref, core_ref, *refs):
@@ -339,7 +339,7 @@
     refs[-1][...] = tree([ref[:rows, :] for ref in refs[:-1]])
 
 
-def mid_kernel(rate_a, rate_b, share, x0, z1, z2, z3, oldb_ref, mine, got, olda_ref, out_ref):
+def mid_kernel(rate_a, rate_b, share, x0, z3, z2, z1, oldb_ref, mine, got, olda_ref, out_ref):
     terms = (x0, z1, z2, z3)
     n = mine.shape[0]
     half = n // 2
@@ -375,7 +375,7 @@
 
 
 def end_kernel(rate_a, rate_b, rate_c, count, *refs):
-    keep, got, old_ref, e0, e1, e2, e3, c_ref, gradb_ref, b_ref, newa_ref, newb_ref, newc_ref, loss_ref = refs
+    keep, got, old_ref, e0, e3, e2, e1, c_ref, gradb_ref, b_ref, newa_ref, newb_ref, newc_ref, loss_ref = refs
     newb_ref[...] = b_ref[: newb_ref.shape[0], :] - rate_b * gradb_ref[...]
     newa_ref[...] = old_ref[: keep.shape[0], :] - rate_a * (keep[...] + got[...])
     total = (e0[...] + e1[...]) + (e2[...] + e3[...])
@@ -423,17 +423,16 @@
     ])
     z1, z2 = small_call(near_kernel, [pair, (2 * share, rank)], own, other_a, own_b, other_b)
     near = [chip_swap(z1, ZHI, 1), chip_swap(z2, 0, 2), chip_swap(z2, 0, 3)]
-    (value,) = small_call(join_kernel, [(4 * sub, rank)], z1, z2, *near, flops=LONG)
+    (value,) = small_call(join_kernel, [(4 * sub, rank)], z1, z2, *near[::-1], flops=LONG)
     block_a, block_b, mine_a, mine_b = far_gather(sub, share, value, 0)
     old = jnp.zeros((weeks + 8, rank), F32)
     errors, gbt, old, factor_c = step_call(rate_c, False, sales, late, block_a, block_b, week_factors, old)
 
-    (part_c,) = small_call(sum_kernel, [(weeks + 8, rank)], old, swap(old, "store", CORE))
-    got_c = swap(part_c, "store", ZHI)
-    send, own = items_grad_call(errors, block_b, factor_c, part_c)
+    got_c = swap(old, "store", ZHI)
+    send, own = items_grad_call(errors, block_b, factor_c, old)
     parts = small_call(core_sum_kernel, [pair] * 4, own, swap(send, "store", CORE))
     parts = [parts[0]] + over(parts[1:], "store", OUTER)
-    dealt = pack_call(gbt, part_c, got_c, 4 * share + weeks, 2 * sub + weeks)
+    dealt = pack_call(gbt, old, got_c, 4 * share + weeks, 2 * sub + weeks)
     dealt = [dealt[0]] + over(dealt[1:], "item", OUTER)
     (part_a,) = small_call(sum_after_kernel, [pair], *parts, dealt[0])
     got_a = swap(part_a, "store", ZHI)
@@ -442,7 +441,7 @@
     (new,) = small_call(
         functools.partial(mid_kernel, rate_a, rate_b, share),
         [(2 * sub + weeks + 4 * share, rank)],
-        part_b, *near, mine_b, part_a, got_a, mine_a,
+        part_b, *near[::-1], mine_b, part_a, got_a, mine_a,
     )
     (value,) = small_call(
         functools.partial(merge_kernel, sub, share), [(4 * sub + weeks, rank)], new, swap(new, "store", CORE)
@@ -469,7 +468,7 @@
         out_specs=[VM, VM, VM, pl.BlockSpec(memory_space=pltpu.SMEM)],
         compiler_params=pltpu.CompilerParams(vmem_limit_bytes=8 * MIB),
         cost_estimate=pl.CostEstimate(flops=0, bytes_accessed=0, transcendentals=0),
-    )(keep, got_a, mine_a, part_c, *over([part_c] * 3, "store", OUTER), factor_c, grad_b, mine_b)
+    )(keep, got_a, mine_a, part_c, *over([part_c] * 3, "store", OUTER)[::-1], factor_c, grad_b, mine_b)
     return shard_a, shard_b, factor_c, losses
 
 

time: 108 us -> 108 us (level)
    ppermute x40 -> x39, starting transfers between devices: 54.3 us -> 53.3 us  [swap(): return lax.ppermute(value, axis, [(i, i ^ bits) for i in range(16)])]
    ppermute x40 -> x39, waiting for transfers between devices: 14.4 us -> 14.2 us  [swap(): return lax.ppermute(value, axis, [(i, i ^ bits) for i in range(16)])]
  transfers between devices with their start and end apart: 49 -> 48, of which waited for: 20 -> 20; matrix products, arithmetic and copies ran while one was open for 0% -> 0% of each run, Pallas kernels for 1% -> 1%
where the time goes in v3:
time: 108 us; the launch traced here: 107 us
  starting transfers between devices  70.9 us (66%)
  waiting for transfers between devices  21.7 us (20%)
  Pallas kernels  13.3 us (12%)
  between operations  1.09 us (1%)
    ppermute x39, starting transfers between devices, swap(): return lax.ppermute(value, axis, [(i, i ^ bits) for i in range(16)])  53.3 us
    ppermute x9, starting transfers between devices, chip_swap(): return lax.ppermute(value, ('item', 'store'), pairs)  17.6 us
    ppermute x39, waiting for transfers between devices, swap(): return lax.ppermute(value, axis, [(i, i ^ bits) for i in range(16)])  14.2 us
    pallas_call x2, Pallas kernels, step_call(): pl.pallas_call(functools.partial(step_kernel, rate_c, riding), out_shape=...  8.29 us
    ppermute x9, waiting for transfers between devices, chip_swap(): return lax.ppermute(value, ('item', 'store'), pairs)  7.45 us
    pallas_call x2, Pallas kernels, items_grad_call(): pl.pallas_call(items_grad_kernel, out_shape=[jax.ShapeDtypeStruct((n_item...  2.6 us
  transfers between devices with their start and end apart: 48, of which 20 were waited for; matrix products, arithmetic and copies ran while one was open for 0% of the time, Pallas kernels for 1%

profile of v3, /device:TPU:6, one launch (start us, length us, event | category | flops | bytes accessed | tf_op | source)
XLA Modules:
  0.0 107.0 jit_solution(15718605180413603830)
XLA Ops:
  2.3 7.3 %collective-permute-start.4 = (f32[128,128]{1,0:T(8,128)S(1)}, f32[128,128]{1,0:T(8,128)S(1)}, u32[]{:S(2)}, u32[]{:S(2)}) collective-permute-start(f32[128,128]{1,0:T(8,128)S(1)} %get-tuple-element.57.z1), channel_id=1, source_target_pairs={{0,2},{1,17},{2,0},{3,19},{4,6},{5,21},{6,4},{7,23},{8,10},{9,25},... | collective-permute-start | bytes 196616 | tf_op jit(solution)/shard_map/ppermute | solution.py:32
  12.2 1.7 %collective-permute-start.7 = (f32[256,128]{1,0:T(8,128)S(1)}, f32[256,128]{1,0:T(8,128)S(1)}, u32[]{:S(2)}, u32[]{:S(2)}) collective-permute-start(f32[256,128]{1,0:T(8,128)S(1)} %shard_map.95.refs_3_), channel_id=1, source_target_pairs={{0,4},{1,65},{2,6},{3,67},{4,0},{5,69},{6,2},{7,71},{8,12},{9,73},... | collective-permute-start | bytes 393224 | tf_op jit(solution)/shard_map/ppermute | solution.py:32
  13.9 2.2 %collective-permute-start.5 = (f32[256,128]{1,0:T(8,128)S(1)}, f32[256,128]{1,0:T(8,128)S(1)}, u32[]{:S(2)}, u32[]{:S(2)}) collective-permute-start(f32[256,128]{1,0:T(8,128)S(1)} %shard_map.95.refs_3_), channel_id=1, source_target_pairs={{0,12},{1,193},{2,14},{3,195},{4,8},{5,197},{6,10},{7,199},{8,4},{... | collective-permute-start | bytes 393224 | tf_op jit(solution)/shard_map/ppermute | solution.py:32
  20.1 2.0 %collective-permute-start.8 = (f32[256,128]{1,0:T(8,128)S(1)}, f32[256,128]{1,0:T(8,128)S(1)}, u32[]{:S(2)}, u32[]{:S(2)}) collective-permute-start(f32[256,128]{1,0:T(8,128)S(1)} %collective-permute-done.5.refs_0_), channel_id=1, source_target_pairs={{0,1},{1,0},{2,3},{3,2},{4,5},{5,4},{6,7},{7,6},{8,9},{9,8},{10,11... | collective-permute-start | bytes 393224 | tf_op jit(solution)/shard_map/ppermute | solution.py:21
  24.0 4.2 %shard_map.97 = (bf16[8,1024,256]{2,1,0:T(8,128)(2,1)S(1)}, f32[128,256]{1,0:T(8,128)S(1)}, f32[16,128]{1,0:T(8,128)S(1)}, f32[8,128]{1,0:T(8,128)S(1)}) custom-call(f32[8,1024,256]{2,1,0:T(8,128)S(1)} %bitcast.3, s32[1024,256]{1,0:T(8,128)S(1)} %get-tuple-element.54.refs_1_, f32[1024,128]{1,0:T(8,128)S(1)} %get-tuple-element.59.refs_2_, ...), custom_call_target="tpu_custom_call" | custom-call | flops 1073741824 | bytes 8388608 | tf_op jit(solution)/shard_map/pallas_call | solution.py:136
  29.7 6.1 %collective-permute-start.12 = (f32[16,128]{1,0:T(8,128)S(1)}, f32[16,128]{1,0:T(8,128)S(1)}, u32[]{:S(2)}, u32[]{:S(2)}) collective-permute-start(f32[16,128]{1,0:T(8,128)S(1)} %get-tuple-element.62.mine_ref.after_ref.refs_5_), channel_id=1, source_target_pairs={{0,2},{1,3},{2,0},{3,1},{4,6},{5,7},{6,4},{7,5},{8,10},{9,11},{10,... | collective-permute-start | bytes 24584 | tf_op jit(solution)/shard_map/ppermute | solution.py:21
  36.8 2.1 %collective-permute-start.21 = (f32[128,128]{1,0:T(8,128)S(1)}, f32[128,128]{1,0:T(8,128)S(1)}, u32[]{:S(2)}, u32[]{:S(2)}) collective-permute-start(f32[128,128]{1,0:T(8,128)S(1)} %get-tuple-element.74), channel_id=1, source_target_pairs={{0,8},{1,9},{2,10},{3,11},{4,12},{5,13},{6,14},{7,15},{8,0},{9,1},... | collective-permute-start | bytes 196616 | tf_op jit(solution)/shard_map/ppermute | solution.py:21
  38.9 1.9 %collective-permute-start.22 = (f32[128,128]{1,0:T(8,128)S(1)}, f32[128,128]{1,0:T(8,128)S(1)}, u32[]{:S(2)}, u32[]{:S(2)}) collective-permute-start(f32[128,128]{1,0:T(8,128)S(1)} %get-tuple-element.75), channel_id=1, source_target_pairs={{0,12},{1,13},{2,14},{3,15},{4,8},{5,9},{6,10},{7,11},{8,4},{9,5},... | collective-permute-start | bytes 196616 | tf_op jit(solution)/shard_map/ppermute | solution.py:21
  43.0 2.8 %collective-permute-start.15 = (f32[136,128]{1,0:T(8,128)S(1)}, f32[136,128]{1,0:T(8,128)S(1)}, u32[]{:S(2)}, u32[]{:S(2)}) collective-permute-start(f32[136,128]{1,0:T(8,128)S(1)} %get-tuple-element.66), channel_id=1, source_target_pairs={{0,192},{16,208},{32,224},{48,240},{64,128},{80,144},{96,160},{112... | collective-permute-start | bytes 208904 | tf_op jit(solution)/shard_map/ppermute | solution.py:21
  45.8 2.6 %collective-permute-start.23 = (f32[128,128]{1,0:T(8,128)S(1)}, f32[128,128]{1,0:T(8,128)S(1)}, u32[]{:S(2)}, u32[]{:S(2)}) collective-permute-start(f32[128,128]{1,0:T(8,128)S(1)} %shard_map.102.mine), channel_id=1, source_target_pairs={{0,2},{1,3},{2,0},{3,1},{4,6},{5,7},{6,4},{7,5},{8,10},{9,11},{10,... | collective-permute-start | bytes 196616 | tf_op jit(solution)/shard_map/ppermute | solution.py:21
  48.5 1.5 %collective-permute-start.16 = (f32[72,128]{1,0:T(8,128)S(1)}, f32[72,128]{1,0:T(8,128)S(1)}, u32[]{:S(2)}, u32[]{:S(2)}) collective-permute-start(f32[72,128]{1,0:T(8,128)S(1)} %shard_map.99.x0), channel_id=1, source_target_pairs={{0,48},{16,32},{32,16},{48,0},{64,112},{80,96},{96,80},{112,64},{1... | collective-permute-start | bytes 110600 | tf_op jit(solution)/shard_map/ppermute | solution.py:21
  50.6 2.4 %collective-permute-start.18 = (f32[72,128]{1,0:T(8,128)S(1)}, f32[72,128]{1,0:T(8,128)S(1)}, u32[]{:S(2)}, u32[]{:S(2)}) collective-permute-start(f32[72,128]{1,0:T(8,128)S(1)} %shard_map.99.x0), channel_id=1, source_target_pairs={{0,16},{16,0},{32,48},{48,32},{64,80},{80,64},{96,112},{112,96},{1... | collective-permute-start | bytes 110600 | tf_op jit(solution)/shard_map/ppermute | solution.py:21
  53.0 1.4 %collective-permute-done.16.z3 = f32[72,128]{1,0:T(8,128)S(1)} collective-permute-done((f32[72,128]{1,0:T(8,128)S(1)}, f32[72,128]{1,0:T(8,128)S(1)}, u32[]{:S(2)}, u32[]{:S(2)}) %collective-permute-start.16) | collective-permute-done | bytes 36896 | tf_op jit(solution)/shard_map/ppermute | solution.py:21
  57.0 2.4 %collective-permute-start.25 = (f32[264,128]{1,0:T(8,128)S(1)}, f32[264,128]{1,0:T(8,128)S(1)}, u32[]{:S(2)}, u32[]{:S(2)}) collective-permute-start(f32[264,128]{1,0:T(8,128)S(1)} %shard_map.104.refs_3_), channel_id=1, source_target_pairs={{0,12},{1,193},{2,14},{3,195},{4,8},{5,197},{6,10},{7,199},{8,4},{... | collective-permute-start | bytes 405512 | tf_op jit(solution)/shard_map/ppermute | solution.py:32
  59.5 1.7 %collective-permute-start.27 = (f32[264,128]{1,0:T(8,128)S(1)}, f32[264,128]{1,0:T(8,128)S(1)}, u32[]{:S(2)}, u32[]{:S(2)}) collective-permute-start(f32[264,128]{1,0:T(8,128)S(1)} %shard_map.104.refs_3_), channel_id=1, source_target_pairs={{0,4},{1,65},{2,6},{3,67},{4,0},{5,69},{6,2},{7,71},{8,12},{9,73},... | collective-permute-start | bytes 405512 | tf_op jit(solution)/shard_map/ppermute | solution.py:32
  61.2 2.1 %collective-permute-done.25.refs_0_ = f32[264,128]{1,0:T(8,128)S(1)} collective-permute-done((f32[264,128]{1,0:T(8,128)S(1)}, f32[264,128]{1,0:T(8,128)S(1)}, u32[]{:S(2)}, u32[]{:S(2)}) %collective-permute-start.25) | collective-permute-done | bytes 135200 | tf_op jit(solution)/shard_map/ppermute | solution.py:32
  63.3 2.6 %collective-permute-done.26.refs_1_ = f32[264,128]{1,0:T(8,128)S(1)} collective-permute-done((f32[264,128]{1,0:T(8,128)S(1)}, f32[264,128]{1,0:T(8,128)S(1)}, u32[]{:S(2)}, u32[]{:S(2)}) %collective-permute-start.26) | collective-permute-done | bytes 135200 | tf_op jit(solution)/shard_map/ppermute | solution.py:32
  67.8 4.1 %shard_map.106 = (bf16[8,1024,256]{2,1,0:T(8,128)(2,1)S(1)}, f32[128,256]{1,0:T(8,128)S(1)}, f32[16,128]{1,0:T(8,128)S(1)}, f32[8,128]{1,0:T(8,128)S(1)}) custom-call(f32[8,1024,256]{2,1,0:T(8,128)S(1)} %bitcast.3, s32[1024,256]{1,0:T(8,128)S(1)} %get-tuple-element.54.refs_1_, f32[1024,128]{1,0:T(8,128)S(1)} %get-tuple-element.77.refs_2_, ...), custom_call_target="tpu_custom_call" | custom-call | flops 1073741824 | bytes 8388608 | tf_op jit(solution)/shard_map/pallas_call | solution.py:136
  73.2 1.3 %shard_map.108 = (f32[512,128]{1,0:T(8,128)S(1)}, f32[512,128]{1,0:T(8,128)S(1)}) custom-call(bf16[8,1024,256]{2,1,0:T(8,128)(2,1)S(1)} %get-tuple-element.80.er, f32[256,128]{1,0:T(8,128)S(1)} %get-tuple-element.78.refs_3_.b_ref, f32[8,128]{1,0:T(8,128)S(1)} %get-tuple-element.81.c_ref.refs_7_, f32[16,128]{1,0:T(8,128)S(1)} %shard_map.107.after_ref.mine_ref), custom_call_target="tpu_custom_call" | custom-call | tf_op jit(solution)/shard_map/pallas_call | solution.py:175
  74.9 2.6 %collective-permute-start.37 = (f32[16,128]{1,0:T(8,128)S(1)}, f32[16,128]{1,0:T(8,128)S(1)}, u32[]{:S(2)}, u32[]{:S(2)}) collective-permute-start(f32[16,128]{1,0:T(8,128)S(1)} %shard_map.107.after_ref.mine_ref), channel_id=1, source_target_pairs={{0,2},{1,3},{2,0},{3,1},{4,6},{5,7},{6,4},{7,5},{8,10},{9,11},{10,... | collective-permute-start | bytes 24584 | tf_op jit(solution)/shard_map/ppermute | solution.py:21
  78.0 2.7 %collective-permute-start.35 = (f32[128,128]{1,0:T(8,128)S(1)}, f32[128,128]{1,0:T(8,128)S(1)}, u32[]{:S(2)}, u32[]{:S(2)}) collective-permute-start(f32[128,128]{1,0:T(8,128)S(1)} %get-tuple-element.87), channel_id=1, source_target_pairs={{0,8},{1,9},{2,10},{3,11},{4,12},{5,13},{6,14},{7,15},{8,0},{9,1},... | collective-permute-start | bytes 196616 | tf_op jit(solution)/shard_map/ppermute | solution.py:21
  80.7 1.6 %collective-permute-start.36 = (f32[128,128]{1,0:T(8,128)S(1)}, f32[128,128]{1,0:T(8,128)S(1)}, u32[]{:S(2)}, u32[]{:S(2)}) collective-permute-start(f32[128,128]{1,0:T(8,128)S(1)} %get-tuple-element.88), channel_id=1, source_target_pairs={{0,12},{1,13},{2,14},{3,15},{4,8},{5,9},{6,10},{7,11},{8,4},{9,5},... | collective-permute-start | bytes 196616 | tf_op jit(solution)/shard_map/ppermute | solution.py:21
  82.6 3.3 %collective-permute-start.40 = (f32[80,128]{1,0:T(8,128)S(1)}, f32[80,128]{1,0:T(8,128)S(1)}, u32[]{:S(2)}, u32[]{:S(2)}) collective-permute-start(f32[80,128]{1,0:T(8,128)S(1)} %get-tuple-element.95), channel_id=1, source_target_pairs={{0,128},{16,144},{32,160},{48,176},{64,192},{80,208},{96,224},{112... | collective-permute-start | bytes 122888 | tf_op jit(solution)/shard_map/ppermute | solution.py:21
  86.0 1.4 %collective-permute-start.41 = (f32[80,128]{1,0:T(8,128)S(1)}, f32[80,128]{1,0:T(8,128)S(1)}, u32[]{:S(2)}, u32[]{:S(2)}) collective-permute-start(f32[80,128]{1,0:T(8,128)S(1)} %get-tuple-element.96), channel_id=1, source_target_pairs={{0,192},{16,208},{32,224},{48,240},{64,128},{80,144},{96,160},{112... | collective-permute-start | bytes 122888 | tf_op jit(solution)/shard_map/ppermute | solution.py:21
  87.4 3.3 %collective-permute-start.38 = (f32[64,128]{1,0:T(8,128)S(1)}, f32[64,128]{1,0:T(8,128)S(1)}, u32[]{:S(2)}, u32[]{:S(2)}) collective-permute-start(f32[64,128]{1,0:T(8,128)S(1)} %get-tuple-element.92), channel_id=1, source_target_pairs={{0,2},{1,3},{2,0},{3,1},{4,6},{5,7},{6,4},{7,5},{8,10},{9,11},{10,... | collective-permute-start | bytes 98312 | tf_op jit(solution)/shard_map/ppermute | solution.py:21
  91.2 1.7 %collective-permute-start.42 = (f32[32,128]{1,0:T(8,128)S(1)}, f32[32,128]{1,0:T(8,128)S(1)}, u32[]{:S(2)}, u32[]{:S(2)}) collective-permute-start(f32[32,128]{1,0:T(8,128)S(1)} %get-tuple-element.98), channel_id=1, source_target_pairs={{0,16},{16,0},{32,48},{48,32},{64,80},{80,64},{96,112},{112,96},{1... | collective-permute-start | bytes 49160 | tf_op jit(solution)/shard_map/ppermute | solution.py:21
  93.8 1.9 %collective-permute-start.44 = (f32[32,128]{1,0:T(8,128)S(1)}, f32[32,128]{1,0:T(8,128)S(1)}, u32[]{:S(2)}, u32[]{:S(2)}) collective-permute-start(f32[32,128]{1,0:T(8,128)S(1)} %get-tuple-element.100), channel_id=1, source_target_pairs={{0,48},{16,32},{32,16},{48,0},{64,112},{80,96},{96,80},{112,64},{1... | collective-permute-start | bytes 49160 | tf_op jit(solution)/shard_map/ppermute | solution.py:21
  95.7 1.9 %collective-permute-done.43.z2 = f32[32,128]{1,0:T(8,128)S(1)} collective-permute-done((f32[32,128]{1,0:T(8,128)S(1)}, f32[32,128]{1,0:T(8,128)S(1)}, u32[]{:S(2)}, u32[]{:S(2)}) %collective-permute-start.43) | collective-permute-done | bytes 16416 | tf_op jit(solution)/shard_map/ppermute | solution.py:21
  97.6 1.8 %collective-permute-done.44.z3 = f32[32,128]{1,0:T(8,128)S(1)} collective-permute-done((f32[32,128]{1,0:T(8,128)S(1)}, f32[32,128]{1,0:T(8,128)S(1)}, u32[]{:S(2)}, u32[]{:S(2)}) %collective-permute-start.44) | collective-permute-done | bytes 16416 | tf_op jit(solution)/shard_map/ppermute | solution.py:21
  99.4 1.7 %collective-permute-start.45 = (f32[16,128]{1,0:T(8,128)S(1)}, f32[16,128]{1,0:T(8,128)S(1)}, u32[]{:S(2)}, u32[]{:S(2)}) collective-permute-start(f32[16,128]{1,0:T(8,128)S(1)} %get-tuple-element.101.refs_3_), channel_id=1, source_target_pairs={{0,12},{1,13},{2,14},{3,15},{4,8},{5,9},{6,10},{7,11},{8,4},{9,5},... | collective-permute-start | bytes 24584 | tf_op jit(solution)/shard_map/ppermute | solution.py:21
  102.1 1.5 %collective-permute-start.47 = (f32[16,128]{1,0:T(8,128)S(1)}, f32[16,128]{1,0:T(8,128)S(1)}, u32[]{:S(2)}, u32[]{:S(2)}) collective-permute-start(f32[16,128]{1,0:T(8,128)S(1)} %get-tuple-element.101.refs_3_), channel_id=1, source_target_pairs={{0,4},{1,5},{2,6},{3,7},{4,0},{5,1},{6,2},{7,3},{8,12},{9,13},{10,... | collective-permute-start | bytes 24584 | tf_op jit(solution)/shard_map/ppermute | solution.py:21
  104.3 1.9 %collective-permute-done.46.refs_5_ = f32[16,128]{1,0:T(8,128)S(1)} collective-permute-done((f32[16,128]{1,0:T(8,128)S(1)}, f32[16,128]{1,0:T(8,128)S(1)}, u32[]{:S(2)}, u32[]{:S(2)}) %collective-permute-start.46) | collective-permute-done | bytes 8224 | tf_op jit(solution)/shard_map/ppermute | solution.py:21
  (94 shorter events, 26.6 us)
Async XLA Ops:
  2.3 9.9 %collective-permute-start.4 = (f32[128,128]{1,0:T(8,128)S(1)}, f32[128,128]{1,0:T(8,128)S(1)}, u32[]{:S(2)}, u32[]{:S(2)}) collective-permute-start(f32[128,128]{1,0:T(8,128)S(1)} %get-tuple-element.57.z1), channel_id=1, source_target_pairs={{0,2},{1,17},{2,0},{3,19},{4,6},{5,21},{6,4},{7,23},{8,10},{9,25},... | collective-permute-start | bytes 196616 | tf_op jit(solution)/shard_map/ppermute | solution.py:32
  12.2 5.8 %collective-permute-start.7 = (f32[256,128]{1,0:T(8,128)S(1)}, f32[256,128]{1,0:T(8,128)S(1)}, u32[]{:S(2)}, u32[]{:S(2)}) collective-permute-start(f32[256,128]{1,0:T(8,128)S(1)} %shard_map.95.refs_3_), channel_id=1, source_target_pairs={{0,4},{1,65},{2,6},{3,67},{4,0},{5,69},{6,2},{7,71},{8,12},{9,73},... | collective-permute-start | bytes 393224 | tf_op jit(solution)/shard_map/ppermute | solution.py:32
  13.9 6.2 %collective-permute-start.5 = (f32[256,128]{1,0:T(8,128)S(1)}, f32[256,128]{1,0:T(8,128)S(1)}, u32[]{:S(2)}, u32[]{:S(2)}) collective-permute-start(f32[256,128]{1,0:T(8,128)S(1)} %shard_map.95.refs_3_), channel_id=1, source_target_pairs={{0,12},{1,193},{2,14},{3,195},{4,8},{5,197},{6,10},{7,199},{8,4},{... | collective-permute-start | bytes 393224 | tf_op jit(solution)/shard_map/ppermute | solution.py:32
  16.1 6.5 %collective-permute-start.6 = (f32[256,128]{1,0:T(8,128)S(1)}, f32[256,128]{1,0:T(8,128)S(1)}, u32[]{:S(2)}, u32[]{:S(2)}) collective-permute-start(f32[256,128]{1,0:T(8,128)S(1)} %shard_map.95.refs_3_), channel_id=1, source_target_pairs={{0,8},{1,129},{2,10},{3,131},{4,12},{5,133},{6,14},{7,135},{8,0},{... | collective-permute-start | bytes 393224 | tf_op jit(solution)/shard_map/ppermute | solution.py:32
  16.8 5.8 %collective-permute-start.11 = (f32[256,128]{1,0:T(8,128)S(1)}, f32[256,128]{1,0:T(8,128)S(1)}, u32[]{:S(2)}, u32[]{:S(2)}) collective-permute-start(f32[256,128]{1,0:T(8,128)S(1)} %shard_map.95.refs_3_), channel_id=1, source_target_pairs={{0,1},{1,0},{2,3},{3,2},{4,5},{5,4},{6,7},{7,6},{8,9},{9,8},{10,11... | collective-permute-start | bytes 393224 | tf_op jit(solution)/shard_map/ppermute | solution.py:21
  29.5 6.3 %collective-permute-start.19 = (f32[512,128]{1,0:T(8,128)S(1)}, f32[512,128]{1,0:T(8,128)S(1)}, u32[]{:S(2)}, u32[]{:S(2)}) collective-permute-start(f32[512,128]{1,0:T(8,128)S(1)} %get-tuple-element.71), channel_id=1, source_target_pairs={{0,1},{1,0},{2,3},{3,2},{4,5},{5,4},{6,7},{7,6},{8,9},{9,8},{10,11... | collective-permute-start | bytes 786440 | tf_op jit(solution)/shard_map/ppermute | solution.py:21
  29.7 11.1 %collective-permute-start.12 = (f32[16,128]{1,0:T(8,128)S(1)}, f32[16,128]{1,0:T(8,128)S(1)}, u32[]{:S(2)}, u32[]{:S(2)}) collective-permute-start(f32[16,128]{1,0:T(8,128)S(1)} %get-tuple-element.62.mine_ref.after_ref.refs_5_), channel_id=1, source_target_pairs={{0,2},{1,3},{2,0},{3,1},{4,6},{5,7},{6,4},{7,5},{8,10},{9,11},{10,... | collective-permute-start | bytes 24584 | tf_op jit(solution)/shard_map/ppermute | solution.py:21
  35.9 7.1 %collective-permute-start.20 = (f32[128,128]{1,0:T(8,128)S(1)}, f32[128,128]{1,0:T(8,128)S(1)}, u32[]{:S(2)}, u32[]{:S(2)}) collective-permute-start(f32[128,128]{1,0:T(8,128)S(1)} %get-tuple-element.73), channel_id=1, source_target_pairs={{0,4},{1,5},{2,6},{3,7},{4,0},{5,1},{6,2},{7,3},{8,12},{9,13},{10,... | collective-permute-start | bytes 196616 | tf_op jit(solution)/shard_map/ppermute | solution.py:21
  36.8 8.9 %collective-permute-start.21 = (f32[128,128]{1,0:T(8,128)S(1)}, f32[128,128]{1,0:T(8,128)S(1)}, u32[]{:S(2)}, u32[]{:S(2)}) collective-permute-start(f32[128,128]{1,0:T(8,128)S(1)} %get-tuple-element.74), channel_id=1, source_target_pairs={{0,8},{1,9},{2,10},{3,11},{4,12},{5,13},{6,14},{7,15},{8,0},{9,1},... | collective-permute-start | bytes 196616 | tf_op jit(solution)/shard_map/ppermute | solution.py:21
  38.9 6.8 %collective-permute-start.22 = (f32[128,128]{1,0:T(8,128)S(1)}, f32[128,128]{1,0:T(8,128)S(1)}, u32[]{:S(2)}, u32[]{:S(2)}) collective-permute-start(f32[128,128]{1,0:T(8,128)S(1)} %get-tuple-element.75), channel_id=1, source_target_pairs={{0,12},{1,13},{2,14},{3,15},{4,8},{5,9},{6,10},{7,11},{8,4},{9,5},... | collective-permute-start | bytes 196616 | tf_op jit(solution)/shard_map/ppermute | solution.py:21
  40.9 7.5 %collective-permute-start.13 = (f32[136,128]{1,0:T(8,128)S(1)}, f32[136,128]{1,0:T(8,128)S(1)}, u32[]{:S(2)}, u32[]{:S(2)}) collective-permute-start(f32[136,128]{1,0:T(8,128)S(1)} %get-tuple-element.64), channel_id=1, source_target_pairs={{0,64},{16,80},{32,96},{48,112},{64,0},{80,16},{96,32},{112,48},{1... | collective-permute-start | bytes 208904 | tf_op jit(solution)/shard_map/ppermute | solution.py:21
  41.9 6.6 %collective-permute-start.14 = (f32[136,128]{1,0:T(8,128)S(1)}, f32[136,128]{1,0:T(8,128)S(1)}, u32[]{:S(2)}, u32[]{:S(2)}) collective-permute-start(f32[136,128]{1,0:T(8,128)S(1)} %get-tuple-element.65), channel_id=1, source_target_pairs={{0,128},{16,144},{32,160},{48,176},{64,192},{80,208},{96,224},{112... | collective-permute-start | bytes 208904 | tf_op jit(solution)/shard_map/ppermute | solution.py:21
  43.0 5.5 %collective-permute-start.15 = (f32[136,128]{1,0:T(8,128)S(1)}, f32[136,128]{1,0:T(8,128)S(1)}, u32[]{:S(2)}, u32[]{:S(2)}) collective-permute-start(f32[136,128]{1,0:T(8,128)S(1)} %get-tuple-element.66), channel_id=1, source_target_pairs={{0,192},{16,208},{32,224},{48,240},{64,128},{80,144},{96,160},{112... | collective-permute-start | bytes 208904 | tf_op jit(solution)/shard_map/ppermute | solution.py:21
  45.8 9.8 %collective-permute-start.23 = (f32[128,128]{1,0:T(8,128)S(1)}, f32[128,128]{1,0:T(8,128)S(1)}, u32[]{:S(2)}, u32[]{:S(2)}) collective-permute-start(f32[128,128]{1,0:T(8,128)S(1)} %shard_map.102.mine), channel_id=1, source_target_pairs={{0,2},{1,3},{2,0},{3,1},{4,6},{5,7},{6,4},{7,5},{8,10},{9,11},{10,... | collective-permute-start | bytes 196616 | tf_op jit(solution)/shard_map/ppermute | solution.py:21
  48.5 5.9 %collective-permute-start.16 = (f32[72,128]{1,0:T(8,128)S(1)}, f32[72,128]{1,0:T(8,128)S(1)}, u32[]{:S(2)}, u32[]{:S(2)}) collective-permute-start(f32[72,128]{1,0:T(8,128)S(1)} %shard_map.99.x0), channel_id=1, source_target_pairs={{0,48},{16,32},{32,16},{48,0},{64,112},{80,96},{96,80},{112,64},{1... | collective-permute-start | bytes 110600 | tf_op jit(solution)/shard_map/ppermute | solution.py:21
  50.0 5.5 %collective-permute-start.17 = (f32[72,128]{1,0:T(8,128)S(1)}, f32[72,128]{1,0:T(8,128)S(1)}, u32[]{:S(2)}, u32[]{:S(2)}) collective-permute-start(f32[72,128]{1,0:T(8,128)S(1)} %shard_map.99.x0), channel_id=1, source_target_pairs={{0,32},{16,48},{32,0},{48,16},{64,96},{80,112},{96,64},{112,80},{1... | collective-permute-start | bytes 110600 | tf_op jit(solution)/shard_map/ppermute | solution.py:21
  50.6 5.0 %collective-permute-start.18 = (f32[72,128]{1,0:T(8,128)S(1)}, f32[72,128]{1,0:T(8,128)S(1)}, u32[]{:S(2)}, u32[]{:S(2)}) collective-permute-start(f32[72,128]{1,0:T(8,128)S(1)} %shard_map.99.x0), channel_id=1, source_target_pairs={{0,16},{16,0},{32,48},{48,32},{64,80},{80,64},{96,112},{112,96},{1... | collective-permute-start | bytes 110600 | tf_op jit(solution)/shard_map/ppermute | solution.py:21
  57.0 6.3 %collective-permute-start.25 = (f32[264,128]{1,0:T(8,128)S(1)}, f32[264,128]{1,0:T(8,128)S(1)}, u32[]{:S(2)}, u32[]{:S(2)}) collective-permute-start(f32[264,128]{1,0:T(8,128)S(1)} %shard_map.104.refs_3_), channel_id=1, source_target_pairs={{0,12},{1,193},{2,14},{3,195},{4,8},{5,197},{6,10},{7,199},{8,4},{... | collective-permute-start | bytes 405512 | tf_op jit(solution)/shard_map/ppermute | solution.py:32
  59.4 6.5 %collective-permute-start.26 = (f32[264,128]{1,0:T(8,128)S(1)}, f32[264,128]{1,0:T(8,128)S(1)}, u32[]{:S(2)}, u32[]{:S(2)}) collective-permute-start(f32[264,128]{1,0:T(8,128)S(1)} %shard_map.104.refs_3_), channel_id=1, source_target_pairs={{0,8},{1,129},{2,10},{3,131},{4,12},{5,133},{6,14},{7,135},{8,0},{... | collective-permute-start | bytes 405512 | tf_op jit(solution)/shard_map/ppermute | solution.py:32
  59.5 6.4 %collective-permute-start.27 = (f32[264,128]{1,0:T(8,128)S(1)}, f32[264,128]{1,0:T(8,128)S(1)}, u32[]{:S(2)}, u32[]{:S(2)}) collective-permute-start(f32[264,128]{1,0:T(8,128)S(1)} %shard_map.104.refs_3_), channel_id=1, source_target_pairs={{0,4},{1,65},{2,6},{3,67},{4,0},{5,69},{6,2},{7,71},{8,12},{9,73},... | collective-permute-start | bytes 405512 | tf_op jit(solution)/shard_map/ppermute | solution.py:32
  61.2 5.3 %collective-permute-start.31 = (f32[264,128]{1,0:T(8,128)S(1)}, f32[264,128]{1,0:T(8,128)S(1)}, u32[]{:S(2)}, u32[]{:S(2)}) collective-permute-start(f32[264,128]{1,0:T(8,128)S(1)} %shard_map.104.refs_3_), channel_id=1, source_target_pairs={{0,1},{1,0},{2,3},{3,2},{4,5},{5,4},{6,7},{7,6},{8,9},{9,8},{10,11... | collective-permute-start | bytes 405512 | tf_op jit(solution)/shard_map/ppermute | solution.py:21
  74.9 7.6 %collective-permute-start.37 = (f32[16,128]{1,0:T(8,128)S(1)}, f32[16,128]{1,0:T(8,128)S(1)}, u32[]{:S(2)}, u32[]{:S(2)}) collective-permute-start(f32[16,128]{1,0:T(8,128)S(1)} %shard_map.107.after_ref.mine_ref), channel_id=1, source_target_pairs={{0,2},{1,3},{2,0},{3,1},{4,6},{5,7},{6,4},{7,5},{8,10},{9,11},{10,... | collective-permute-start | bytes 24584 | tf_op jit(solution)/shard_map/ppermute | solution.py:21
  77.5 8.5 %collective-permute-start.34 = (f32[128,128]{1,0:T(8,128)S(1)}, f32[128,128]{1,0:T(8,128)S(1)}, u32[]{:S(2)}, u32[]{:S(2)}) collective-permute-start(f32[128,128]{1,0:T(8,128)S(1)} %get-tuple-element.86), channel_id=1, source_target_pairs={{0,4},{1,5},{2,6},{3,7},{4,0},{5,1},{6,2},{7,3},{8,12},{9,13},{10,... | collective-permute-start | bytes 196616 | tf_op jit(solution)/shard_map/ppermute | solution.py:21
  78.0 9.3 %collective-permute-start.35 = (f32[128,128]{1,0:T(8,128)S(1)}, f32[128,128]{1,0:T(8,128)S(1)}, u32[]{:S(2)}, u32[]{:S(2)}) collective-permute-start(f32[128,128]{1,0:T(8,128)S(1)} %get-tuple-element.87), channel_id=1, source_target_pairs={{0,8},{1,9},{2,10},{3,11},{4,12},{5,13},{6,14},{7,15},{8,0},{9,1},... | collective-permute-start | bytes 196616 | tf_op jit(solution)/shard_map/ppermute | solution.py:21
  80.7 6.7 %collective-permute-start.36 = (f32[128,128]{1,0:T(8,128)S(1)}, f32[128,128]{1,0:T(8,128)S(1)}, u32[]{:S(2)}, u32[]{:S(2)}) collective-permute-start(f32[128,128]{1,0:T(8,128)S(1)} %get-tuple-element.88), channel_id=1, source_target_pairs={{0,12},{1,13},{2,14},{3,15},{4,8},{5,9},{6,10},{7,11},{8,4},{9,5},... | collective-permute-start | bytes 196616 | tf_op jit(solution)/shard_map/ppermute | solution.py:21
  82.5 8.1 %collective-permute-start.39 = (f32[80,128]{1,0:T(8,128)S(1)}, f32[80,128]{1,0:T(8,128)S(1)}, u32[]{:S(2)}, u32[]{:S(2)}) collective-permute-start(f32[80,128]{1,0:T(8,128)S(1)} %get-tuple-element.94), channel_id=1, source_target_pairs={{0,64},{16,80},{32,96},{48,112},{64,0},{80,16},{96,32},{112,48},{1... | collective-permute-start | bytes 122888 | tf_op jit(solution)/shard_map/ppermute | solution.py:21
  82.6 8.0 %collective-permute-start.40 = (f32[80,128]{1,0:T(8,128)S(1)}, f32[80,128]{1,0:T(8,128)S(1)}, u32[]{:S(2)}, u32[]{:S(2)}) collective-permute-start(f32[80,128]{1,0:T(8,128)S(1)} %get-tuple-element.95), channel_id=1, source_target_pairs={{0,128},{16,144},{32,160},{48,176},{64,192},{80,208},{96,224},{112... | collective-permute-start | bytes 122888 | tf_op jit(solution)/shard_map/ppermute | solution.py:21
  86.0 5.2 %collective-permute-start.41 = (f32[80,128]{1,0:T(8,128)S(1)}, f32[80,128]{1,0:T(8,128)S(1)}, u32[]{:S(2)}, u32[]{:S(2)}) collective-permute-start(f32[80,128]{1,0:T(8,128)S(1)} %get-tuple-element.96), channel_id=1, source_target_pairs={{0,192},{16,208},{32,224},{48,240},{64,128},{80,144},{96,160},{112... | collective-permute-start | bytes 122888 | tf_op jit(solution)/shard_map/ppermute | solution.py:21
  87.4 18.8 %collective-permute-start.38 = (f32[64,128]{1,0:T(8,128)S(1)}, f32[64,128]{1,0:T(8,128)S(1)}, u32[]{:S(2)}, u32[]{:S(2)}) collective-permute-start(f32[64,128]{1,0:T(8,128)S(1)} %get-tuple-element.92), channel_id=1, source_target_pairs={{0,2},{1,3},{2,0},{3,1},{4,6},{5,7},{6,4},{7,5},{8,10},{9,11},{10,... | collective-permute-start | bytes 98312 | tf_op jit(solution)/shard_map/ppermute | solution.py:21
  93.8 5.5 %collective-permute-start.44 = (f32[32,128]{1,0:T(8,128)S(1)}, f32[32,128]{1,0:T(8,128)S(1)}, u32[]{:S(2)}, u32[]{:S(2)}) collective-permute-start(f32[32,128]{1,0:T(8,128)S(1)} %get-tuple-element.100), channel_id=1, source_target_pairs={{0,48},{16,32},{32,16},{48,0},{64,112},{80,96},{96,80},{112,64},{1... | collective-permute-start | bytes 49160 | tf_op jit(solution)/shard_map/ppermute | solution.py:21
  99.4 4.9 %collective-permute-start.45 = (f32[16,128]{1,0:T(8,128)S(1)}, f32[16,128]{1,0:T(8,128)S(1)}, u32[]{:S(2)}, u32[]{:S(2)}) collective-permute-start(f32[16,128]{1,0:T(8,128)S(1)} %get-tuple-element.101.refs_3_), channel_id=1, source_target_pairs={{0,12},{1,13},{2,14},{3,15},{4,8},{5,9},{6,10},{7,11},{8,4},{9,5},... | collective-permute-start | bytes 24584 | tf_op jit(solution)/shard_map/ppermute | solution.py:21
  101.0 5.2 %collective-permute-start.46 = (f32[16,128]{1,0:T(8,128)S(1)}, f32[16,128]{1,0:T(8,128)S(1)}, u32[]{:S(2)}, u32[]{:S(2)}) collective-permute-start(f32[16,128]{1,0:T(8,128)S(1)} %get-tuple-element.101.refs_3_), channel_id=1, source_target_pairs={{0,8},{1,9},{2,10},{3,11},{4,12},{5,13},{6,14},{7,15},{8,0},{9,1},... | collective-permute-start | bytes 24584 | tf_op jit(solution)/shard_map/ppermute | solution.py:21
  (19 other events, 82.5 us)
